TPU v7x, 128 devices: a whole 4x4x4 slice. The times are simulated.
128 devices in a mesh: expert: 32 (over y, x, core), tensor: 4 (over z).
Axes of the slice: x: 4, y: 4, z: 4, core: 2. Of those that a mesh axis runs over, the one named last changes fastest.
Arguments:
- residual: bfloat16 [1024, 7168], P(('expert', 'tensor')), may hold values from -3 to 3
- query_latent: bfloat16 [512, 2, 32, 512], P(('expert', 'tensor')), may hold values from -48 to 48
- query_rope: bfloat16 [512, 2, 32, 64], P(('expert', 'tensor')), may hold values from -6 to 6
- cache_latent: bfloat16 [512, 2048, 512], P(('expert', 'tensor')), may hold values from -6 to 6
- cache_rope: bfloat16 [512, 64, 2048], P(('expert', 'tensor')), may hold values from -6 to 6
- new_latent: bfloat16 [512, 2, 512], P(('expert', 'tensor')), may hold values from -6 to 6
- new_rope: bfloat16 [512, 2, 64], P(('expert', 'tensor')), may hold values from -6 to 6
- lengths: int32 [512], P(('expert', 'tensor')), may hold values from 256 to 2048, as said below
- value_proj: bfloat16 [32, 512, 128], replicated, may hold values from -2.5 to 2.5
- out_proj: bfloat16 [4096, 7168], P(None, 'expert'), may hold values from -0.09375 to 0.09375
- norm_gain: bfloat16 [7168], replicated, may hold values from 0.099609375 to 1.8984375
- expert_ids: int32 [1024, 8], P(('expert', 'tensor')), may hold values from 0 to 31, all different within a row; in each aligned block of 8 rows (0 to 7, 8 to 15, ...) at most 4 rows name the same one
- expert_gates: float32 [1024, 8], P(('expert', 'tensor')), may hold values from 0.05 to 0.5
- w_gate: bfloat16 [32, 7168, 1024], P('expert', None, 'tensor'), may hold values from -0.0625 to 0.0625
- w_up: bfloat16 [32, 7168, 1024], P('expert', None, 'tensor'), may hold values from -0.0625 to 0.0625
- w_down: bfloat16 [32, 1024, 7168], P('expert', 'tensor'), may hold values from -0.1875 to 0.1875
Outputs:
- layer_out: bfloat16 [1024, 7168], P(('expert', 'tensor'))
Inputs may be any that keep to these rules, and one draw needn't show every extreme that they name: `lengths`: some request's context holds all 2048 cached entries. `expert_ids`: among the rows of one device each expert is named at most 4 times.
All inputs are finite; a program needn't handle non-finite values.
Results may differ from a plain program's by a relative error of at most 0.012.
Values may be sent and summed in bfloat16 or wider, within the bound.
No kernel may reach another device: no remote copies, remote signals or barrier semaphores. Data moves between devices by JAX's collectives and lax.ppermute only.
A program may use at most 128 MiB of HBM per device.

v0:
```python
import jax
import jax.numpy as jnp
from jax import lax
from jax.sharding import PartitionSpec as P

EPSILON = 1e-06


def attention_heads(
    query_latent, query_rope, cache_latent, cache_rope, new_latent, new_rope, lengths, value_proj
):
    score_scale = (value_proj.shape[2] + query_rope.shape[3]) ** (-0.5)
    context = cache_latent.shape[1]
    steps_count = query_latent.shape[1]
    cached = jnp.einsum(
        "rshl,rcl->rshc", query_latent, cache_latent, preferred_element_type=jnp.float32
    )
    cached = cached + jnp.einsum(
        "rshp,rpc->rshc", query_rope, cache_rope, preferred_element_type=jnp.float32
    )
    recent = jnp.einsum(
        "rshl,rnl->rshn", query_latent, new_latent, preferred_element_type=jnp.float32
    )
    recent = recent + jnp.einsum(
        "rshp,rnp->rshn", query_rope, new_rope, preferred_element_type=jnp.float32
    )
    cache_valid = jnp.arange(context, dtype=jnp.int32)[None, :] < lengths[:, None]
    recent_valid = (
        jnp.arange(steps_count, dtype=jnp.int32)[None, :]
        <= jnp.arange(steps_count, dtype=jnp.int32)[:, None]
    )
    cached = jnp.where(cache_valid[:, None, None, :], cached * score_scale, -1e30)
    recent = jnp.where(recent_valid[None, :, None, :], recent * score_scale, -1e30)
    weights = jax.nn.softmax(jnp.concatenate([cached, recent], axis=-1), axis=-1).astype(
        jnp.bfloat16
    )
    mixed = jnp.einsum(
        "rshc,rcl->rshl", weights[..., :context], cache_latent, preferred_element_type=jnp.float32
    )
    mixed = mixed + jnp.einsum(
        "rshn,rnl->rshl", weights[..., context:], new_latent, preferred_element_type=jnp.float32
    )
    mixed = mixed.astype(jnp.bfloat16)
    head_values = jnp.einsum(
        "rshl,hlv->rshv", mixed, value_proj, preferred_element_type=jnp.float32
    )
    rows_count = head_values.shape[0] * head_values.shape[1]
    return head_values.astype(jnp.bfloat16).reshape(rows_count, -1)


def per_device(
    residual,
    query_latent,
    query_rope,
    cache_latent,
    cache_rope,
    new_latent,
    new_rope,
    lengths,
    value_proj,
    out_proj,
    norm_gain,
    expert_ids,
    expert_gates,
    w_gate,
    w_up,
    w_down,
):
    head_values = attention_heads(
        query_latent,
        query_rope,
        cache_latent,
        cache_rope,
        new_latent,
        new_rope,
        lengths,
        value_proj,
    )
    column_block = jnp.dot(
        lax.all_gather(head_values, "expert", axis=0, tiled=True),
        out_proj,
        preferred_element_type=jnp.float32,
    ).astype(jnp.bfloat16)
    attn_out = lax.all_to_all(column_block, "expert", split_axis=0, concat_axis=1, tiled=True)
    stream = residual.astype(jnp.float32) + attn_out.astype(jnp.float32)
    inverse = lax.rsqrt(jnp.mean(stream * stream, axis=-1, keepdims=True) + EPSILON)
    normed = (stream * inverse * norm_gain.astype(jnp.float32)).astype(jnp.bfloat16)
    tok_rows, top_count = expert_ids.shape
    width = residual.shape[1]
    expert_count = lax.axis_size("expert")
    group_count = lax.axis_size("tensor")
    capacity = min(tok_rows, 2 * max(1, tok_rows * top_count // expert_count))
    flat_ids = expert_ids.reshape(-1)
    expert_hot = (flat_ids[:, None] == jnp.arange(expert_count, dtype=jnp.int32)[None, :]).astype(
        jnp.int32
    )
    slot_index = jnp.sum(expert_hot * (jnp.cumsum(expert_hot, axis=0) - 1), axis=1)
    place_index = flat_ids * capacity + slot_index
    slot_hot = (
        place_index[:, None] == jnp.arange(expert_count * capacity, dtype=jnp.int32)[None, :]
    ).astype(jnp.float32)
    owner_index = jnp.arange(tok_rows * top_count, dtype=jnp.int32) // top_count
    owner_hot = (owner_index[:, None] == jnp.arange(tok_rows, dtype=jnp.int32)[None, :]).astype(
        jnp.float32
    )
    send_table = jnp.dot(slot_hot.T, owner_hot).astype(jnp.bfloat16)
    gathered = jnp.dot(send_table, normed, preferred_element_type=jnp.float32).astype(jnp.bfloat16)
    buffer = gathered.reshape(expert_count, capacity, width)
    gate_table = jnp.dot(
        owner_hot.T, slot_hot * expert_gates.reshape(-1)[:, None], precision=lax.Precision.HIGHEST
    )
    landed = lax.all_to_all(buffer, "expert", split_axis=0, concat_axis=0, tiled=True)
    arrived = lax.all_gather(landed[:, None], "tensor", axis=1, tiled=True)
    rows = arrived.reshape(-1, width)
    gate_act = jnp.dot(rows, w_gate[0], preferred_element_type=jnp.float32)
    up_act = jnp.dot(rows, w_up[0], preferred_element_type=jnp.float32)
    hidden = (jax.nn.silu(gate_act) * up_act).astype(jnp.bfloat16)
    partial_value = jnp.dot(hidden, w_down[0], preferred_element_type=jnp.float32)
    partial_value = partial_value.reshape(expert_count, group_count, capacity, width)
    own_sums = lax.psum_scatter(
        partial_value.astype(jnp.bfloat16), "tensor", scatter_dimension=1, tiled=True
    )
    expert_out = lax.all_to_all(own_sums, "expert", split_axis=0, concat_axis=0, tiled=True)
    expert_out = lax.optimization_barrier(
        expert_out.reshape(expert_count * capacity, width)
    ).astype(jnp.float32)
    routed = jnp.dot(gate_table, expert_out, precision=lax.Precision.HIGHEST)
    return (stream + routed).astype(jnp.bfloat16)


def solution(mesh):
    return jax.shard_map(
        per_device,
        mesh=mesh,
        in_specs=(
            P(("expert", "tensor"), None),
            P(("expert", "tensor"), None, None, None),
            P(("expert", "tensor"), None, None, None),
            P(("expert", "tensor"), None, None),
            P(("expert", "tensor"), None, None),
            P(("expert", "tensor"), None, None),
            P(("expert", "tensor"), None, None),
            P(("expert", "tensor")),
            P(),
            P(None, "expert"),
            P(),
            P(("expert", "tensor"), None),
            P(("expert", "tensor"), None),
            P("expert", None, "tensor"),
            P("expert", None, "tensor"),
            P("expert", "tensor", None),
        ),
        out_specs=P(("expert", "tensor"), None),
        check_vma=False,
    )
```

profile of v0, /device:TPU:0, one launch (start us, length us, event | category | flops | bytes accessed | tf_op | source)
XLA Modules:
  0.0 335.4 jit_solution(7967603862132979009)
XLA Ops:
  6.5 0.0 copy-start
  6.5 0.9 iota_compare_fusion.9
  7.4 0.0 copy-start.4
  7.4 0.0 copy-start.7
  7.4 0.0 copy-start.3
  7.5 0.0 copy-start.6
  7.5 0.0 slice-start
  7.5 6.2 %fusion.2 = f32[4,2,32,2048]{3,2,1,0:T(8,128)S(1)} fusion(bf16[4,2,32,512]{3,2,1,0:T(8,128)(2,1)} %param.17, bf16[4,2048,512]{2,1,0:T(8,128)(2,1)} %param.19), kind=kOutput, calls=%fused_computation.4 | convolution fusion | flops 536870912 | bytes 10747904 | tf_op jit(solution)/shard_map/rshl,rcl->rshc/dot_general | solution.py:15
  13.7 0.0 copy-done.4
  13.7 0.0 copy-done.7
  13.7 0.2 fusion.50
  13.9 0.0 copy-done.3
  13.9 0.0 copy-start.11
  14.0 0.0 slice-start.1
  14.0 0.7 fusion.54
  14.6 0.0 copy-done.11
  14.6 0.2 fusion.55
  14.9 0.5 fusion.15
  15.3 0.5 divide_convert_fusion
  15.8 0.0 slice-done
  15.9 0.3 slice-done.1
  16.2 1.6 fusion
  17.7 0.2 fusion.19
  17.9 0.4 copy-done.2
  18.3 0.8 fusion.28
  19.1 0.7 copy.75
  19.8 0.0 all-gather.4.cloned.1.call-update
  19.8 0.1 reshape.90
  19.9 0.1 fusion.40
  20.0 0.1 reduce_window_sum.11
  20.1 0.2 select_reduce_fusion
  20.3 0.0 copy-start.8
  20.3 0.0 copy-start.5
  20.3 45.8 %all-gather.4.cloned.1.call-done = bf16[256,4096]{1,0:T(8,128)(2,1)} async-done(((bf16[8,4096]{1,0:T(8,128)(2,1)}), bf16[256,4096]{1,0:T(8,128)(2,1)}) %all-gather.4.cloned.1.call-update) | async-done | bytes 2097168 | tf_op jit(solution)/shard_map/all_gather | solution.py:80
  66.1 2.4 convolution_convert_fusion.2
  68.5 0.8 copy.54
  69.3 5.1 %all-to-all-start = ((bf16[32,8,224]{2,1,0:T(8,128)(2,1)}), bf16[32,8,224]{2,1,0:T(8,128)(2,1)S(1)}, u32[]{:S(2)}, u32[]{:S(2)}) async-start(bf16[32,8,224]{2,1,0:T(8,128)(2,1)} %bitcast.12), calls=%async_computation | async-start | bytes 262144 | tf_op jit(solution)/shard_map/all_to_all | solution.py:84
  74.4 0.0 all-gather.6.cloned.1.call-start
  74.5 7.7 %all-to-all-done = bf16[32,8,224]{2,1,0:T(8,128)(2,1)S(1)} async-done(((bf16[32,8,224]{2,1,0:T(8,128)(2,1)}), bf16[32,8,224]{2,1,0:T(8,128)(2,1)S(1)}, u32[]{:S(2)}, u32[]{:S(2)}) %all-to-all-start) | async-done | bytes 114720 | tf_op jit(solution)/shard_map/all_to_all | solution.py:84
  82.2 0.1 copy.55
  82.3 0.2 reshape.94
  82.5 0.2 multiply_reduce_fusion
  82.7 0.9 convolution_convert_fusion.1
  83.6 1.7 reshape.91
  85.3 29.8 %all_to_all.23 = bf16[32,4,7168]{2,1,0:T(4,128)(2,1)S(1)} all-to-all(bf16[32,4,7168]{2,1,0:T(4,128)(2,1)} %reshape.91), channel_id=1, replica_groups=mesh['expert'=32,'tensor'=4] {'expert'}, dimensions={0} | all-to-all | bytes 3670016 | tf_op jit(solution)/shard_map/all_to_all | solution.py:112
  115.0 1.8 copy.56
  116.9 0.0 all-gather.6.cloned.1.call-update
  116.9 0.2 reduce-scatter.2.cloned.1.call-start
  117.1 72.2 %all-gather.6.cloned.1.call-done = bf16[32,16,7168]{2,0,1:T(8,128)(2,1)} async-done(((bf16[32,4,7168]{2,0,1:T(8,128)(2,1)}), bf16[32,16,7168]{2,0,1:T(8,128)(2,1)}) %all-gather.6.cloned.1.call-update) | async-done | bytes 7340048 | tf_op jit(solution)/shard_map/all_gather | solution.py:113
  189.4 7.1 %copy.57 = bf16[32,16,7168]{2,1,0:T(8,128)(2,1)S(1)} copy(bf16[32,16,7168]{2,0,1:T(8,128)(2,1)} %all-gather.6.cloned.1.call-done) | data formatting | bytes 14680064 | tf_op jit(solution)/shard_map/all_gather | solution.py:113
  196.5 0.0 copy-start.12
  196.5 4.2 %fusion.10 = f32[512,256]{1,0:T(8,128)S(1)} fusion(bf16[512,7168]{1,0:T(8,128)(2,1)S(1)} %bitcast.77, bf16[1,7168,256]{2,1,0:T(8,128)(2,1)} %param.29), kind=kOutput, calls=%fused_computation.13 | convolution fusion | flops 1879048192 | bytes 11534336 | tf_op jit(solution)/shard_map/dot_general | solution.py:115
  200.8 2.1 fusion.20
  202.8 0.1 dot_general.60
  202.9 7.1 %convolution_convert_fusion = bf16[32,4,4,7168]{3,0,2,1:T(8,128)(2,1)} fusion(bf16[1,256,7168]{2,1,0:T(8,128)(2,1)} %param.31, bf16[32,4,4,256]{3,2,1,0:T(4,128)(2,1)S(1)} %dot_general.60), kind=kOutput, calls=%fused_computation | convolution fusion | flops 1882718208 | bytes 11272192 | tf_op jit(solution)/shard_map/dot_general | solution.py:118
  210.0 0.0 reduce-scatter.2.cloned.1.call-update
  210.0 73.5 %reduce-scatter.2.cloned.1.call-done = bf16[32,1,4,7168]{3,0,2,1:T(8,128)(2,1)} async-done(((bf16[32,4,4,7168]{3,0,2,1:T(8,128)(2,1)}), bf16[32,1,4,7168]{3,0,2,1:T(8,128)(2,1)}) %reduce-scatter.2.cloned.1.call-update) | async-done | bytes 1835024 | tf_op jit(solution)/shard_map/reduce_scatter | solution.py:120
  283.6 4.2 %copy.59 = bf16[32,1,4,7168]{3,2,1,0:T(4,128)(2,1)} copy(bf16[32,1,4,7168]{3,0,2,1:T(8,128)(2,1)} %reduce-scatter.2.cloned.1.call-done) | data formatting | bytes 3670016 | tf_op jit(solution)/shard_map/reduce_scatter | solution.py:120
  287.7 7.3 %all-to-all-start.2 = ((bf16[32,1,4,7168]{3,2,1,0:T(4,128)(2,1)}), bf16[32,1,4,7168]{3,2,1,0:T(4,128)(2,1)}, u32[]{:S(2)}, u32[]{:S(2)}) async-start(bf16[32,1,4,7168]{3,2,1,0:T(4,128)(2,1)} %copy.59), calls=%async_computation.3 | async-start | bytes 3670016 | tf_op jit(solution)/shard_map/all_to_all | solution.py:123
  295.1 0.1 mul.68
  295.1 0.3 fusion.38
  295.4 26.6 %all-to-all-done.2 = bf16[32,1,4,7168]{3,2,1,0:T(4,128)(2,1)} async-done(((bf16[32,1,4,7168]{3,2,1,0:T(4,128)(2,1)}), bf16[32,1,4,7168]{3,2,1,0:T(4,128)(2,1)}, u32[]{:S(2)}, u32[]{:S(2)}) %all-to-all-start.2) | async-done | bytes 1835040 | tf_op jit(solution)/shard_map/all_to_all | solution.py:123
  322.0 3.9 %reshape.93 = bf16[128,7168]{1,0:T(8,128)(2,1)} reshape(bf16[32,1,4,7168]{3,2,1,0:T(4,128)(2,1)} %all-to-all-done.2) | data formatting | bytes 3670016 | tf_op jit(solution)/shard_map/reshape | solution.py:125
  325.9 3.0 fusion.4
  (21 shorter events, 0.1 us)
Async XLA Ops:
  6.5 59.6 %copy-start = (bf16[4096,224]{0,1:T(8,128)(2,1)S(1)}, bf16[4096,224]{0,1:T(8,128)(2,1)}, u32[]{:S(2)}) copy-start(bf16[4096,224]{0,1:T(8,128)(2,1)} %param.25) | copy-start | bytes 5505028
  6.5 59.6 %all-gather.4.cloned.1.call-start = ((), (), s32[]{:S(2)}) async-start(), calls=%async_computation.4 | async-start | bytes 2162688 | tf_op jit(solution)/shard_map/all_gather | solution.py:80
  7.4 6.3 %copy-start.4 = (bf16[4,2,32,512]{3,2,1,0:T(8,128)(2,1)S(1)}, bf16[4,2,32,512]{3,2,1,0:T(8,128)(2,1)}, u32[]{:S(2)}) copy-start(bf16[4,2,32,512]{3,2,1,0:T(8,128)(2,1)} %param.17) | copy-start | bytes 786436
  7.4 6.3 %copy-start.7 = (bf16[4,2,512]{2,1,0:T(2,128)(2,1)S(1)}, bf16[4,2,512]{2,1,0:T(2,128)(2,1)}, u32[]{:S(2)}) copy-start(bf16[4,2,512]{2,1,0:T(2,128)(2,1)} %param.21) | copy-start | bytes 24580
  7.4 6.5 %copy-start.3 = (bf16[4,64,2048]{2,1,0:T(8,128)(2,1)S(1)}, bf16[4,64,2048]{2,1,0:T(8,128)(2,1)}, u32[]{:S(2)}) copy-start(bf16[4,64,2048]{2,1,0:T(8,128)(2,1)} %param.20) | copy-start | bytes 3145732
  7.5 6.5 %copy-start.6 = (bf16[4,2,32,64]{3,2,1,0:T(8,128)(2,1)S(1)}, bf16[4,2,32,64]{3,2,1,0:T(8,128)(2,1)}, u32[]{:S(2)}) copy-start(bf16[4,2,32,64]{3,2,1,0:T(8,128)(2,1)} %param.18) | copy-start | bytes 98308
  7.5 8.4 %slice-start = ((s8[8388608]{0:T(1024)(128)(4,1)}), s8[4194304]{0:T(1024)(128)(4,1)S(1)}, s32[]{:S(2)}) async-start(s8[8388608]{0:T(1024)(128)(4,1)} %bitcast.75), calls=%async_computation.7 | async-start | bytes 8388608
  13.9 0.7 copy-start.11
  14.0 2.2 slice-start.1
  16.1 2.2 copy-start.2
  18.3 1.5 copy-start.9
  20.3 54.2 %copy-start.8 = (bf16[7168]{0:T(1024)(128)(2,1)S(1)}, bf16[7168]{0:T(1024)(128)(2,1)}, u32[]{:S(2)}) copy-start(bf16[7168]{0:T(1024)(128)(2,1)} %param.26) | copy-start | bytes 43012
  20.3 62.2 %copy-start.5 = (bf16[8,7168]{1,0:T(8,128)(2,1)S(1)}, bf16[8,7168]{1,0:T(8,128)(2,1)}, u32[]{:S(2)}) copy-start(bf16[8,7168]{1,0:T(8,128)(2,1)} %param.16) | copy-start | bytes 344068
  69.3 12.9 %all-to-all-start = ((bf16[32,8,224]{2,1,0:T(8,128)(2,1)}), bf16[32,8,224]{2,1,0:T(8,128)(2,1)S(1)}, u32[]{:S(2)}, u32[]{:S(2)}) async-start(bf16[32,8,224]{2,1,0:T(8,128)(2,1)} %bitcast.12), calls=%async_computation | async-start | bytes 262144 | tf_op jit(solution)/shard_map/all_to_all | solution.py:84
  74.4 115.0 %all-gather.6.cloned.1.call-start = ((), (), s32[]{:S(2)}) async-start(), calls=%async_computation.6 | async-start | bytes 9175040 | tf_op jit(solution)/shard_map/all_gather | solution.py:113
  116.9 166.6 %reduce-scatter.2.cloned.1.call-start = ((), (), s32[]{:S(2)}) async-start(), calls=%async_computation.5 | async-start | bytes 9175040 | tf_op jit(solution)/shard_map/reduce_scatter | solution.py:120
  196.5 4.3 %copy-start.12 = (bf16[1,7168,256]{2,1,0:T(8,128)(2,1)S(1)}, bf16[1,7168,256]{2,1,0:T(8,128)(2,1)}, u32[]{:S(2)}) copy-start(bf16[1,7168,256]{2,1,0:T(8,128)(2,1)} %param.30) | copy-start | bytes 11010052
  287.7 7.4 %copy-start.10 = (f32[8,8]{1,0:T(8,128)S(1)}, f32[8,8]{1,0:T(8,128)}, u32[]{:S(2)}) copy-start(f32[8,8]{1,0:T(8,128)} %param.28) | copy-start | bytes 772
  287.7 34.3 %all-to-all-start.2 = ((bf16[32,1,4,7168]{3,2,1,0:T(4,128)(2,1)}), bf16[32,1,4,7168]{3,2,1,0:T(4,128)(2,1)}, u32[]{:S(2)}, u32[]{:S(2)}) async-start(bf16[32,1,4,7168]{3,2,1,0:T(4,128)(2,1)} %copy.59), calls=%async_computation.3 | async-start | bytes 3670016 | tf_op jit(solution)/shard_map/all_to_all | solution.py:123
  295.1 33.7 %copy-start.1 = (bf16[4096,224]{0,1:T(8,128)(2,1)S(1)}, bf16[4096,224]{0,1:T(8,128)(2,1)}, u32[]{:S(2)}) copy-start(bf16[4096,224]{0,1:T(8,128)(2,1)} %param.25) | copy-start | bytes 5505028
Sparse Core Ops, SparseCore 0:
  19.9 46.1 all-gather.3
  117.0 72.2 all-gather.5
  210.1 73.3 reduce-scatter.1
where the time goes:
time: 336 us; the launch traced here: 335 us
  waiting for transfers between devices  226 us (67%)
  matrix products  29.8 us (9%)
  blocking collectives  29.8 us (9%)
  local copies, waits for them, and re-layouts  21.4 us (6%)
  between operations  13.4 us (4%)
  starting transfers between devices  12.7 us (4%)
    reduce_scatter x1, waiting for transfers between devices, per_device(): lax.psum_scatter(partial_value.astype(jnp.bfloat16), 'tensor', scatter_di...  73.5 us
    all_gather x1, waiting for transfers between devices, per_device(): arrived = lax.all_gather(landed[:, None], 'tensor', axis=1, tiled=True)  72.2 us
    all_gather x1, waiting for transfers between devices, per_device(): lax.all_gather(head_values, 'expert', axis=0, tiled=True)  45.8 us
    all_to_all x1, blocking collectives, per_device(): lax.all_to_all(buffer, 'expert', split_axis=0, concat_axis=0, tiled=True)  29.8 us
    all_to_all x1, waiting for transfers between devices, per_device(): lax.all_to_all(own_sums, 'expert', split_axis=0, concat_axis=0, tiled=True)  26.6 us
    all_to_all x1, waiting for transfers between devices, per_device(): lax.all_to_all(column_block, 'expert', split_axis=0, concat_axis=1, tiled...  7.71 us
    all_to_all x1, starting transfers between devices, per_device(): lax.all_to_all(own_sums, 'expert', split_axis=0, concat_axis=0, tiled=True)  7.34 us
    all_gather x1, local copies, waits for them, and re-layouts, per_device(): arrived = lax.all_gather(landed[:, None], 'tensor', axis=1, tiled=True)  7.1 us
  transfers between devices with their start and end apart: 5, of which 5 were waited for; matrix products, arithmetic and copies ran while one was open for 0% of the time, Pallas kernels for 0%

commit v1 on v0

v1 whole, which is shorter than its diff:
```python
import functools

import jax
import jax.numpy as jnp
from jax import lax
from jax.experimental import pallas as pl
from jax.experimental.pallas import tpu as pltpu
from jax.sharding import PartitionSpec as P

EPSILON = 1e-06
BOTH = ("expert", "tensor")
SIDE = 4
CHIPS = 16
ROWS_A, ROWS_B, ROWS_C = 336, 352, 336
F32 = jnp.float32
BF16 = jnp.bfloat16


def expert_of(y, x, core):
    return (y * SIDE + x) * 2 + core


def masks_of(core):
    return (1, 3) if core == 0 else (3, 1)


def swap_core(value):
    pairs = [(e, e ^ 1) for e in range(2 * CHIPS)]
    return lax.ppermute(value, "expert", pairs)


def shift_z(value, amount):
    pairs = [(z, (z + amount) % SIDE) for z in range(SIDE)]
    return lax.ppermute(value, "tensor", pairs)


def exchange(value, axis, turn):
    pairs = []
    for y in range(SIDE):
        for x in range(SIDE):
            for core in range(2):
                mask = masks_of(core)[turn]
                here = expert_of(y, x, core)
                if axis == "x":
                    pairs.append((here, expert_of(y, x ^ mask, core)))
                elif axis == "y":
                    pairs.append((here, expert_of(y ^ mask, x, core)))
                else:
                    for z in range(SIDE):
                        pairs.append((here * SIDE + z, here * SIDE + (z ^ mask)))
    return lax.ppermute(value, BOTH if axis == "z" else "expert", pairs)


def after(first, *later):
    return lax.optimization_barrier((first[-8:, :128], *later))[1:]


def grow(value, axis, turn):
    return jnp.concatenate([value, exchange(value, axis, turn)], axis=0)


def attend_kernel(length_ref, q_ref, qr_ref, latent_ref, rope_ref, fresh_ref, fresh_rope_ref, out_ref, *, scale, heads):
    request = pl.program_id(0)
    query = q_ref[0]
    query_rope = qr_ref[0]
    latent = latent_ref[0]
    last = (((1,), (1,)), ((), ()))
    scores = lax.dot_general(query, latent, last, preferred_element_type=F32)
    scores = scores + jnp.dot(query_rope, rope_ref[0], preferred_element_type=F32)
    lane = lax.broadcasted_iota(jnp.int32, (1, scores.shape[1]), 1)
    scores = jnp.where(lane < length_ref[request], scores * scale, -1e30)
    fresh = fresh_ref[0]
    fresh_rope = fresh_rope_ref[0]
    recent = lax.dot_general(query, fresh, last, preferred_element_type=F32)
    recent = recent + lax.dot_general(query_rope, fresh_rope, last, preferred_element_type=F32)
    step = lax.broadcasted_iota(jnp.int32, recent.shape, 0) // heads
    place = lax.broadcasted_iota(jnp.int32, recent.shape, 1)
    recent = jnp.where(place <= step, recent * scale, -1e30)
    top = jnp.maximum(
        jnp.max(scores, axis=1, keepdims=True), jnp.max(recent, axis=1, keepdims=True)
    )
    weights = jnp.exp(scores - top)
    recent = jnp.exp(recent - top)
    total = jnp.sum(weights, axis=1, keepdims=True) + jnp.sum(recent, axis=1, keepdims=True)
    share = 1.0 / total
    mixed = jnp.dot((weights * share).astype(BF16), latent, preferred_element_type=F32)
    recent = (recent * share).astype(BF16).astype(F32)
    for n in range(fresh.shape[0]):
        mixed = mixed + recent[:, n : n + 1] * fresh[n : n + 1].astype(F32)
    out_ref[0] = mixed.astype(BF16)


def attention_heads(
    query_latent, query_rope, cache_latent, cache_rope, new_latent, new_rope, lengths, value_proj
):
    requests, steps, heads, latent = query_latent.shape
    rope = query_rope.shape[3]
    context = cache_latent.shape[1]
    rows = steps * heads
    scale = (value_proj.shape[2] + rope) ** (-0.5)
    whole = lambda *shape: pl.BlockSpec((1,) + shape, lambda i, s: (i, 0, 0))
    mixed = pl.pallas_call(
        functools.partial(attend_kernel, scale=scale, heads=heads),
        grid_spec=pltpu.PrefetchScalarGridSpec(
            num_scalar_prefetch=1,
            grid=(requests,),
            in_specs=[
                whole(rows, latent),
                whole(rows, rope),
                whole(context, latent),
                whole(rope, context),
                whole(steps, latent),
                whole(steps, rope),
            ],
            out_specs=whole(rows, latent),
        ),
        out_shape=jax.ShapeDtypeStruct((requests, rows, latent), BF16),
        cost_estimate=pl.CostEstimate(
            flops=2 * requests * rows * context * (2 * latent + rope),
            bytes_accessed=2 * requests * context * (latent + rope),
            transcendentals=requests * rows * context,
        ),
        compiler_params=pltpu.CompilerParams(vmem_limit_bytes=56 << 20),
    )(
        lengths,
        query_latent.reshape(requests, rows, latent),
        query_rope.reshape(requests, rows, rope),
        cache_latent,
        cache_rope,
        new_latent,
        new_rope,
    )
    head_values = jnp.einsum(
        "rshl,hlv->rshv",
        mixed.reshape(requests, steps, heads, latent),
        value_proj,
        preferred_element_type=F32,
    )
    return head_values.astype(BF16).reshape(requests * steps, -1)


def pack_kernel(heads_ref, residual_ref, routing_ref, out_ref):
    width = heads_ref.shape[1]
    cols = residual_ref.shape[1] // CHIPS
    for chip in range(CHIPS):
        out_ref[chip, :, :width] = heads_ref[...]
        part = residual_ref[:, chip * cols : (chip + 1) * cols]
        out_ref[chip, :, width:] = jnp.concatenate([part, routing_ref[chip]], axis=1)


def pack(heads, residual, routing):
    rows, width = heads.shape
    cols = residual.shape[1] // CHIPS
    routing = jnp.pad(routing, ((0, 0), (0, 0), (0, 512 - cols - routing.shape[2])))
    return pl.pallas_call(
        pack_kernel,
        out_shape=jax.ShapeDtypeStruct((CHIPS, rows, width + 512), BF16),
        cost_estimate=pl.CostEstimate(
            flops=0, bytes_accessed=2 * CHIPS * rows * (width + 512), transcendentals=0
        ),
    )(heads, residual, routing)


def project_kernel(
    place_ref, in_ref, own_ref, other_ref, gain_ref, out_ref, sum_own, sum_other, *, width
):
    step = pl.program_id(0)
    depth = own_ref.shape[1]

    @pl.when(step == 0)
    def _():
        sum_own[...] = jnp.zeros_like(sum_own)
        sum_other[...] = jnp.zeros_like(sum_other)

    heads = in_ref[:, pl.ds(pl.multiple_of(step * depth, 128), depth)]
    dims = (((1,), (1,)), ((), ()))
    sum_own[...] += lax.dot_general(heads, own_ref[...], dims, preferred_element_type=F32)
    sum_other[...] += lax.dot_general(heads, other_ref[...], dims, preferred_element_type=F32)

    @pl.when(step == pl.num_programs(0) - 1)
    def _():
        first = place_ref[0] == 0
        own, other = sum_own[...], sum_other[...]
        left = jnp.where(first, own, other)
        right = jnp.where(first, other, own)
        both = jnp.concatenate([left, right], axis=1).astype(BF16).astype(F32)
        tail = in_ref[:, width:].astype(F32)
        cols = both.shape[1]
        stream = tail[:, :cols] + both
        square = jnp.sum(stream * stream, axis=1, keepdims=True)
        high = square.astype(BF16).astype(F32)
        low = square - high
        extra = tail[:, cols:]
        lane = lax.broadcasted_iota(jnp.int32, extra.shape, 1)
        extra = jnp.where(lane == 6, high, jnp.where(lane == 7, low, extra))
        stream = stream * gain_ref[0].astype(F32)
        out_ref[...] = jnp.concatenate([stream, extra], axis=1).astype(BF16)


def project(place, landed, own, other, gain):
    rows, total = landed.shape
    cols, width = own.shape
    steps = 4
    depth = width // steps
    out = total - width
    return pl.pallas_call(
        functools.partial(project_kernel, width=width),
        grid_spec=pltpu.PrefetchScalarGridSpec(
            num_scalar_prefetch=1,
            grid=(steps,),
            in_specs=[
                pl.BlockSpec((rows, total), lambda i, s: (0, 0)),
                pl.BlockSpec((cols, depth), lambda i, s: (0, i)),
                pl.BlockSpec((cols, depth), lambda i, s: (0, i)),
                pl.BlockSpec((1, 1, 2 * cols), lambda i, s: (s[1], 0, 0)),
            ],
            out_specs=pl.BlockSpec((rows, out), lambda i, s: (0, 0)),
            scratch_shapes=[pltpu.VMEM((rows, cols), F32)] * 2,
        ),
        out_shape=jax.ShapeDtypeStruct((rows, out), BF16),
        cost_estimate=pl.CostEstimate(
            flops=4 * rows * width * cols, bytes_accessed=4 * width * cols, transcendentals=0
        ),
        compiler_params=pltpu.CompilerParams(vmem_limit_bytes=24 << 20),
    )(place, landed, own, other, gain.reshape(CHIPS, 1, 2 * cols))


def hidden_kernel(
    place_ref,
    a0_ref,
    a1_ref,
    b0_ref,
    b1_ref,
    c0_ref,
    c1_ref,
    wg_ref,
    wgo_ref,
    wu_ref,
    wuo_ref,
    hidden_ref,
    index_ref,
    own_ref,
    tokens,
    weight,
    total,
    extras,
    named,
    arrived,
    *,
    model,
):
    far_y, far_x = pl.program_id(0), pl.program_id(1)
    step = far_y * 2 + far_x
    wide = a0_ref.shape[-1]
    cols = model // CHIPS
    part = wg_ref.shape[1]

    def fetch(at, near):
        source = pl.ds(pl.multiple_of(place_ref[at * 4 + near] * cols, 64), cols)
        return [
            pltpu.make_async_copy(
                ref.at[source],
                weight.at[at, pl.ds(near * wide, cols), pl.ds(i * part, part)],
                arrived.at[at, near, i],
            )
            for i, ref in enumerate((wg_ref, wgo_ref, wu_ref, wuo_ref))
        ]

    @pl.when(step == 0)
    def _():
        total[...] = jnp.zeros_like(total)
        extras[...] = jnp.zeros_like(extras)
        for at in range(4):
            for near in range(4):
                for copy in fetch(at, near):
                    copy.start()
        for at in range(4):
            for near in range(4):
                weight[at, near * wide + cols : (near + 1) * wide] = jnp.zeros(
                    (wide - cols, weight.shape[2]), BF16
                )

    def place_rows(far_z, first, value):
        start = 0
        while start < value.shape[0]:
            row = first + start
            count = min(128 - row % 128, value.shape[0] - start)
            near_z, near = divmod(row // 128, 4)
            at = (far_z * 2 + near_z) * 128 + row % 128
            tokens[at : at + count, near * wide : (near + 1) * wide] = value[start : start + count]
            start += count

    place_rows(0, 0, a0_ref[0])
    place_rows(1, 0, a1_ref[0])
    for bit, ref in ((0, b0_ref), (1, b1_ref)):

        @pl.when(far_x == bit)
        def _(ref=ref):
            place_rows(0, ROWS_A, ref[0, 0])
            place_rows(1, ROWS_A, ref[1, 0])

    for bit, ref in ((0, c0_ref), (1, c1_ref)):

        @pl.when(far_y == bit)
        def _(ref=ref):
            place_rows(0, ROWS_A + ROWS_B, ref[0, 0])
            place_rows(1, ROWS_A + ROWS_B, ref[0, 1])

    for near in range(4):
        for copy in fetch(step, near):
            copy.wait()
    total[...] += jnp.dot(tokens[...], weight[step], preferred_element_type=F32)

    @pl.when(step == 0)
    def _():
        named[...] = tokens[:, cols:wide].astype(F32)

    chip = place_ref[20]
    start = pl.multiple_of((chip // 2) * 16, 16)
    for near in range(4):
        extras[...] += tokens[:, near * wide + cols : (near + 1) * wide].astype(F32)
        mine = tokens[pl.ds(start, 16), near * wide : (near + 1) * wide].astype(F32)
        own_ref[pl.ds(place_ref[step * 4 + near], 1)] = jnp.where(
            lax.rem(chip, 2) == 0, mine[:8], mine[8:]
        )[None]

    @pl.when(step == 3)
    def _():
        sums = extras[...]
        square = (sums[:, 6:7] + sums[:, 7:8]) * (1.0 / model)
        inverse = lax.rsqrt(square + EPSILON)
        names = named[...]
        group = lax.broadcasted_iota(jnp.int32, (128, 1), 0) // 8
        bases = jnp.concatenate(
            [group * 4 + place_ref[16 + i] * (4 * CHIPS) for i in range(4)], axis=0
        )
        slots = bases.shape[0] // 2
        lanes = lax.broadcasted_iota(jnp.int32, (1, slots), 1)
        even = place_ref[21] == 0
        gates = [names[:, 2 * i : 2 * i + 1] + names[:, 2 * i + 1 : 2 * i + 2] for i in range(2)]
        ranks = [names[:, 4 + i : 5 + i].astype(jnp.int32) for i in range(2)]
        for i in range(2):
            gate = total[:, i * part : (i + 1) * part] * inverse
            up = total[:, (2 + i) * part : (3 + i) * part] * inverse
            share = jnp.where(even, gates[i], gates[1 - i])
            rank = jnp.where(even, ranks[i], ranks[1 - i])
            value = gate * (1.0 / (1.0 + jnp.exp(-gate))) * up * share
            place_index = jnp.where(rank < 4, bases + rank, -1)
            index_ref[:, i : i + 1] = place_index
            hot = (place_index == lanes).astype(BF16)
            hidden_ref[i] = lax.dot_general(
                hot, value.astype(BF16), (((0,), (0,)), ((), ())), preferred_element_type=F32
            ).astype(BF16)


def hidden_values(place, parts, weights):
    (a0, a1), (b0, b1), (c0, c1) = parts
    wide = a0.shape[-1]
    model, part = weights[0].shape
    cols = model // CHIPS
    tok = SIDE * 128
    a0, a1 = (v.reshape(4, ROWS_A, wide) for v in (a0, a1))
    b0, b1 = (v.reshape(2, 2, ROWS_B, wide) for v in (b0, b1))
    c0, c1 = (v.reshape(2, 2, ROWS_C, wide) for v in (c0, c1))
    a_spec = pl.BlockSpec((1, ROWS_A, wide), lambda y, x, s: (y * 2 + x, 0, 0))
    b_spec = pl.BlockSpec((2, 1, ROWS_B, wide), lambda y, x, s: (0, y, 0, 0))
    c_spec = pl.BlockSpec((1, 2, ROWS_C, wide), lambda y, x, s: (x, 0, 0, 0))
    return pl.pallas_call(
        functools.partial(hidden_kernel, model=model),
        grid_spec=pltpu.PrefetchScalarGridSpec(
            num_scalar_prefetch=1,
            grid=(2, 2),
            in_specs=[a_spec] * 2
            + [b_spec] * 2
            + [c_spec] * 2
            + [pl.BlockSpec(memory_space=pltpu.HBM)] * 4,
            out_specs=[
                pl.BlockSpec((2, tok // 2, part), lambda y, x, s: (0, 0, 0)),
                pl.BlockSpec((tok, 2), lambda y, x, s: (0, 0)),
                pl.BlockSpec((CHIPS, 8, wide), lambda y, x, s: (0, 0, 0)),
            ],
            scratch_shapes=[
                pltpu.VMEM((tok, 4 * wide), BF16),
                pltpu.VMEM((4, 4 * wide, 4 * part), BF16),
                pltpu.VMEM((tok, 4 * part), F32),
                pltpu.VMEM((tok, wide - cols), F32),
                pltpu.VMEM((tok, wide - cols), F32),
                pltpu.SemaphoreType.DMA((4, 4, 4)),
            ],
        ),
        out_shape=[
            jax.ShapeDtypeStruct((2, tok // 2, part), BF16),
            jax.ShapeDtypeStruct((tok, 2), jnp.int32),
            jax.ShapeDtypeStruct((CHIPS, 8, wide), F32),
        ],
        cost_estimate=pl.CostEstimate(
            flops=8 * tok * CHIPS * wide * part,
            bytes_accessed=8 * model * part + 2 * tok * CHIPS * wide,
            transcendentals=2 * tok * part,
        ),
        compiler_params=pltpu.CompilerParams(vmem_limit_bytes=50 << 20),
    )(place, a0, a1, b0, b1, c0, c1, *weights)


def down_kernel(place_ref, index_ref, *refs):
    hidden, weights, (out_ref, spread) = refs[:4], refs[4:12], refs[12:]
    slots, part = hidden[0].shape[1:]

    @pl.when(pl.program_id(0) == 0)
    def _():
        lanes = lax.broadcasted_iota(jnp.int32, (1, slots), 1)
        for i in range(2):
            hot = (index_ref[:, i : i + 1] == lanes).astype(BF16)
            for k, ref in enumerate(hidden):
                at = (i * 4 + k) * part
                spread[:, at : at + part] = jnp.dot(
                    hot, ref[i], preferred_element_type=F32
                ).astype(BF16)

    weight = jnp.concatenate([ref[...] for ref in weights], axis=0)
    total = jnp.dot(spread[...], weight, preferred_element_type=F32).astype(BF16)
    for i in range(4):
        start = pl.multiple_of(place_ref[16 + i] * 128, 128)
        out_ref[pl.ds(start, 128), :] = total[i * 128 : (i + 1) * 128]


def down(place, index, hidden, own, other):
    tok = index.shape[0]
    slots, part = hidden[0].shape[1:]
    width = own[1].shape[1]
    tile = width // 2
    h_spec = pl.BlockSpec((2, slots, part), lambda i, s: (0, 0, 0))
    return pl.pallas_call(
        down_kernel,
        grid_spec=pltpu.PrefetchScalarGridSpec(
            num_scalar_prefetch=1,
            grid=(width // tile,),
            in_specs=[pl.BlockSpec((tok, 2), lambda i, s: (0, 0))]
            + [h_spec] * 4
            + [
                pl.BlockSpec((part, tile), lambda i, s: (0, s[22] * 2 + i)),
            ]
            + [pl.BlockSpec((part, tile), lambda i, s: (0, i))] * 7,
            out_specs=pl.BlockSpec((tok, tile), lambda i, s: (0, i)),
            scratch_shapes=[pltpu.VMEM((tok, 8 * part), BF16)],
        ),
        out_shape=jax.ShapeDtypeStruct((tok, width), BF16),
        cost_estimate=pl.CostEstimate(
            flops=16 * tok * part * width, bytes_accessed=16 * part * width, transcendentals=0
        ),
        compiler_params=pltpu.CompilerParams(vmem_limit_bytes=48 << 20),
    )(place, index, *hidden, *own, *other)


def routing_columns(expert_ids, expert_gates):
    rows, count = expert_ids.shape
    experts = 2 * CHIPS
    hot = expert_ids[:, :, None] == jnp.arange(experts, dtype=jnp.int32)
    gates = jnp.sum(jnp.where(hot, expert_gates[:, :, None], 0.0), axis=1)
    named = jnp.any(hot, axis=1)
    ones = named.astype(F32)
    below = jnp.tril(jnp.ones((rows, rows), F32), -1)
    rank = jnp.where(named, jnp.sum(below[:, :, None] * ones[None], axis=1), 8.0)
    high = lax.reduce_precision(gates, 8, 7)
    low = gates - high
    pair = lambda v: v.reshape(rows, CHIPS, 2).transpose(1, 0, 2)
    gate_pair = jnp.stack([pair(high), pair(low)], axis=-1).reshape(CHIPS, rows, 4)
    return jnp.concatenate([gate_pair, pair(rank)], axis=-1).astype(BF16)


def per_device(
    residual,
    query_latent,
    query_rope,
    cache_latent,
    cache_rope,
    new_latent,
    new_rope,
    lengths,
    value_proj,
    out_proj,
    norm_gain,
    expert_ids,
    expert_gates,
    w_gate,
    w_up,
    w_down,
):
    rows, model = residual.shape
    expert = lax.axis_index("expert")
    plane = lax.axis_index("tensor")
    core = expert % 2
    chip = expert // 2
    first = jnp.where(core == 0, 1, 3)
    second = 4 - first
    table = []
    for far_y in range(2):
        for far_x in range(2):
            for near_y in range(2):
                for near_x in range(2):
                    mask_x = (first * near_x) ^ (second * far_x)
                    mask_y = (first * near_y) ^ (second * far_y)
                    table.append(chip ^ (mask_y * SIDE + mask_x))
    for far_z in range(2):
        for near_z in range(2):
            table.append(plane ^ ((first * near_z) ^ (second * far_z)))
    table += [chip, core, plane, chip]
    place = jnp.stack([jnp.asarray(v, jnp.int32) for v in table])

    quarter = model // SIDE
    half = w_down.shape[1]
    cut = lambda v, z: lax.dynamic_slice(v, (0, z * quarter), (half, quarter))
    lengths, passed = lax.optimization_barrier((lengths, cut(w_down[0], plane ^ first ^ second)))
    passed = exchange(passed, "z", 0)
    out_own = out_proj.T
    out_other = swap_core(out_own)
    gate_own, up_own = w_gate[0], w_up[0]
    gate_other, up_other = swap_core(gate_own), swap_core(up_own)

    heads = attention_heads(
        query_latent,
        query_rope,
        cache_latent,
        cache_rope,
        new_latent,
        new_rope,
        lengths,
        value_proj,
    )
    cols = model // CHIPS
    sent = pack(heads, residual, routing_columns(expert_ids, expert_gates))
    sent, out_other, gate_other, up_other, passed, late_down = lax.optimization_barrier(
        (sent, out_other, gate_other, up_other, passed, w_down[0])
    )
    near = exchange(cut(late_down, plane ^ first), "z", 0)
    far = exchange(cut(late_down, plane ^ second), "z", 1)
    lane_plane = [
        [expert_of(y, x, core) for y in range(SIDE) for x in range(SIDE)] for core in range(2)
    ]
    landed = lax.all_to_all(
        sent, "expert", split_axis=0, concat_axis=0, tiled=True, axis_index_groups=lane_plane
    )
    landed, near, far = lax.optimization_barrier((landed, near, far))
    block = project(
        jnp.stack([core, chip]).astype(jnp.int32),
        landed.reshape(CHIPS * rows, -1),
        out_own,
        out_other,
        norm_gain,
    )
    block = grow(block, "x", 0)
    block = grow(block, "y", 0)
    block = grow(block, "z", 0)
    part_a = block[:ROWS_A]
    part_b = block[ROWS_A : ROWS_A + ROWS_B]
    part_c = block[ROWS_A + ROWS_B :]
    part_a, part_b, part_c = grow(part_a, "x", 1), grow(part_b, "y", 1), grow(part_c, "z", 1)
    part_a, part_b, part_c = grow(part_a, "y", 1), grow(part_b, "z", 1), grow(part_c, "x", 1)
    late_down, near_sent, far_sent = after(part_a, w_down[0], near, far)
    first_other = swap_core(cut(late_down, plane))
    near_other, far_other = swap_core(near_sent), swap_core(far_sent)
    parts = (
        (part_a, exchange(part_a, "z", 1)),
        (part_b, exchange(part_b, "x", 1)),
        (part_c, exchange(part_c, "y", 1)),
    )
    (passed,) = after(parts[2][1], passed)
    last = exchange(passed, "z", 1)
    hidden, index, own = hidden_values(
        place, parts, (gate_own, gate_other, up_own, up_other)
    )
    index, last = lax.optimization_barrier((index, last))
    last_other = swap_core(last)
    spread = [hidden, exchange(hidden, "z", 0), exchange(hidden, "z", 1), shift_z(hidden, 2)]
    sums = down(
        place,
        index,
        spread,
        (w_down[0], near, far, last),
        (first_other, far_other, near_other, last_other),
    )
    lane_all = [
        [expert_of(y, x, core) * SIDE + z for z in range(SIDE) for y in range(SIDE) for x in range(SIDE)]
        for core in range(2)
    ]
    returned = lax.all_to_all(
        sums.reshape(SIDE * CHIPS, rows, quarter),
        BOTH,
        split_axis=0,
        concat_axis=0,
        tiled=True,
        axis_index_groups=lane_all,
    )
    routed = jnp.sum(returned.reshape(SIDE, CHIPS, rows, quarter).astype(F32), axis=1)
    routed = routed.transpose(1, 0, 2).reshape(rows, model)
    stream = own[:, :, :cols].transpose(1, 0, 2).reshape(rows, model) / norm_gain.astype(F32)
    return (stream + routed).astype(BF16)


def solution(mesh):
    return jax.shard_map(
        per_device,
        mesh=mesh,
        in_specs=(
            P(BOTH, None),
            P(BOTH, None, None, None),
            P(BOTH, None, None, None),
            P(BOTH, None, None),
            P(BOTH, None, None),
            P(BOTH, None, None),
            P(BOTH, None, None),
            P(BOTH),
            P(),
            P(None, "expert"),
            P(),
            P(BOTH, None),
            P(BOTH, None),
            P("expert", None, "tensor"),
            P("expert", None, "tensor"),
            P("expert", "tensor", None),
        ),
        out_specs=P(BOTH, None),
        check_vma=False,
    )
```

time: 336 us -> 207 us (0.62)
  waiting for transfers between devices: 226 us -> 99.8 us
  Pallas kernels: 0 us -> 41.3 us
  starting transfers between devices: 12.7 us -> 47.8 us
  blocking collectives: 29.8 us -> 0 us
  matrix products: 29.8 us -> 1.7 us
  between operations: 13.4 us -> 0.28 us
  local copies, waits for them, and re-layouts: 21.4 us -> 11 us
    all_gather x2 -> x0, waiting for transfers between devices: 118 us -> none  [the longest x1 72.2 us: per_device(): arrived = lax.all_gather(landed[:, None], 'tensor', axis=1, tiled=True)]
    reduce_scatter x1 -> x0, waiting for transfers between devices: 73.5 us -> none  [per_device(): lax.psum_scatter(partial_value.astype(jnp.bfloat16), 'tensor', scatter_di...]
    ppermute x0 -> x26, waiting for transfers between devices: none -> 73.4 us  [the longest x18 73.4 us: exchange(): return lax.ppermute(value, BOTH if axis == 'z' else 'expert', pairs)]
    pallas_call x0 -> x5, Pallas kernels: none -> 41.3 us  [the longest x1 17.7 us: hidden_values(): pl.pallas_call(functools.partial(hidden_kernel, model=model), grid_spec=p...]
    ppermute x0 -> x26, starting transfers between devices: none -> 33.7 us  [the longest x18 29.2 us: exchange(): return lax.ppermute(value, BOTH if axis == 'z' else 'expert', pairs)]
    all_to_all x1 -> x0, blocking collectives: 29.8 us -> none  [per_device(): lax.all_to_all(buffer, 'expert', split_axis=0, concat_axis=0, tiled=True)]
    dot_general x14 -> x1, matrix products: 29.8 us -> 1.7 us  [attention_heads(): jnp.einsum('rshl,hlv->rshv', mixed.reshape(requests, steps, heads, latent...]
    all_to_all x2, waiting for transfers between devices: 34.3 us -> 26.4 us  [the longest x1 26.4 us: per_device(): lax.all_to_all(sums.reshape(SIDE * CHIPS, rows, quarter), BOTH, split_axi...]
  transfers between devices with their start and end apart: 5 -> 28, of which waited for: 5 -> 14; matrix products, arithmetic and copies ran while one was open for 0% -> 6% of each run, Pallas kernels for 0% -> 14%
where the time goes in v1:
time: 207 us
  waiting for transfers between devices  99.8 us (48%)
  starting transfers between devices  47.8 us (23%)
  Pallas kernels  41.3 us (20%)
  local copies, waits for them, and re-layouts  11 us (5%)
  other arithmetic  4.9 us (2%)
    ppermute x18, waiting for transfers between devices, exchange(): return lax.ppermute(value, BOTH if axis == 'z' else 'expert', pairs)  73.4 us
    ppermute x18, starting transfers between devices, exchange(): return lax.ppermute(value, BOTH if axis == 'z' else 'expert', pairs)  29.2 us
    all_to_all x1, waiting for transfers between devices, per_device(): lax.all_to_all(sums.reshape(SIDE * CHIPS, rows, quarter), BOTH, split_axi...  26.4 us
    pallas_call x1, Pallas kernels, hidden_values(): pl.pallas_call(functools.partial(hidden_kernel, model=model), grid_spec=p...  17.7 us
    pallas_call x1, Pallas kernels, attention_heads(): pl.pallas_call(functools.partial(attend_kernel, scale=scale, heads=heads)...  9.96 us
    pallas_call x1, Pallas kernels, down(): pl.pallas_call(down_kernel, grid_spec=pltpu.PrefetchScalarGridSpec(num_sc...  8.65 us
    all_to_all x1, starting transfers between devices, per_device(): lax.all_to_all(sums.reshape(SIDE * CHIPS, rows, quarter), BOTH, split_axi...  7.06 us
    all_to_all x1, starting transfers between devices, per_device(): lax.all_to_all(sent, 'expert', split_axis=0, concat_axis=0, tiled=True, a...  7.05 us
  transfers between devices with their start and end apart: 28, of which 14 were waited for; matrix products, arithmetic and copies ran while one was open for 6% of the time, Pallas kernels for 14%

profile of v1, /device:TPU:0, one launch (start us, length us, event | category | flops | bytes accessed | tf_op | source)
XLA Modules:
  0.0 206.9 jit_solution(1207594783294284797)
XLA Ops:
  0.0 0.5 collective-permute-start.2
  0.5 1.2 dynamic-slice_bitcast_fusion
  1.8 2.2 %collective-permute-start.3 = (bf16[256,1792]{1,0:T(8,128)(2,1)S(1)}, bf16[256,1792]{1,0:T(8,128)(2,1)}, u32[]{:S(2)}, u32[]{:S(2)}) collective-permute-start(bf16[256,1792]{1,0:T(8,128)(2,1)S(1)} %dynamic-slice_bitcast_fusion), channel_id=1, source_target_pairs={{0,1},{1,0},{2,3},{3,2},{4,7},{5,6},{6,5},{7,4},{8,9},{9,8},{10,11... | collective-permute-start | bytes 2752520 | tf_op jit(solution)/shard_map/ppermute | solution.py:51
  3.9 0.1 select_reduce_fusion
  4.1 10.0 %shard_map.154 = bf16[4,64,512]{2,1,0:T(8,128)(2,1)} custom-call(s32[4]{0:T(128)} %length_ref, bf16[4,64,512]{2,1,0:T(8,128)(2,1)} %bitcast.85, bf16[4,64,64]{2,1,0:T(8,128)(2,1)} %bitcast.89, bf16[4,2048,512]{2,1,0:T(8,128)(2,1)} %latent_ref.1, bf16[4,64,2048]{2,1,0:T(8,128)(2,1)} %rope_ref.1, bf16[4,2,512]{2,1,0:T(2,128)(2,1)} %fresh_ref.1, ...), custom_call_target="tpu_custom_call" | custom-call | flops 1140850688 | bytes 9437184 | tf_op jit(solution)/shard_map/pallas_call | solution.py:102
  14.1 1.7 fusion.5
  15.9 0.7 copy.57
  16.6 0.2 copy.48
  16.8 0.1 fusion.12
  17.0 0.1 multiply_reduce_fusion
  17.1 0.1 copy.46
  17.2 0.2 copy.47
  17.3 0.7 fusion.11.routing_ref
  18.0 2.0 shard_map.155
  20.1 1.3 copy-done.1
  21.4 7.1 %all-to-all-start = ((bf16[16,8,4608]{2,1,0:T(8,128)(2,1)}), bf16[16,8,4608]{2,1,0:T(8,128)(2,1)S(1)}, u32[]{:S(2)}, u32[]{:S(2)}) async-start(bf16[16,8,4608]{2,1,0:T(8,128)(2,1)} %shard_map.155), calls=%async_computation | async-start | bytes 2359296 | tf_op jit(solution)/shard_map/all_to_all | solution.py:540
  28.5 3.0 %constant_dynamic-slice_fusion.1 = (bf16[256,1792]{1,0:T(8,128)(2,1)}, bf16[256,1792]{1,0:T(8,128)(2,1)}) fusion(bf16[256,7168]{1,0:T(8,128)(2,1)} %bitcast.79, s32[]{:T(128)S(6)} %select_n.56, s32[]{:T(128)S(6)} %select_n.55), kind=kLoop, calls=%fused_computation.37 | loop fusion | bytes 3670024 | tf_op jit(solution)/shard_map/dynamic_slice | solution.py:512
  31.5 0.1 collective-permute-start.4
  31.6 4.0 %collective-permute-start.5 = (bf16[256,1792]{1,0:T(8,128)(2,1)}, bf16[256,1792]{1,0:T(8,128)(2,1)}, u32[]{:S(2)}, u32[]{:S(2)}) collective-permute-start(bf16[256,1792]{1,0:T(8,128)(2,1)} %get-tuple-element.43), channel_id=1, source_target_pairs={{0,3},{1,2},{2,1},{3,0},{4,5},{5,4},{6,7},{7,6},{8,11},{9,10},{10,... | collective-permute-start | bytes 2752520 | tf_op jit(solution)/shard_map/ppermute | solution.py:51
  35.6 0.1 reshape.105.gain_ref
  35.8 18.2 %collective-permute-done.4.refs_5_ = bf16[256,1792]{1,0:T(8,128)(2,1)} collective-permute-done((bf16[256,1792]{1,0:T(8,128)(2,1)}, bf16[256,1792]{1,0:T(8,128)(2,1)}, u32[]{:S(2)}, u32[]{:S(2)}) %collective-permute-start.4) | collective-permute-done | bytes 917536 | tf_op jit(solution)/shard_map/ppermute | solution.py:51
  54.0 3.0 %collective-permute-done.5.refs_6_ = bf16[256,1792]{1,0:T(8,128)(2,1)} collective-permute-done((bf16[256,1792]{1,0:T(8,128)(2,1)}, bf16[256,1792]{1,0:T(8,128)(2,1)}, u32[]{:S(2)}, u32[]{:S(2)}) %collective-permute-start.5) | collective-permute-done | bytes 917536 | tf_op jit(solution)/shard_map/ppermute | solution.py:51
  57.1 1.5 copy-done.2
  58.5 3.0 %shard_map.156 = bf16[128,512]{1,0:T(8,128)(2,1)S(1)} custom-call(s32[2]{0:T(128)S(1)} %pad_add_fusion.place_ref, bf16[128,4608]{1,0:T(8,128)(2,1)S(1)} %bitcast.74, bf16[224,4096]{1,0:T(8,128)(2,1)S(1)} %bitcast.76, bf16[224,4096]{1,0:T(8,128)(2,1)S(1)} %copy-done.2, bf16[16,1,448]{2,1,0:T(2,128)(2,1)S(1)} %reshape.105.gain_ref), custom_call_target="tpu_custom_call" | custom-call | flops 469762048 | bytes 3670016 | tf_op jit(solution)/shard_map/pallas_call | solution.py:206
  61.5 1.9 collective-permute-start.6
  63.5 3.1 %collective-permute-done.6 = bf16[128,512]{1,0:T(8,128)(2,1)S(1)} collective-permute-done((bf16[128,512]{1,0:T(8,128)(2,1)S(1)}, bf16[128,512]{1,0:T(8,128)(2,1)S(1)}, u32[]{:S(2)}, u32[]{:S(2)}) %collective-permute-start.6) | collective-permute-done | bytes 131104 | tf_op jit(solution)/shard_map/ppermute | solution.py:51
  66.6 1.9 collective-permute-start.7
  68.5 4.5 %collective-permute-done.7 = bf16[256,512]{1,0:T(8,128)(2,1)S(1)} collective-permute-done((bf16[256,512]{1,0:T(8,128)(2,1)S(1)}, bf16[256,512]{1,0:T(8,128)(2,1)S(1)}, u32[]{:S(2)}, u32[]{:S(2)}) %collective-permute-start.7) | collective-permute-done | bytes 262176 | tf_op jit(solution)/shard_map/ppermute | solution.py:51
  73.2 3.1 %collective-permute-start.8 = (bf16[336,512]{1,0:T(8,128)(2,1)S(1)}, bf16[336,512]{1,0:T(8,128)(2,1)S(1)}, u32[]{:S(2)}, u32[]{:S(2)}) collective-permute-start(bf16[336,512]{1,0:T(8,128)(2,1)S(1)} %slice.19), channel_id=1, source_target_pairs={{0,24},{4,12},{8,16},{12,4},{16,8},{20,28},{24,0},{28,20},{32,56},... | collective-permute-start | bytes 1032200 | tf_op jit(solution)/shard_map/ppermute | solution.py:51
  76.3 6.0 %collective-permute-done.11 = bf16[512,512]{1,0:T(8,128)(2,1)S(1)} collective-permute-done((bf16[512,512]{1,0:T(8,128)(2,1)S(1)}, bf16[512,512]{1,0:T(8,128)(2,1)S(1)}, u32[]{:S(2)}, u32[]{:S(2)}) %collective-permute-start.11) | collective-permute-done | bytes 524320 | tf_op jit(solution)/shard_map/ppermute | solution.py:51
  82.4 3.1 %collective-permute-start.12 = (bf16[352,512]{1,0:T(8,128)(2,1)S(1)}, bf16[352,512]{1,0:T(8,128)(2,1)S(1)}, u32[]{:S(2)}, u32[]{:S(2)}) collective-permute-start(bf16[352,512]{1,0:T(8,128)(2,1)S(1)} %pad_maximum_fusion.7), channel_id=1, source_target_pairs={{0,96},{4,36},{8,104},{12,44},{16,112},{20,52},{24,120},{28,60},{3... | collective-permute-start | bytes 1081352 | tf_op jit(solution)/shard_map/ppermute | solution.py:51
  85.6 0.2 collective-permute-start.9
  85.8 1.2 collective-permute-start.15
  87.1 4.0 %collective-permute-done.12 = bf16[352,512]{1,0:T(8,128)(2,1)S(1)} collective-permute-done((bf16[352,512]{1,0:T(8,128)(2,1)S(1)}, bf16[352,512]{1,0:T(8,128)(2,1)S(1)}, u32[]{:S(2)}, u32[]{:S(2)}) %collective-permute-start.12) | collective-permute-done | bytes 360480 | tf_op jit(solution)/shard_map/ppermute | solution.py:51
  91.1 0.6 collective-permute-start.13
  91.7 2.7 %collective-permute-done.15 = bf16[336,512]{1,0:T(8,128)(2,1)S(1)} collective-permute-done((bf16[336,512]{1,0:T(8,128)(2,1)S(1)}, bf16[336,512]{1,0:T(8,128)(2,1)S(1)}, u32[]{:S(2)}, u32[]{:S(2)}) %collective-permute-start.15) | collective-permute-done | bytes 344096 | tf_op jit(solution)/shard_map/ppermute | solution.py:51
  94.4 3.1 %collective-permute-start.16 = (bf16[672,512]{1,0:T(8,128)(2,1)S(1)}, bf16[672,512]{1,0:T(8,128)(2,1)S(1)}, u32[]{:S(2)}, u32[]{:S(2)}) collective-permute-start(bf16[672,512]{1,0:T(8,128)(2,1)S(1)} %pad_maximum_fusion.5), channel_id=1, source_target_pairs={{0,24},{4,12},{8,16},{12,4},{16,8},{20,28},{24,0},{28,20},{32,56},... | collective-permute-start | bytes 2064392 | tf_op jit(solution)/shard_map/ppermute | solution.py:51
  97.6 0.9 collective-permute-done.9
  98.5 0.1 pad_maximum_fusion.1
  98.6 0.6 collective-permute-start.10
  99.1 4.6 %collective-permute-done.13 = bf16[704,512]{1,0:T(8,128)(2,1)S(1)} collective-permute-done((bf16[704,512]{1,0:T(8,128)(2,1)S(1)}, bf16[704,512]{1,0:T(8,128)(2,1)S(1)}, u32[]{:S(2)}, u32[]{:S(2)}) %collective-permute-start.13) | collective-permute-done | bytes 720928 | tf_op jit(solution)/shard_map/ppermute | solution.py:51
  103.7 1.3 pad_maximum_fusion
  105.0 3.1 %collective-permute-start.14 = (bf16[1408,512]{1,0:T(8,128)(2,1)}, bf16[1408,512]{1,0:T(8,128)(2,1)}, u32[]{:S(2)}, u32[]{:S(2)}) collective-permute-start(bf16[1408,512]{1,0:T(8,128)(2,1)} %pad_maximum_fusion), channel_id=1, source_target_pairs={{0,24},{4,12},{8,16},{12,4},{16,8},{20,28},{24,0},{28,20},{32,56},... | collective-permute-start | bytes 4325384 | tf_op jit(solution)/shard_map/ppermute | solution.py:51
  108.1 1.2 pad_maximum_fusion.2
  109.3 2.7 %collective-permute-start.17 = (bf16[1344,512]{1,0:T(8,128)(2,1)}, bf16[1344,512]{1,0:T(8,128)(2,1)}, u32[]{:S(2)}, u32[]{:S(2)}) collective-permute-start(bf16[1344,512]{1,0:T(8,128)(2,1)} %pad_maximum_fusion.2), channel_id=1, source_target_pairs={{0,96},{4,36},{8,104},{12,44},{16,112},{20,52},{24,120},{28,60},{3... | collective-permute-start | bytes 4128776 | tf_op jit(solution)/shard_map/ppermute | solution.py:51
  111.9 0.1 stack.107.place_ref
  112.0 0.4 collective-permute-start.18
  112.4 1.2 constant_dynamic-slice_fusion
  113.7 4.7 %collective-permute-done.10 = bf16[1344,512]{1,0:T(8,128)(2,1)S(1)} collective-permute-done((bf16[1344,512]{1,0:T(8,128)(2,1)S(1)}, bf16[1344,512]{1,0:T(8,128)(2,1)S(1)}, u32[]{:S(2)}, u32[]{:S(2)}) %collective-permute-start.10) | collective-permute-done | bytes 1376288 | tf_op jit(solution)/shard_map/ppermute | solution.py:51
  118.5 10.6 %collective-permute-done.17 = bf16[1344,512]{1,0:T(8,128)(2,1)} collective-permute-done((bf16[1344,512]{1,0:T(8,128)(2,1)}, bf16[1344,512]{1,0:T(8,128)(2,1)}, u32[]{:S(2)}, u32[]{:S(2)}) %collective-permute-start.17) | collective-permute-done | bytes 1376288 | tf_op jit(solution)/shard_map/ppermute | solution.py:51
  129.1 17.7 %shard_map.157 = (bf16[2,256,256]{2,1,0:T(8,128)(2,1)S(1)}, s32[512,2]{1,0:T(8,128)S(1)}, f32[16,8,512]{2,1,0:T(8,128)S(1)}) custom-call(s32[24]{0:T(128)S(1)} %stack.107.place_ref, bf16[4,336,512]{2,1,0:T(8,128)(2,1)S(1)} %bitcast.77, bf16[4,336,512]{2,1,0:T(8,128)(2,1)S(1)} %bitcast.78, bf16[2,2,352,512]{3,2,1,0:T(8,128)(2,1)} %bitcast.43.b0_ref, ...), custom_call_target="tpu_custom_call" | custom-call | flops 8589934592 | bytes 23068672 | tf_op jit(solution)/shard_map/pallas_call | solution.py:368
  146.8 0.6 collective-permute-start.25
  147.4 0.8 collective-permute-start.20
  148.3 3.3 %collective-permute-start.21 = (bf16[2,256,256]{2,1,0:T(8,128)(2,1)S(1)}, bf16[2,256,256]{2,1,0:T(8,128)(2,1)S(1)}, u32[]{:S(2)}, u32[]{:S(2)}) collective-permute-start(bf16[2,256,256]{2,1,0:T(8,128)(2,1)S(1)} %get-tuple-element.36.refs_0_), channel_id=1, source_target_pairs={{0,2},{1,3},{2,0},{3,1},{4,6},{5,7},{6,4},{7,5},{8,10},{9,11},{10,... | collective-permute-start | bytes 786440 | tf_op jit(solution)/shard_map/ppermute | solution.py:34
  151.5 5.0 %collective-permute-done.19.refs_1_ = bf16[2,256,256]{2,1,0:T(8,128)(2,1)S(1)} collective-permute-done((bf16[2,256,256]{2,1,0:T(8,128)(2,1)S(1)}, bf16[2,256,256]{2,1,0:T(8,128)(2,1)S(1)}, u32[]{:S(2)}, u32[]{:S(2)}) %collective-permute-start.19) | collective-permute-done | bytes 262176 | tf_op jit(solution)/shard_map/ppermute | solution.py:51
  156.6 6.0 %collective-permute-done.20.refs_2_ = bf16[2,256,256]{2,1,0:T(8,128)(2,1)S(1)} collective-permute-done((bf16[2,256,256]{2,1,0:T(8,128)(2,1)S(1)}, bf16[2,256,256]{2,1,0:T(8,128)(2,1)S(1)}, u32[]{:S(2)}, u32[]{:S(2)}) %collective-permute-start.20) | collective-permute-done | bytes 262176 | tf_op jit(solution)/shard_map/ppermute | solution.py:51
  162.6 0.9 copy-done.8
  163.5 8.6 %shard_map.158 = bf16[512,1792]{1,0:T(8,128)(2,1)} custom-call(s32[24]{0:T(128)S(1)} %stack.107.place_ref, s32[512,2]{1,0:T(8,128)S(1)} %get-tuple-element.35.index_ref, bf16[2,256,256]{2,1,0:T(8,128)(2,1)S(1)} %get-tuple-element.36.refs_0_, bf16[2,256,256]{2,1,0:T(8,128)(2,1)S(1)} %collective-permute-done.19.refs_1_, ...), custom_call_target="tpu_custom_call" | custom-call | flops 3758096384 | bytes 7340032 | tf_op jit(solution)/shard_map/pallas_call | solution.py:433
  172.1 7.1 %all-to-all-start.1 = ((bf16[64,8,1792]{2,1,0:T(8,128)(2,1)}), bf16[64,8,1792]{2,1,0:T(8,128)(2,1)S(1)}, u32[]{:S(2)}, u32[]{:S(2)}) async-start(bf16[64,8,1792]{2,1,0:T(8,128)(2,1)} %bitcast.82), calls=%async_computation.1 | async-start | bytes 3670016 | tf_op jit(solution)/shard_map/all_to_all | solution.py:586
  179.3 0.2 copy.50
  179.4 0.1 reshape.100
  179.6 26.4 %all-to-all-done.1 = bf16[64,8,1792]{2,1,0:T(8,128)(2,1)S(1)} async-done(((bf16[64,8,1792]{2,1,0:T(8,128)(2,1)}), bf16[64,8,1792]{2,1,0:T(8,128)(2,1)S(1)}, u32[]{:S(2)}, u32[]{:S(2)}) %all-to-all-start.1) | async-done | bytes 1835040 | tf_op jit(solution)/shard_map/all_to_all | solution.py:586
  206.0 0.2 convert_reduce_fusion
  206.2 0.7 add_convert_fusion
  (56 shorter events, 0.9 us)
Async XLA Ops:
  0.0 3.9 %copy-start.5 = (s32[8,8]{1,0:T(8,128)S(1)}, s32[8,8]{1,0:T(8,128)}, u32[]{:S(2)}) copy-start(s32[8,8]{1,0:T(8,128)} %param.27) | copy-start | bytes 772
  0.0 3.9 %copy-start.6 = (f32[8,8]{1,0:T(8,128)S(1)}, f32[8,8]{1,0:T(8,128)}, u32[]{:S(2)}) copy-start(f32[8,8]{1,0:T(8,128)} %param.28) | copy-start | bytes 772
  0.0 21.4 %collective-permute-start.1 = (bf16[7168,256]{1,0:T(8,128)(2,1)}, bf16[7168,256]{1,0:T(8,128)(2,1)}, u32[]{:S(2)}, u32[]{:S(2)}) collective-permute-start(bf16[7168,256]{1,0:T(8,128)(2,1)} %bitcast.93), channel_id=1, source_target_pairs={{0,4},{4,0},{8,12},{12,8},{16,20},{20,16},{24,28},{28,24},{32,36},... | collective-permute-start | bytes 11010056 | tf_op jit(solution)/shard_map/ppermute | solution.py:29
  0.0 21.4 %collective-permute-start.2 = (bf16[7168,256]{1,0:T(8,128)(2,1)}, bf16[7168,256]{1,0:T(8,128)(2,1)}, u32[]{:S(2)}, u32[]{:S(2)}) collective-permute-start(bf16[7168,256]{1,0:T(8,128)(2,1)} %bitcast.95), channel_id=1, source_target_pairs={{0,4},{4,0},{8,12},{12,8},{16,20},{20,16},{24,28},{28,24},{32,36},... | collective-permute-start | bytes 11010056 | tf_op jit(solution)/shard_map/ppermute | solution.py:29
  0.5 19.6 %collective-permute-start = (bf16[224,4096]{1,0:T(8,128)(2,1)}, bf16[224,4096]{1,0:T(8,128)(2,1)S(1)}, u32[]{:S(2)}, u32[]{:S(2)}) collective-permute-start(bf16[224,4096]{1,0:T(8,128)(2,1)} %bitcast.75), channel_id=1, source_target_pairs={{0,4},{4,0},{8,12},{12,8},{16,20},{20,16},{24,28},{28,24},{32,36},... | collective-permute-start | bytes 5505032 | tf_op jit(solution)/shard_map/ppermute | solution.py:29
  1.8 18.3 %collective-permute-start.3 = (bf16[256,1792]{1,0:T(8,128)(2,1)S(1)}, bf16[256,1792]{1,0:T(8,128)(2,1)}, u32[]{:S(2)}, u32[]{:S(2)}) collective-permute-start(bf16[256,1792]{1,0:T(8,128)(2,1)S(1)} %dynamic-slice_bitcast_fusion), channel_id=1, source_target_pairs={{0,1},{1,0},{2,3},{3,2},{4,7},{5,6},{6,5},{7,4},{8,9},{9,8},{10,11... | collective-permute-start | bytes 2752520 | tf_op jit(solution)/shard_map/ppermute | solution.py:51
  4.1 10.0 %copy-start.3 = (bf16[32,512,128]{2,1,0:T(8,128)(2,1)S(1)}, bf16[32,512,128]{2,1,0:T(8,128)(2,1)}, u32[]{:S(2)}) copy-start(bf16[32,512,128]{2,1,0:T(8,128)(2,1)} %param.24) | copy-start | bytes 12582916
  20.1 1.3 copy-start.1
  21.4 35.6 %all-to-all-start = ((bf16[16,8,4608]{2,1,0:T(8,128)(2,1)}), bf16[16,8,4608]{2,1,0:T(8,128)(2,1)S(1)}, u32[]{:S(2)}, u32[]{:S(2)}) async-start(bf16[16,8,4608]{2,1,0:T(8,128)(2,1)} %shard_map.155), calls=%async_computation | async-start | bytes 2359296 | tf_op jit(solution)/shard_map/all_to_all | solution.py:540
  28.5 7.1 %copy-start.4 = (bf16[7168]{0:T(1024)(128)(2,1)S(1)}, bf16[7168]{0:T(1024)(128)(2,1)}, u32[]{:S(2)}) copy-start(bf16[7168]{0:T(1024)(128)(2,1)} %param.26) | copy-start | bytes 43012
  28.5 28.5 %copy-start = (bf16[4096,224]{0,1:T(8,128)(2,1)S(1)}, bf16[4096,224]{0,1:T(8,128)(2,1)}, u32[]{:S(2)}) copy-start(bf16[4096,224]{0,1:T(8,128)(2,1)} %param.25) | copy-start | bytes 5505028
  31.5 22.5 %collective-permute-start.4 = (bf16[256,1792]{1,0:T(8,128)(2,1)}, bf16[256,1792]{1,0:T(8,128)(2,1)}, u32[]{:S(2)}, u32[]{:S(2)}) collective-permute-start(bf16[256,1792]{1,0:T(8,128)(2,1)} %get-tuple-element.44), channel_id=1, source_target_pairs={{0,1},{1,0},{2,3},{3,2},{4,7},{5,6},{6,5},{7,4},{8,9},{9,8},{10,11... | collective-permute-start | bytes 2752520 | tf_op jit(solution)/shard_map/ppermute | solution.py:51
  31.6 25.4 %collective-permute-start.5 = (bf16[256,1792]{1,0:T(8,128)(2,1)}, bf16[256,1792]{1,0:T(8,128)(2,1)}, u32[]{:S(2)}, u32[]{:S(2)}) collective-permute-start(bf16[256,1792]{1,0:T(8,128)(2,1)} %get-tuple-element.43), channel_id=1, source_target_pairs={{0,3},{1,2},{2,1},{3,0},{4,5},{5,4},{6,7},{7,6},{8,11},{9,10},{10,... | collective-permute-start | bytes 2752520 | tf_op jit(solution)/shard_map/ppermute | solution.py:51
  57.0 1.5 copy-start.2
  61.5 5.0 %collective-permute-start.6 = (bf16[128,512]{1,0:T(8,128)(2,1)S(1)}, bf16[128,512]{1,0:T(8,128)(2,1)S(1)}, u32[]{:S(2)}, u32[]{:S(2)}) collective-permute-start(bf16[128,512]{1,0:T(8,128)(2,1)S(1)} %shard_map.156), channel_id=1, source_target_pairs={{0,8},{4,28},{8,0},{12,20},{16,24},{20,12},{24,16},{28,4},{32,40},... | collective-permute-start | bytes 393224 | tf_op jit(solution)/shard_map/ppermute | solution.py:51
  66.6 6.5 %collective-permute-start.7 = (bf16[256,512]{1,0:T(8,128)(2,1)S(1)}, bf16[256,512]{1,0:T(8,128)(2,1)S(1)}, u32[]{:S(2)}, u32[]{:S(2)}) collective-permute-start(bf16[256,512]{1,0:T(8,128)(2,1)S(1)} %pad_maximum_fusion.8), channel_id=1, source_target_pairs={{0,32},{4,100},{8,40},{12,108},{16,48},{20,116},{24,56},{28,124},{... | collective-permute-start | bytes 786440 | tf_op jit(solution)/shard_map/ppermute | solution.py:51
  73.1 9.3 %collective-permute-start.11 = (bf16[512,512]{1,0:T(8,128)(2,1)S(1)}, bf16[512,512]{1,0:T(8,128)(2,1)S(1)}, u32[]{:S(2)}, u32[]{:S(2)}) collective-permute-start(bf16[512,512]{1,0:T(8,128)(2,1)S(1)} %pad_maximum_fusion.6), channel_id=1, source_target_pairs={{0,1},{1,0},{2,3},{3,2},{4,7},{5,6},{6,5},{7,4},{8,9},{9,8},{10,11... | collective-permute-start | bytes 1572872 | tf_op jit(solution)/shard_map/ppermute | solution.py:51
  73.2 12.3 %collective-permute-start.8 = (bf16[336,512]{1,0:T(8,128)(2,1)S(1)}, bf16[336,512]{1,0:T(8,128)(2,1)S(1)}, u32[]{:S(2)}, u32[]{:S(2)}) collective-permute-start(bf16[336,512]{1,0:T(8,128)(2,1)S(1)} %slice.19), channel_id=1, source_target_pairs={{0,24},{4,12},{8,16},{12,4},{16,8},{20,28},{24,0},{28,20},{32,56},... | collective-permute-start | bytes 1032200 | tf_op jit(solution)/shard_map/ppermute | solution.py:51
  82.4 8.7 %collective-permute-start.12 = (bf16[352,512]{1,0:T(8,128)(2,1)S(1)}, bf16[352,512]{1,0:T(8,128)(2,1)S(1)}, u32[]{:S(2)}, u32[]{:S(2)}) collective-permute-start(bf16[352,512]{1,0:T(8,128)(2,1)S(1)} %pad_maximum_fusion.7), channel_id=1, source_target_pairs={{0,96},{4,36},{8,104},{12,44},{16,112},{20,52},{24,120},{28,60},{3... | collective-permute-start | bytes 1081352 | tf_op jit(solution)/shard_map/ppermute | solution.py:51
  85.6 12.9 %collective-permute-start.9 = (bf16[672,512]{1,0:T(8,128)(2,1)S(1)}, bf16[672,512]{1,0:T(8,128)(2,1)S(1)}, u32[]{:S(2)}, u32[]{:S(2)}) collective-permute-start(bf16[672,512]{1,0:T(8,128)(2,1)S(1)} %pad_maximum_fusion.4), channel_id=1, source_target_pairs={{0,96},{4,36},{8,104},{12,44},{16,112},{20,52},{24,120},{28,60},{3... | collective-permute-start | bytes 2064392 | tf_op jit(solution)/shard_map/ppermute | solution.py:51
  85.8 8.5 %collective-permute-start.15 = (bf16[336,512]{1,0:T(8,128)(2,1)S(1)}, bf16[336,512]{1,0:T(8,128)(2,1)S(1)}, u32[]{:S(2)}, u32[]{:S(2)}) collective-permute-start(bf16[336,512]{1,0:T(8,128)(2,1)S(1)} %slice.20), channel_id=1, source_target_pairs={{0,3},{1,2},{2,1},{3,0},{4,5},{5,4},{6,7},{7,6},{8,11},{9,10},{10,... | collective-permute-start | bytes 1032200 | tf_op jit(solution)/shard_map/ppermute | solution.py:51
  91.1 12.6 %collective-permute-start.13 = (bf16[704,512]{1,0:T(8,128)(2,1)S(1)}, bf16[704,512]{1,0:T(8,128)(2,1)S(1)}, u32[]{:S(2)}, u32[]{:S(2)}) collective-permute-start(bf16[704,512]{1,0:T(8,128)(2,1)S(1)} %pad_maximum_fusion.3), channel_id=1, source_target_pairs={{0,3},{1,2},{2,1},{3,0},{4,5},{5,4},{6,7},{7,6},{8,11},{9,10},{10,... | collective-permute-start | bytes 2162696 | tf_op jit(solution)/shard_map/ppermute | solution.py:51
  94.4 13.6 %collective-permute-start.16 = (bf16[672,512]{1,0:T(8,128)(2,1)S(1)}, bf16[672,512]{1,0:T(8,128)(2,1)S(1)}, u32[]{:S(2)}, u32[]{:S(2)}) collective-permute-start(bf16[672,512]{1,0:T(8,128)(2,1)S(1)} %pad_maximum_fusion.5), channel_id=1, source_target_pairs={{0,24},{4,12},{8,16},{12,4},{16,8},{20,28},{24,0},{28,20},{32,56},... | collective-permute-start | bytes 2064392 | tf_op jit(solution)/shard_map/ppermute | solution.py:51
  98.6 19.9 %collective-permute-start.10 = (bf16[1344,512]{1,0:T(8,128)(2,1)S(1)}, bf16[1344,512]{1,0:T(8,128)(2,1)S(1)}, u32[]{:S(2)}, u32[]{:S(2)}) collective-permute-start(bf16[1344,512]{1,0:T(8,128)(2,1)S(1)} %pad_maximum_fusion.1), channel_id=1, source_target_pairs={{0,3},{1,2},{2,1},{3,0},{4,5},{5,4},{6,7},{7,6},{8,11},{9,10},{10,... | collective-permute-start | bytes 4128776 | tf_op jit(solution)/shard_map/ppermute | solution.py:51
  105.0 24.1 %collective-permute-start.14 = (bf16[1408,512]{1,0:T(8,128)(2,1)}, bf16[1408,512]{1,0:T(8,128)(2,1)}, u32[]{:S(2)}, u32[]{:S(2)}) collective-permute-start(bf16[1408,512]{1,0:T(8,128)(2,1)} %pad_maximum_fusion), channel_id=1, source_target_pairs={{0,24},{4,12},{8,16},{12,4},{16,8},{20,28},{24,0},{28,20},{32,56},... | collective-permute-start | bytes 4325384 | tf_op jit(solution)/shard_map/ppermute | solution.py:51
  109.3 19.8 %collective-permute-start.17 = (bf16[1344,512]{1,0:T(8,128)(2,1)}, bf16[1344,512]{1,0:T(8,128)(2,1)}, u32[]{:S(2)}, u32[]{:S(2)}) collective-permute-start(bf16[1344,512]{1,0:T(8,128)(2,1)} %pad_maximum_fusion.2), channel_id=1, source_target_pairs={{0,96},{4,36},{8,104},{12,44},{16,112},{20,52},{24,120},{28,60},{3... | collective-permute-start | bytes 4128776 | tf_op jit(solution)/shard_map/ppermute | solution.py:51
  112.0 34.8 %collective-permute-start.18 = (bf16[256,1792]{1,0:T(8,128)(2,1)}, bf16[256,1792]{1,0:T(8,128)(2,1)S(1)}, u32[]{:S(2)}, u32[]{:S(2)}) collective-permute-start(bf16[256,1792]{1,0:T(8,128)(2,1)} %collective-permute-done.3), channel_id=1, source_target_pairs={{0,3},{1,2},{2,1},{3,0},{4,5},{5,4},{6,7},{7,6},{8,11},{9,10},{10,... | collective-permute-start | bytes 2752520 | tf_op jit(solution)/shard_map/ppermute | solution.py:51
  113.6 33.8 %collective-permute-start.22 = (bf16[256,1792]{1,0:T(8,128)(2,1)S(1)}, bf16[256,1792]{1,0:T(8,128)(2,1)S(1)}, u32[]{:S(2)}, u32[]{:S(2)}) collective-permute-start(bf16[256,1792]{1,0:T(8,128)(2,1)S(1)} %constant_dynamic-slice_fusion), channel_id=1, source_target_pairs={{0,4},{4,0},{8,12},{12,8},{16,20},{20,16},{24,28},{28,24},{32,36},... | collective-permute-start | bytes 2752520 | tf_op jit(solution)/shard_map/ppermute | solution.py:29
  118.5 29.8 %collective-permute-start.23 = (bf16[256,1792]{1,0:T(8,128)(2,1)}, bf16[256,1792]{1,0:T(8,128)(2,1)S(1)}, u32[]{:S(2)}, u32[]{:S(2)}) collective-permute-start(bf16[256,1792]{1,0:T(8,128)(2,1)} %collective-permute-done.5.refs_6_), channel_id=1, source_target_pairs={{0,4},{4,0},{8,12},{12,8},{16,20},{20,16},{24,28},{28,24},{32,36},... | collective-permute-start | bytes 2752520 | tf_op jit(solution)/shard_map/ppermute | solution.py:29
  129.1 22.4 %collective-permute-start.24 = (bf16[256,1792]{1,0:T(8,128)(2,1)}, bf16[256,1792]{1,0:T(8,128)(2,1)S(1)}, u32[]{:S(2)}, u32[]{:S(2)}) collective-permute-start(bf16[256,1792]{1,0:T(8,128)(2,1)} %collective-permute-done.4.refs_5_), channel_id=1, source_target_pairs={{0,4},{4,0},{8,12},{12,8},{16,20},{20,16},{24,28},{28,24},{32,36},... | collective-permute-start | bytes 2752520 | tf_op jit(solution)/shard_map/ppermute | solution.py:29
  146.8 15.7 %collective-permute-start.25 = (bf16[256,1792]{1,0:T(8,128)(2,1)S(1)}, bf16[256,1792]{1,0:T(8,128)(2,1)S(1)}, u32[]{:S(2)}, u32[]{:S(2)}) collective-permute-start(bf16[256,1792]{1,0:T(8,128)(2,1)S(1)} %collective-permute-done.18.refs_7_), channel_id=1, source_target_pairs={{0,4},{4,0},{8,12},{12,8},{16,20},{20,16},{24,28},{28,24},{32,36},... | collective-permute-start | bytes 2752520 | tf_op jit(solution)/shard_map/ppermute | solution.py:29
  147.4 9.1 %collective-permute-start.19 = (bf16[2,256,256]{2,1,0:T(8,128)(2,1)S(1)}, bf16[2,256,256]{2,1,0:T(8,128)(2,1)S(1)}, u32[]{:S(2)}, u32[]{:S(2)}) collective-permute-start(bf16[2,256,256]{2,1,0:T(8,128)(2,1)S(1)} %get-tuple-element.36.refs_0_), channel_id=1, source_target_pairs={{0,1},{1,0},{2,3},{3,2},{4,7},{5,6},{6,5},{7,4},{8,9},{9,8},{10,11... | collective-permute-start | bytes 786440 | tf_op jit(solution)/shard_map/ppermute | solution.py:51
  147.4 15.1 %collective-permute-start.20 = (bf16[2,256,256]{2,1,0:T(8,128)(2,1)S(1)}, bf16[2,256,256]{2,1,0:T(8,128)(2,1)S(1)}, u32[]{:S(2)}, u32[]{:S(2)}) collective-permute-start(bf16[2,256,256]{2,1,0:T(8,128)(2,1)S(1)} %get-tuple-element.36.refs_0_), channel_id=1, source_target_pairs={{0,3},{1,2},{2,1},{3,0},{4,5},{5,4},{6,7},{7,6},{8,11},{9,10},{10,... | collective-permute-start | bytes 786440 | tf_op jit(solution)/shard_map/ppermute | solution.py:51
  148.3 14.3 %collective-permute-start.21 = (bf16[2,256,256]{2,1,0:T(8,128)(2,1)S(1)}, bf16[2,256,256]{2,1,0:T(8,128)(2,1)S(1)}, u32[]{:S(2)}, u32[]{:S(2)}) collective-permute-start(bf16[2,256,256]{2,1,0:T(8,128)(2,1)S(1)} %get-tuple-element.36.refs_0_), channel_id=1, source_target_pairs={{0,2},{1,3},{2,0},{3,1},{4,6},{5,7},{6,4},{7,5},{8,10},{9,11},{10,... | collective-permute-start | bytes 786440 | tf_op jit(solution)/shard_map/ppermute | solution.py:34
  151.5 11.0 %copy-start.7 = (bf16[256,1792]{1,0:T(8,128)(2,1)}, bf16[256,1792]{1,0:T(8,128)(2,1)S(1)}, u32[]{:S(2)}) copy-start(bf16[256,1792]{1,0:T(8,128)(2,1)S(1)} %collective-permute-done.24.refs_10_) | copy-start | bytes 2752516
  162.6 0.9 copy-start.8
  172.1 33.8 %all-to-all-start.1 = ((bf16[64,8,1792]{2,1,0:T(8,128)(2,1)}), bf16[64,8,1792]{2,1,0:T(8,128)(2,1)S(1)}, u32[]{:S(2)}, u32[]{:S(2)}) async-start(bf16[64,8,1792]{2,1,0:T(8,128)(2,1)} %bitcast.82), calls=%async_computation.1 | async-start | bytes 3670016 | tf_op jit(solution)/shard_map/all_to_all | solution.py:586

commit v2 on v1

--- a/solution.py
+++ b/solution.py
@@ -11,7 +11,7 @@
 BOTH = ("expert", "tensor")
 SIDE = 4
 CHIPS = 16
-ROWS_A, ROWS_B, ROWS_C = 336, 352, 336
+THIRDS = ((0, 336), (336, 688), (688, 1024))
 F32 = jnp.float32
 BF16 = jnp.bfloat16
 
@@ -49,10 +49,6 @@
                     for z in range(SIDE):
                         pairs.append((here * SIDE + z, here * SIDE + (z ^ mask)))
     return lax.ppermute(value, BOTH if axis == "z" else "expert", pairs)
-
-
-def after(first, *later):
-    return lax.optimization_barrier((first[-8:, :128], *later))[1:]
 
 
 def grow(value, axis, turn):
@@ -139,13 +135,24 @@
     return head_values.astype(BF16).reshape(requests * steps, -1)
 
 
-def pack_kernel(heads_ref, residual_ref, routing_ref, out_ref):
+def pack_kernel(heads_ref, residual_ref, routing_ref, out_ref, tail, done):
     width = heads_ref.shape[1]
     cols = residual_ref.shape[1] // CHIPS
+    copies = [
+        pltpu.make_async_copy(heads_ref, out_ref.at[chip, :, pl.ds(0, width)], done.at[chip])
+        for chip in range(CHIPS)
+    ]
+    for copy in copies:
+        copy.start()
     for chip in range(CHIPS):
-        out_ref[chip, :, :width] = heads_ref[...]
         part = residual_ref[:, chip * cols : (chip + 1) * cols]
-        out_ref[chip, :, width:] = jnp.concatenate([part, routing_ref[chip]], axis=1)
+        tail[chip] = jnp.concatenate([part, routing_ref[chip]], axis=1)
+    last = pltpu.make_async_copy(
+        tail, out_ref.at[:, :, pl.ds(width, tail.shape[2])], done.at[CHIPS]
+    )
+    last.start()
+    for copy in copies + [last]:
+        copy.wait()
 
 
 def pack(heads, residual, routing):
@@ -154,6 +161,12 @@
     routing = jnp.pad(routing, ((0, 0), (0, 0), (0, 512 - cols - routing.shape[2])))
     return pl.pallas_call(
         pack_kernel,
+        in_specs=[pl.BlockSpec(memory_space=pltpu.VMEM)] * 3,
+        out_specs=pl.BlockSpec(memory_space=pl.ANY),
+        scratch_shapes=[
+            pltpu.VMEM((CHIPS, rows, 512), BF16),
+            pltpu.SemaphoreType.DMA((CHIPS + 1,)),
+        ],
         out_shape=jax.ShapeDtypeStruct((CHIPS, rows, width + 512), BF16),
         cost_estimate=pl.CostEstimate(
             flops=0, bytes_accessed=2 * CHIPS * rows * (width + 512), transcendentals=0
@@ -165,7 +178,7 @@
     place_ref, in_ref, own_ref, other_ref, gain_ref, out_ref, sum_own, sum_other, *, width
 ):
     step = pl.program_id(0)
-    depth = own_ref.shape[1]
+    depth = own_ref.shape[0]
 
     @pl.when(step == 0)
     def _():
@@ -173,9 +186,8 @@
         sum_other[...] = jnp.zeros_like(sum_other)
 
     heads = in_ref[:, pl.ds(pl.multiple_of(step * depth, 128), depth)]
-    dims = (((1,), (1,)), ((), ()))
-    sum_own[...] += lax.dot_general(heads, own_ref[...], dims, preferred_element_type=F32)
-    sum_other[...] += lax.dot_general(heads, other_ref[...], dims, preferred_element_type=F32)
+    sum_own[...] += jnp.dot(heads, own_ref[...], preferred_element_type=F32)
+    sum_other[...] += jnp.dot(heads, other_ref[...], preferred_element_type=F32)
 
     @pl.when(step == pl.num_programs(0) - 1)
     def _():
@@ -199,7 +211,7 @@
 
 def project(place, landed, own, other, gain):
     rows, total = landed.shape
-    cols, width = own.shape
+    width, cols = own.shape
     steps = 4
     depth = width // steps
     out = total - width
@@ -210,8 +222,8 @@
             grid=(steps,),
             in_specs=[
                 pl.BlockSpec((rows, total), lambda i, s: (0, 0)),
-                pl.BlockSpec((cols, depth), lambda i, s: (0, i)),
-                pl.BlockSpec((cols, depth), lambda i, s: (0, i)),
+                pl.BlockSpec((depth, cols), lambda i, s: (i, 0)),
+                pl.BlockSpec((depth, cols), lambda i, s: (i, 0)),
                 pl.BlockSpec((1, 1, 2 * cols), lambda i, s: (s[1], 0, 0)),
             ],
             out_specs=pl.BlockSpec((rows, out), lambda i, s: (0, 0)),
@@ -225,181 +237,155 @@
     )(place, landed, own, other, gain.reshape(CHIPS, 1, 2 * cols))
 
 
-def hidden_kernel(
-    place_ref,
-    a0_ref,
-    a1_ref,
-    b0_ref,
-    b1_ref,
-    c0_ref,
-    c1_ref,
-    wg_ref,
-    wgo_ref,
-    wu_ref,
-    wuo_ref,
-    hidden_ref,
-    index_ref,
-    own_ref,
-    tokens,
-    weight,
-    total,
-    extras,
-    named,
-    arrived,
-    *,
-    model,
-):
-    far_y, far_x = pl.program_id(0), pl.program_id(1)
-    step = far_y * 2 + far_x
-    wide = a0_ref.shape[-1]
+def gather_kernel(place_ref, *refs, units, first, final, model):
+    counts = [len(rows) for rows, _, _ in units]
+    blocks, refs = refs[: sum(counts)], refs[sum(counts) :]
+    sources, refs = refs[:4], refs[4:]
+    if not first:
+        (total_in, own_in), refs = refs[:2], refs[2:]
+    if final:
+        hidden_ref, index_ref, own_ref, total, tokens, weight, arrived = refs
+    else:
+        total, own_ref, tokens, weight, arrived = refs
+    part = sources[0].shape[1]
     cols = model // CHIPS
-    part = wg_ref.shape[1]
-
-    def fetch(at, near):
-        source = pl.ds(pl.multiple_of(place_ref[at * 4 + near] * cols, 64), cols)
+    wide = blocks[0].shape[1]
+    width = 4 * part
+    spare = wide - cols
+
+    def fetch(unit, near):
+        chip = place_ref[units[unit][1] * 4 + near]
+        source = pl.ds(pl.multiple_of(chip * cols, 64), cols)
         return [
             pltpu.make_async_copy(
                 ref.at[source],
-                weight.at[at, pl.ds(near * wide, cols), pl.ds(i * part, part)],
-                arrived.at[at, near, i],
+                weight.at[unit, pl.ds(near * wide, cols), pl.ds(i * part, part)],
+                arrived.at[unit, near, i],
             )
-            for i, ref in enumerate((wg_ref, wgo_ref, wu_ref, wuo_ref))
+            for i, ref in enumerate(sources)
         ]
 
-    @pl.when(step == 0)
-    def _():
+    for unit in range(len(units)):
+        for near in range(4):
+            for copy in fetch(unit, near):
+                copy.start()
+    for unit in range(len(units)):
+        for near in range(4):
+            weight[unit, near * wide + cols : (near + 1) * wide] = jnp.zeros((spare, width), BF16)
+    if first:
         total[...] = jnp.zeros_like(total)
-        extras[...] = jnp.zeros_like(extras)
-        for at in range(4):
-            for near in range(4):
-                for copy in fetch(at, near):
-                    copy.start()
-        for at in range(4):
-            for near in range(4):
-                weight[at, near * wide + cols : (near + 1) * wide] = jnp.zeros(
-                    (wide - cols, weight.shape[2]), BF16
-                )
-
-    def place_rows(far_z, first, value):
-        start = 0
-        while start < value.shape[0]:
-            row = first + start
-            count = min(128 - row % 128, value.shape[0] - start)
-            near_z, near = divmod(row // 128, 4)
-            at = (far_z * 2 + near_z) * 128 + row % 128
-            tokens[at : at + count, near * wide : (near + 1) * wide] = value[start : start + count]
-            start += count
-
-    place_rows(0, 0, a0_ref[0])
-    place_rows(1, 0, a1_ref[0])
-    for bit, ref in ((0, b0_ref), (1, b1_ref)):
-
-        @pl.when(far_x == bit)
-        def _(ref=ref):
-            place_rows(0, ROWS_A, ref[0, 0])
-            place_rows(1, ROWS_A, ref[1, 0])
-
-    for bit, ref in ((0, c0_ref), (1, c1_ref)):
-
-        @pl.when(far_y == bit)
-        def _(ref=ref):
-            place_rows(0, ROWS_A + ROWS_B, ref[0, 0])
-            place_rows(1, ROWS_A + ROWS_B, ref[0, 1])
-
-    for near in range(4):
-        for copy in fetch(step, near):
-            copy.wait()
-    total[...] += jnp.dot(tokens[...], weight[step], preferred_element_type=F32)
-
-    @pl.when(step == 0)
-    def _():
-        named[...] = tokens[:, cols:wide].astype(F32)
+        own_ref[...] = jnp.zeros_like(own_ref)
+    else:
+        total[...] = total_in[...]
+        own_ref[...] = own_in[...]
 
     chip = place_ref[20]
     start = pl.multiple_of((chip // 2) * 16, 16)
-    for near in range(4):
-        extras[...] += tokens[:, near * wide + cols : (near + 1) * wide].astype(F32)
-        mine = tokens[pl.ds(start, 16), near * wide : (near + 1) * wide].astype(F32)
-        own_ref[pl.ds(place_ref[step * 4 + near], 1)] = jnp.where(
-            lax.rem(chip, 2) == 0, mine[:8], mine[8:]
-        )[None]
-
-    @pl.when(step == 3)
-    def _():
-        sums = extras[...]
-        square = (sums[:, 6:7] + sums[:, 7:8]) * (1.0 / model)
+    for unit, (rows, far, far_z) in enumerate(units):
+        here, blocks = blocks[: len(rows)], blocks[len(rows) :]
+        for (low, high), ref in zip(rows, here):
+            row = low
+            while row < high:
+                count = min(128 - row % 128, high - row)
+                near_z, near = divmod(row // 128, 4)
+                at = near_z * 128 + row % 128
+                tokens[at : at + count, near * wide : (near + 1) * wide] = ref[
+                    row - low : row - low + count
+                ]
+                row += count
+        extra = None
+        for near in range(4):
+            term = tokens[:, near * wide + cols : (near + 1) * wide].astype(F32)
+            extra = term if extra is None else extra + term
+            if far == 0 and near == 0:
+                total[far_z, :, width + spare :] = term
+            if far_z == 0:
+                mine = tokens[pl.ds(start, 16), near * wide : (near + 1) * wide].astype(F32)
+                own_ref[pl.ds(place_ref[far * 4 + near], 1)] = jnp.where(
+                    lax.rem(chip, 2) == 0, mine[:8], mine[8:]
+                )[None]
+            for copy in fetch(unit, near):
+                copy.wait()
+        total[far_z, :, width : width + spare] += extra
+        total[far_z, :, :width] += jnp.dot(
+            tokens[...], weight[unit], preferred_element_type=F32
+        )
+    if not final:
+        return
+
+    group = lax.broadcasted_iota(jnp.int32, (128, 1), 0) // 8
+    half = total.shape[1]
+    slots = 4 * 4 * CHIPS
+    lanes = lax.broadcasted_iota(jnp.int32, (1, slots), 1)
+    even = place_ref[21] == 0
+    sums = [None, None]
+    for far_z in range(2):
+        extra = total[far_z, :, width:]
+        square = (extra[:, 6:7] + extra[:, 7:8]) * (1.0 / model)
         inverse = lax.rsqrt(square + EPSILON)
-        names = named[...]
-        group = lax.broadcasted_iota(jnp.int32, (128, 1), 0) // 8
+        names = extra[:, spare:]
         bases = jnp.concatenate(
-            [group * 4 + place_ref[16 + i] * (4 * CHIPS) for i in range(4)], axis=0
+            [group * 4 + place_ref[16 + far_z * 2 + i] * (4 * CHIPS) for i in range(2)], axis=0
         )
-        slots = bases.shape[0] // 2
-        lanes = lax.broadcasted_iota(jnp.int32, (1, slots), 1)
-        even = place_ref[21] == 0
         gates = [names[:, 2 * i : 2 * i + 1] + names[:, 2 * i + 1 : 2 * i + 2] for i in range(2)]
         ranks = [names[:, 4 + i : 5 + i].astype(jnp.int32) for i in range(2)]
         for i in range(2):
-            gate = total[:, i * part : (i + 1) * part] * inverse
-            up = total[:, (2 + i) * part : (3 + i) * part] * inverse
+            gate = total[far_z, :, i * part : (i + 1) * part] * inverse
+            up = total[far_z, :, (2 + i) * part : (3 + i) * part] * inverse
             share = jnp.where(even, gates[i], gates[1 - i])
             rank = jnp.where(even, ranks[i], ranks[1 - i])
             value = gate * (1.0 / (1.0 + jnp.exp(-gate))) * up * share
             place_index = jnp.where(rank < 4, bases + rank, -1)
-            index_ref[:, i : i + 1] = place_index
+            index_ref[far_z * half : (far_z + 1) * half, i : i + 1] = place_index
             hot = (place_index == lanes).astype(BF16)
-            hidden_ref[i] = lax.dot_general(
+            term = lax.dot_general(
                 hot, value.astype(BF16), (((0,), (0,)), ((), ())), preferred_element_type=F32
-            ).astype(BF16)
-
-
-def hidden_values(place, parts, weights):
-    (a0, a1), (b0, b1), (c0, c1) = parts
-    wide = a0.shape[-1]
+            )
+            sums[i] = term if sums[i] is None else sums[i] + term
+    for i in range(2):
+        hidden_ref[i] = sums[i].astype(BF16)
+
+
+def gather_products(place, units, blocks, weights, carried, final):
     model, part = weights[0].shape
-    cols = model // CHIPS
+    wide = blocks[0].shape[1]
+    width = 4 * part
     tok = SIDE * 128
-    a0, a1 = (v.reshape(4, ROWS_A, wide) for v in (a0, a1))
-    b0, b1 = (v.reshape(2, 2, ROWS_B, wide) for v in (b0, b1))
-    c0, c1 = (v.reshape(2, 2, ROWS_C, wide) for v in (c0, c1))
-    a_spec = pl.BlockSpec((1, ROWS_A, wide), lambda y, x, s: (y * 2 + x, 0, 0))
-    b_spec = pl.BlockSpec((2, 1, ROWS_B, wide), lambda y, x, s: (0, y, 0, 0))
-    c_spec = pl.BlockSpec((1, 2, ROWS_C, wide), lambda y, x, s: (x, 0, 0, 0))
+    spare = wide - model // CHIPS
+    whole = lambda *shape: pl.BlockSpec(shape, lambda i, s: (0,) * len(shape))
+    total_shape = (2, tok // 2, width + 2 * spare)
+    own_shape = (CHIPS, 8, wide)
+    scratch = [
+        pltpu.VMEM((tok // 2, 4 * wide), BF16),
+        pltpu.VMEM((len(units), 4 * wide, width), BF16),
+        pltpu.SemaphoreType.DMA((len(units), 4, 4)),
+    ]
+    if final:
+        outs = [((2, tok // 2, part), BF16), ((tok, 2), jnp.int32), (own_shape, F32)]
+        scratch = [pltpu.VMEM(total_shape, F32)] + scratch
+    else:
+        outs = [(total_shape, F32), (own_shape, F32)]
     return pl.pallas_call(
-        functools.partial(hidden_kernel, model=model),
+        functools.partial(
+            gather_kernel, units=units, first=carried is None, final=final, model=model
+        ),
         grid_spec=pltpu.PrefetchScalarGridSpec(
             num_scalar_prefetch=1,
-            grid=(2, 2),
-            in_specs=[a_spec] * 2
-            + [b_spec] * 2
-            + [c_spec] * 2
-            + [pl.BlockSpec(memory_space=pltpu.HBM)] * 4,
-            out_specs=[
-                pl.BlockSpec((2, tok // 2, part), lambda y, x, s: (0, 0, 0)),
-                pl.BlockSpec((tok, 2), lambda y, x, s: (0, 0)),
-                pl.BlockSpec((CHIPS, 8, wide), lambda y, x, s: (0, 0, 0)),
-            ],
-            scratch_shapes=[
-                pltpu.VMEM((tok, 4 * wide), BF16),
-                pltpu.VMEM((4, 4 * wide, 4 * part), BF16),
-                pltpu.VMEM((tok, 4 * part), F32),
-                pltpu.VMEM((tok, wide - cols), F32),
-                pltpu.VMEM((tok, wide - cols), F32),
-                pltpu.SemaphoreType.DMA((4, 4, 4)),
-            ],
-        ),
-        out_shape=[
-            jax.ShapeDtypeStruct((2, tok // 2, part), BF16),
-            jax.ShapeDtypeStruct((tok, 2), jnp.int32),
-            jax.ShapeDtypeStruct((CHIPS, 8, wide), F32),
-        ],
+            grid=(1,),
+            in_specs=[whole(*b.shape) for b in blocks]
+            + [pl.BlockSpec(memory_space=pltpu.HBM)] * 4
+            + ([] if carried is None else [whole(*total_shape), whole(*own_shape)]),
+            out_specs=[whole(*shape) for shape, _ in outs],
+            scratch_shapes=scratch,
+        ),
+        out_shape=[jax.ShapeDtypeStruct(shape, kind) for shape, kind in outs],
         cost_estimate=pl.CostEstimate(
-            flops=8 * tok * CHIPS * wide * part,
-            bytes_accessed=8 * model * part + 2 * tok * CHIPS * wide,
-            transcendentals=2 * tok * part,
-        ),
-        compiler_params=pltpu.CompilerParams(vmem_limit_bytes=50 << 20),
-    )(place, a0, a1, b0, b1, c0, c1, *weights)
+            flops=len(units) * tok * 4 * wide * width,
+            bytes_accessed=len(units) * 8 * wide * width,
+            transcendentals=0,
+        ),
+        compiler_params=pltpu.CompilerParams(vmem_limit_bytes=44 << 20),
+    )(place, *blocks, *weights, *(() if carried is None else carried))
 
 
 def down_kernel(place_ref, index_ref, *refs):
@@ -412,7 +398,7 @@
         for i in range(2):
             hot = (index_ref[:, i : i + 1] == lanes).astype(BF16)
             for k, ref in enumerate(hidden):
-                at = (i * 4 + k) * part
+                at = (i * 4 + (k if i == 0 else (0, 2, 1, 3)[k])) * part
                 spread[:, at : at + part] = jnp.dot(
                     hot, ref[i], preferred_element_type=F32
                 ).astype(BF16)
@@ -437,9 +423,7 @@
             grid=(width // tile,),
             in_specs=[pl.BlockSpec((tok, 2), lambda i, s: (0, 0))]
             + [h_spec] * 4
-            + [
-                pl.BlockSpec((part, tile), lambda i, s: (0, s[22] * 2 + i)),
-            ]
+            + [pl.BlockSpec((part, tile), lambda i, s: (0, s[22] * 2 + i))]
             + [pl.BlockSpec((part, tile), lambda i, s: (0, i))] * 7,
             out_specs=pl.BlockSpec((tok, tile), lambda i, s: (0, i)),
             scratch_shapes=[pltpu.VMEM((tok, 8 * part), BF16)],
@@ -510,10 +494,11 @@
     quarter = model // SIDE
     half = w_down.shape[1]
     cut = lambda v, z: lax.dynamic_slice(v, (0, z * quarter), (half, quarter))
-    lengths, passed = lax.optimization_barrier((lengths, cut(w_down[0], plane ^ first ^ second)))
-    passed = exchange(passed, "z", 0)
-    out_own = out_proj.T
-    out_other = swap_core(out_own)
+    lengths, passed, near = lax.optimization_barrier(
+        (lengths, cut(w_down[0], plane ^ first ^ second), cut(w_down[0], plane ^ first))
+    )
+    passed, near = exchange(passed, "z", 0), exchange(near, "z", 0)
+    out_other = swap_core(out_proj.T)
     gate_own, up_own = w_gate[0], w_up[0]
     gate_other, up_other = swap_core(gate_own), swap_core(up_own)
 
@@ -532,7 +517,6 @@
     sent, out_other, gate_other, up_other, passed, late_down = lax.optimization_barrier(
         (sent, out_other, gate_other, up_other, passed, w_down[0])
     )
-    near = exchange(cut(late_down, plane ^ first), "z", 0)
     far = exchange(cut(late_down, plane ^ second), "z", 1)
     lane_plane = [
         [expert_of(y, x, core) for y in range(SIDE) for x in range(SIDE)] for core in range(2)
@@ -544,41 +528,56 @@
     block = project(
         jnp.stack([core, chip]).astype(jnp.int32),
         landed.reshape(CHIPS * rows, -1),
-        out_own,
-        out_other,
+        out_proj,
+        out_other.T,
         norm_gain,
     )
+    last = exchange(passed, "z", 1)
     block = grow(block, "x", 0)
     block = grow(block, "y", 0)
+    block, last = lax.optimization_barrier((block, last))
     block = grow(block, "z", 0)
-    part_a = block[:ROWS_A]
-    part_b = block[ROWS_A : ROWS_A + ROWS_B]
-    part_c = block[ROWS_A + ROWS_B :]
-    part_a, part_b, part_c = grow(part_a, "x", 1), grow(part_b, "y", 1), grow(part_c, "z", 1)
-    part_a, part_b, part_c = grow(part_a, "y", 1), grow(part_b, "z", 1), grow(part_c, "x", 1)
-    late_down, near_sent, far_sent = after(part_a, w_down[0], near, far)
-    first_other = swap_core(cut(late_down, plane))
-    near_other, far_other = swap_core(near_sent), swap_core(far_sent)
-    parts = (
-        (part_a, exchange(part_a, "z", 1)),
-        (part_b, exchange(part_b, "x", 1)),
-        (part_c, exchange(part_c, "y", 1)),
-    )
-    (passed,) = after(parts[2][1], passed)
-    last = exchange(passed, "z", 1)
-    hidden, index, own = hidden_values(
-        place, parts, (gate_own, gate_other, up_own, up_other)
-    )
-    index, last = lax.optimization_barrier((index, last))
-    last_other = swap_core(last)
+    others = [swap_core(v) for v in (cut(late_down, plane), near, far, last)]
+    weights = (gate_own, gate_other, up_own, up_other)
+    all_rows = (THIRDS[0][:1] + THIRDS[-1][1:],)
+    by_x, by_y, by_z = exchange(block, "x", 1), exchange(block, "y", 1), exchange(block, "z", 1)
+    carried = gather_products(place, ((all_rows, 0, 0),), (block,), weights, None, False)
+    own, on_x = lax.optimization_barrier((carried[1], by_x))
+    own, on_y = lax.optimization_barrier((own, by_y))
+    own, on_z, *others[:2] = lax.optimization_barrier((own, by_z, *others[:2]))
+    carried = (carried[0], own)
+    by_xy, by_yz, by_xz = exchange(on_x, "y", 1), exchange(on_y, "z", 1), exchange(on_z, "x", 1)
+    carried = gather_products(
+        place,
+        ((all_rows, 1, 0), (all_rows, 2, 0), (all_rows, 0, 1)),
+        (by_x, by_y, by_z),
+        weights,
+        carried,
+        False,
+    )
+    cuts = [
+        value[low:high] for value, (low, high) in zip((by_xy, by_yz, by_xz), THIRDS)
+    ]
+    own, cuts[0] = lax.optimization_barrier((carried[1], cuts[0]))
+    own, cuts[1] = lax.optimization_barrier((own, cuts[1]))
+    own, cuts[2], others[2], others[3] = lax.optimization_barrier(
+        (own, cuts[2], others[2], others[3])
+    )
+    carried = (carried[0], own)
+    thirds = [exchange(value, axis, 1) for value, axis in zip(cuts, "zxy")]
+    carried = gather_products(
+        place,
+        ((all_rows, 3, 0), (all_rows, 2, 1), (all_rows, 1, 1)),
+        (by_xy, by_yz, by_xz),
+        weights,
+        carried,
+        False,
+    )
+    hidden, index, own = gather_products(
+        place, ((THIRDS, 3, 1),), tuple(thirds), weights, carried, True
+    )
     spread = [hidden, exchange(hidden, "z", 0), exchange(hidden, "z", 1), shift_z(hidden, 2)]
-    sums = down(
-        place,
-        index,
-        spread,
-        (w_down[0], near, far, last),
-        (first_other, far_other, near_other, last_other),
-    )
+    sums = down(place, index, spread, (w_down[0], near, far, last), others)
     lane_all = [
         [expert_of(y, x, core) * SIDE + z for z in range(SIDE) for y in range(SIDE) for x in range(SIDE)]
         for core in range(2)

time: 207 us -> 183 us (0.88)
  waiting for transfers between devices: 99.8 us -> 57 us
  local copies, waits for them, and re-layouts: 11 us -> 19.3 us
  starting transfers between devices: 47.8 us -> 54.4 us
  Pallas kernels: 41.3 us -> 47.6 us
  other arithmetic: 4.9 us -> 2.18 us
    ppermute x18, waiting for transfers between devices: 73.4 us -> 30.3 us  [exchange(): return lax.ppermute(value, BOTH if axis == 'z' else 'expert', pairs)]
    pallas_call x2 -> x5, Pallas kernels: 19.8 us -> 26.5 us  [the longest x4 24.4 us: gather_products(): pl.pallas_call(functools.partial(gather_kernel, units=units, first=carrie...]
    ppermute x18, starting transfers between devices: 29.2 us -> 35.8 us  [exchange(): return lax.ppermute(value, BOTH if axis == 'z' else 'expert', pairs)]
    unnamed x19 -> x23, local copies, waits for them, and re-layouts: 4.44 us -> 8.76 us
    optimization_barrier x0 -> x1, local copies, waits for them, and re-layouts: none -> 3.95 us  [per_device(): lax.optimization_barrier((sent, out_other, gate_other, up_other, passed,...]
    concatenate x9 -> x2, other arithmetic: 2.77 us -> 0.05 us  [grow(): return jnp.concatenate([value, exchange(value, axis, turn)], axis=0)]
    dynamic_slice x3 -> x2, local copies, waits for them, and re-layouts: 5.44 us -> 5.36 us  [per_device(): cut = lambda v, z: lax.dynamic_slice(v, (0, z * quarter), (half, quarter))]
  transfers between devices with their start and end apart: 28 -> 28, of which waited for: 14 -> 10; matrix products, arithmetic and copies ran while one was open for 6% -> 9% of each run, Pallas kernels for 14% -> 19%
where the time goes in v2:
time: 183 us
  waiting for transfers between devices  57 us (31%)
  starting transfers between devices  54.4 us (30%)
  Pallas kernels  47.6 us (26%)
  local copies, waits for them, and re-layouts  19.3 us (11%)
  other arithmetic  2.18 us (1%)
    ppermute x18, starting transfers between devices, exchange(): return lax.ppermute(value, BOTH if axis == 'z' else 'expert', pairs)  35.8 us
    ppermute x18, waiting for transfers between devices, exchange(): return lax.ppermute(value, BOTH if axis == 'z' else 'expert', pairs)  30.3 us
    all_to_all x1, waiting for transfers between devices, per_device(): lax.all_to_all(sums.reshape(SIDE * CHIPS, rows, quarter), BOTH, split_axi...  25.6 us
    pallas_call x4, Pallas kernels, gather_products(): pl.pallas_call(functools.partial(gather_kernel, units=units, first=carrie...  24.4 us
    pallas_call x1, Pallas kernels, attention_heads(): pl.pallas_call(functools.partial(attend_kernel, scale=scale, heads=heads)...  9.95 us
    pallas_call x1, Pallas kernels, down(): pl.pallas_call(down_kernel, grid_spec=pltpu.PrefetchScalarGridSpec(num_sc...  8.97 us
    unnamed x23, local copies, waits for them, and re-layouts  8.76 us
    all_to_all x1, starting transfers between devices, per_device(): lax.all_to_all(sent, 'expert', split_axis=0, concat_axis=0, tiled=True, a...  7.13 us
  transfers between devices with their start and end apart: 28, of which 10 were waited for; matrix products, arithmetic and copies ran while one was open for 9% of the time, Pallas kernels for 19%

profile of v2, /device:TPU:0, one launch (start us, length us, event | category | flops | bytes accessed | tf_op | source)
XLA Modules:
  0.0 182.5 jit_solution(4232812533656541943)
XLA Ops:
  0.0 0.5 collective-permute-start.2
  0.5 2.5 %dynamic-slice_bitcast_fusion = (bf16[256,1792]{1,0:T(8,128)(2,1)}, bf16[256,1792]{1,0:T(8,128)(2,1)S(1)}) fusion(bf16[1,256,7168]{2,1,0:T(8,128)(2,1)} %param.31, s32[]{:T(128)S(6)} %select_n.51, s32[]{:T(128)S(6)} %select_n.50), kind=kLoop, calls=%fused_computation.5 | loop fusion | bytes 3670024 | tf_op jit(solution)/shard_map/dynamic_slice | solution.py:496
  3.0 2.0 %collective-permute-start.3 = (bf16[256,1792]{1,0:T(8,128)(2,1)S(1)}, bf16[256,1792]{1,0:T(8,128)(2,1)}, u32[]{:S(2)}, u32[]{:S(2)}) collective-permute-start(bf16[256,1792]{1,0:T(8,128)(2,1)S(1)} %get-tuple-element.45), channel_id=1, source_target_pairs={{0,1},{1,0},{2,3},{3,2},{4,7},{5,6},{6,5},{7,4},{8,9},{9,8},{10,11... | collective-permute-start | bytes 2752520 | tf_op jit(solution)/shard_map/ppermute | solution.py:51
  5.1 10.0 %shard_map.154 = bf16[4,64,512]{2,1,0:T(8,128)(2,1)} custom-call(s32[4]{0:T(128)} %length_ref, bf16[4,64,512]{2,1,0:T(8,128)(2,1)} %bitcast.89, bf16[4,64,64]{2,1,0:T(8,128)(2,1)} %bitcast.93, bf16[4,2048,512]{2,1,0:T(8,128)(2,1)} %latent_ref.1, bf16[4,64,2048]{2,1,0:T(8,128)(2,1)} %rope_ref.1, bf16[4,2,512]{2,1,0:T(2,128)(2,1)} %fresh_ref.1, ...), custom_call_target="tpu_custom_call" | custom-call | flops 1140850688 | bytes 9437184 | tf_op jit(solution)/shard_map/pallas_call | solution.py:98
  15.1 1.7 fusion.5
  16.8 0.1 fusion.12
  17.0 0.7 copy.65
  17.6 0.1 multiply_reduce_fusion
  17.7 0.1 copy.52
  17.8 0.2 copy.53
  18.0 0.1 select_reduce_fusion
  18.1 0.1 copy.48
  18.2 0.1 copy.51
  18.3 0.2 copy.54
  18.5 0.7 fusion.11.routing_ref
  19.2 2.1 %shard_map.155 = bf16[16,8,4608]{2,1,0:T(8,128)(2,1)} custom-call(bf16[8,4096]{1,0:T(8,128)(2,1)} %bitcast.90, bf16[8,7168]{1,0:T(8,128)(2,1)} %residual_ref.1, bf16[16,8,64]{2,1,0:T(8,128)(2,1)} %fusion.11.routing_ref), custom_call_target="tpu_custom_call" | custom-call | bytes 1179648 | tf_op jit(solution)/shard_map/pallas_call | solution.py:162
  21.3 1.2 copy-done.4
  22.5 7.1 %all-to-all-start = ((bf16[16,8,4608]{2,1,0:T(8,128)(2,1)}), bf16[16,8,4608]{2,1,0:T(8,128)(2,1)S(1)}, u32[]{:S(2)}, u32[]{:S(2)}) async-start(bf16[16,8,4608]{2,1,0:T(8,128)(2,1)} %shard_map.155), calls=%async_computation | async-start | bytes 2359296 | tf_op jit(solution)/shard_map/all_to_all | solution.py:524
  29.7 2.8 %constant_dynamic-slice_fusion = (bf16[256,1792]{1,0:T(8,128)(2,1)}, bf16[256,1792]{1,0:T(8,128)(2,1)}) fusion(bf16[256,7168]{1,0:T(8,128)(2,1)} %bitcast.83, s32[]{:T(128)S(6)} %select_n.57, s32[]{:T(128)S(6)} %select_n.56), kind=kLoop, calls=%fused_computation.32 | loop fusion | bytes 3670024 | tf_op jit(solution)/shard_map/dynamic_slice | solution.py:496
  32.5 4.0 %collective-permute-start.5 = (bf16[256,1792]{1,0:T(8,128)(2,1)}, bf16[256,1792]{1,0:T(8,128)(2,1)}, u32[]{:S(2)}, u32[]{:S(2)}) collective-permute-start(bf16[256,1792]{1,0:T(8,128)(2,1)} %get-tuple-element.84), channel_id=1, source_target_pairs={{0,3},{1,2},{2,1},{3,0},{4,5},{5,4},{6,7},{7,6},{8,11},{9,10},{10,... | collective-permute-start | bytes 2752520 | tf_op jit(solution)/shard_map/ppermute | solution.py:51
  36.6 3.2 %copy.56.own_ref = bf16[4096,224]{1,0:T(8,128)(2,1)S(1)} copy(bf16[4096,224]{0,1:T(8,128)(2,1)} %param.25) | data formatting | bytes 3670016 | tf_op args[9]
  39.8 0.1 reshape.82.gain_ref
  40.0 3.9 %copy.55 = bf16[224,4096]{0,1:T(8,128)(2,1)} copy(bf16[224,4096]{1,0:T(8,128)(2,1)} %copy-done.4) | data formatting | bytes 3670016 | tf_op jit(solution)/shard_map/optimization_barrier | solution.py:517
  43.9 4.3 %collective-permute-done.5.refs_6_ = bf16[256,1792]{1,0:T(8,128)(2,1)} collective-permute-done((bf16[256,1792]{1,0:T(8,128)(2,1)}, bf16[256,1792]{1,0:T(8,128)(2,1)}, u32[]{:S(2)}, u32[]{:S(2)}) %collective-permute-start.5) | collective-permute-done | bytes 917536 | tf_op jit(solution)/shard_map/ppermute | solution.py:51
  48.2 1.0 all-to-all-done
  49.3 1.6 copy-done.2
  50.9 2.2 %shard_map.156 = bf16[128,512]{1,0:T(8,128)(2,1)S(1)} custom-call(s32[2]{0:T(128)S(1)} %pad_add_fusion.place_ref, bf16[128,4608]{1,0:T(8,128)(2,1)S(1)} %bitcast.77, bf16[4096,224]{1,0:T(8,128)(2,1)S(1)} %copy.56.own_ref, bf16[4096,224]{1,0:T(8,128)(2,1)S(1)} %bitcast.76, bf16[16,1,448]{2,1,0:T(2,128)(2,1)S(1)} %reshape.82.gain_ref), custom_call_target="tpu_custom_call" | custom-call | flops 469762048 | bytes 3670016 | tf_op jit(solution)/shard_map/pallas_call | solution.py:218
  53.0 1.0 collective-permute-start.6
  54.0 4.1 %collective-permute-done.6 = bf16[128,512]{1,0:T(8,128)(2,1)S(1)} collective-permute-done((bf16[128,512]{1,0:T(8,128)(2,1)S(1)}, bf16[128,512]{1,0:T(8,128)(2,1)S(1)}, u32[]{:S(2)}, u32[]{:S(2)}) %collective-permute-start.6) | collective-permute-done | bytes 131104 | tf_op jit(solution)/shard_map/ppermute | solution.py:51
  58.1 1.0 collective-permute-start.7
  59.0 5.5 %collective-permute-done.7 = bf16[256,512]{1,0:T(8,128)(2,1)S(1)} collective-permute-done((bf16[256,512]{1,0:T(8,128)(2,1)S(1)}, bf16[256,512]{1,0:T(8,128)(2,1)S(1)}, u32[]{:S(2)}, u32[]{:S(2)}) %collective-permute-start.7) | collective-permute-done | bytes 262176 | tf_op jit(solution)/shard_map/ppermute | solution.py:51
  64.6 2.0 %collective-permute-start.9 = (bf16[512,512]{1,0:T(8,128)(2,1)S(1)}, bf16[512,512]{1,0:T(8,128)(2,1)S(1)}, u32[]{:S(2)}, u32[]{:S(2)}) collective-permute-start(bf16[512,512]{1,0:T(8,128)(2,1)S(1)} %pad_maximum_fusion), channel_id=1, source_target_pairs={{0,1},{1,0},{2,3},{3,2},{4,7},{5,6},{6,5},{7,4},{8,9},{9,8},{10,11... | collective-permute-start | bytes 1572872 | tf_op jit(solution)/shard_map/ppermute | solution.py:51
  66.7 7.2 %collective-permute-done.9 = bf16[512,512]{1,0:T(8,128)(2,1)S(1)} collective-permute-done((bf16[512,512]{1,0:T(8,128)(2,1)S(1)}, bf16[512,512]{1,0:T(8,128)(2,1)S(1)}, u32[]{:S(2)}, u32[]{:S(2)}) %collective-permute-start.9) | collective-permute-done | bytes 524320 | tf_op jit(solution)/shard_map/ppermute | solution.py:51
  73.9 2.2 %collective-permute-start.10 = (bf16[1024,512]{1,0:T(8,128)(2,1)S(1)}, bf16[1024,512]{1,0:T(8,128)(2,1)}, u32[]{:S(2)}, u32[]{:S(2)}) collective-permute-start(bf16[1024,512]{1,0:T(8,128)(2,1)S(1)} %constant_dynamic-update-slice_fusion.refs_0_), channel_id=1, source_target_pairs={{0,24},{4,12},{8,16},{12,4},{16,8},{20,28},{24,0},{28,20},{32,56},... | collective-permute-start | bytes 3145736 | tf_op jit(solution)/shard_map/ppermute | solution.py:51
  76.1 2.7 %collective-permute-start.11 = (bf16[1024,512]{1,0:T(8,128)(2,1)S(1)}, bf16[1024,512]{1,0:T(8,128)(2,1)S(1)}, u32[]{:S(2)}, u32[]{:S(2)}) collective-permute-start(bf16[1024,512]{1,0:T(8,128)(2,1)S(1)} %constant_dynamic-update-slice_fusion.refs_0_), channel_id=1, source_target_pairs={{0,96},{4,36},{8,104},{12,44},{16,112},{20,52},{24,120},{28,60},{3... | collective-permute-start | bytes 3145736 | tf_op jit(solution)/shard_map/ppermute | solution.py:51
  78.7 3.9 %collective-permute-start.12 = (bf16[1024,512]{1,0:T(8,128)(2,1)S(1)}, bf16[1024,512]{1,0:T(8,128)(2,1)S(1)}, u32[]{:S(2)}, u32[]{:S(2)}) collective-permute-start(bf16[1024,512]{1,0:T(8,128)(2,1)S(1)} %constant_dynamic-update-slice_fusion.refs_0_), channel_id=1, source_target_pairs={{0,3},{1,2},{2,1},{3,0},{4,5},{5,4},{6,7},{7,6},{8,11},{9,10},{10,... | collective-permute-start | bytes 3145736 | tf_op jit(solution)/shard_map/ppermute | solution.py:51
  82.6 0.5 collective-permute-start.14
  83.1 0.1 stack.107.place_ref
  83.2 2.0 %copy-done = bf16[1,7168,256]{2,1,0:T(8,128)(2,1)S(1)} copy-done((bf16[1,7168,256]{2,1,0:T(8,128)(2,1)S(1)}, bf16[1,7168,256]{2,1,0:T(8,128)(2,1)}, u32[]{:S(2)}) %copy-start) | copy-done | bytes 3670040
  85.3 3.9 %shard_map.157 = (f32[2,256,1152]{2,1,0:T(8,128)S(1)}, f32[16,8,512]{2,1,0:T(8,128)S(1)}) custom-call(s32[24]{0:T(128)S(1)} %stack.107.place_ref, bf16[1024,512]{1,0:T(8,128)(2,1)S(1)} %constant_dynamic-update-slice_fusion.refs_0_, bf16[7168,256]{1,0:T(8,128)(2,1)S(1)} %bitcast.74, bf16[7168,256]{1,0:T(8,128)(2,1)} %collective-permute-done.1.refs_2_.refs_4_, ...), custom_call_target="tpu_custom_call" | custom-call | flops 1073741824 | bytes 4194304 | tf_op jit(solution)/shard_map/pallas_call | solution.py:368
  89.1 0.9 collective-permute-done.10.refs_0_
  90.1 2.1 %collective-permute-start.15 = (bf16[1024,512]{1,0:T(8,128)(2,1)}, bf16[1024,512]{1,0:T(8,128)(2,1)S(1)}, u32[]{:S(2)}, u32[]{:S(2)}) collective-permute-start(bf16[1024,512]{1,0:T(8,128)(2,1)} %collective-permute-done.10.refs_0_), channel_id=1, source_target_pairs={{0,96},{4,36},{8,104},{12,44},{16,112},{20,52},{24,120},{28,60},{3... | collective-permute-start | bytes 3145736 | tf_op jit(solution)/shard_map/ppermute | solution.py:51
  92.2 6.5 %collective-permute-start.17 = (bf16[1024,512]{1,0:T(8,128)(2,1)S(1)}, bf16[1024,512]{1,0:T(8,128)(2,1)S(1)}, u32[]{:S(2)}, u32[]{:S(2)}) collective-permute-start(bf16[1024,512]{1,0:T(8,128)(2,1)S(1)} %collective-permute-done.11.refs_1_), channel_id=1, source_target_pairs={{0,3},{1,2},{2,1},{3,0},{4,5},{5,4},{6,7},{7,6},{8,11},{9,10},{10,... | collective-permute-start | bytes 3145736 | tf_op jit(solution)/shard_map/ppermute | solution.py:51
  98.6 1.7 collective-permute-start.19
  100.4 0.5 collective-permute-start.21
  100.9 8.6 %shard_map.158 = (f32[2,256,1152]{2,1,0:T(8,128)S(1)}, f32[16,8,512]{2,1,0:T(8,128)S(1)}) custom-call(s32[24]{0:T(128)S(1)} %stack.107.place_ref, bf16[1024,512]{1,0:T(8,128)(2,1)} %collective-permute-done.10.refs_0_, bf16[1024,512]{1,0:T(8,128)(2,1)S(1)} %collective-permute-done.11.refs_1_, bf16[1024,512]{1,0:T(8,128)(2,1)S(1)} %collective-permute-done.12.refs_2_, ...), custom_call_target="tpu_custom_call" | custom-call | flops 3221225472 | bytes 12582912 | tf_op jit(solution)/shard_map/pallas_call | solution.py:368
  109.5 1.9 %collective-permute-done.17.refs_1_ = bf16[1024,512]{1,0:T(8,128)(2,1)S(1)} collective-permute-done((bf16[1024,512]{1,0:T(8,128)(2,1)S(1)}, bf16[1024,512]{1,0:T(8,128)(2,1)S(1)}, u32[]{:S(2)}, u32[]{:S(2)}) %collective-permute-start.17) | collective-permute-done | bytes 1048608 | tf_op jit(solution)/shard_map/ppermute | solution.py:51
  111.4 1.7 collective-permute-start.18
  113.2 3.2 %collective-permute-start.16 = (bf16[336,512]{1,0:T(8,128)(2,1)S(1)}, bf16[336,512]{1,0:T(8,128)(2,1)S(1)}, u32[]{:S(2)}, u32[]{:S(2)}) collective-permute-start(bf16[336,512]{1,0:T(8,128)(2,1)S(1)} %slice.16), channel_id=1, source_target_pairs={{0,3},{1,2},{2,1},{3,0},{4,5},{5,4},{6,7},{7,6},{8,11},{9,10},{10,... | collective-permute-start | bytes 1032200 | tf_op jit(solution)/shard_map/ppermute | solution.py:51
  116.5 1.5 collective-permute-start.22
  118.0 7.4 %shard_map.159 = (f32[2,256,1152]{2,1,0:T(8,128)S(1)}, f32[16,8,512]{2,1,0:T(8,128)S(1)}) custom-call(s32[24]{0:T(128)S(1)} %stack.107.place_ref, bf16[1024,512]{1,0:T(8,128)(2,1)S(1)} %collective-permute-done.15.refs_0_, bf16[1024,512]{1,0:T(8,128)(2,1)S(1)} %collective-permute-done.17.refs_1_, bf16[1024,512]{1,0:T(8,128)(2,1)S(1)} %collective-permute-done.19.refs_2_, ...), custom_call_target="tpu_custom_call" | custom-call | flops 3221225472 | bytes 12582912 | tf_op jit(solution)/shard_map/pallas_call | solution.py:368
  125.5 4.6 %shard_map.160 = (bf16[2,256,256]{2,1,0:T(8,128)(2,1)S(1)}, s32[512,2]{1,0:T(8,128)S(1)}, f32[16,8,512]{2,1,0:T(8,128)S(1)}) custom-call(s32[24]{0:T(128)S(1)} %stack.107.place_ref, bf16[336,512]{1,0:T(8,128)(2,1)S(1)} %collective-permute-done.16.refs_0_, bf16[352,512]{1,0:T(8,128)(2,1)S(1)} %collective-permute-done.18.refs_1_, ...), custom_call_target="tpu_custom_call" | custom-call | flops 1073741824 | bytes 4194304 | tf_op jit(solution)/shard_map/pallas_call | solution.py:368
  130.1 0.1 collective-permute-start.23
  130.2 0.1 collective-permute-start.24
  130.3 4.0 %collective-permute-start.25 = (bf16[2,256,256]{2,1,0:T(8,128)(2,1)S(1)}, bf16[2,256,256]{2,1,0:T(8,128)(2,1)S(1)}, u32[]{:S(2)}, u32[]{:S(2)}) collective-permute-start(bf16[2,256,256]{2,1,0:T(8,128)(2,1)S(1)} %get-tuple-element.78.refs_0_), channel_id=1, source_target_pairs={{0,2},{1,3},{2,0},{3,1},{4,6},{5,7},{6,4},{7,5},{8,10},{9,11},{10,... | collective-permute-start | bytes 786440 | tf_op jit(solution)/shard_map/ppermute | solution.py:34
  134.3 2.3 %collective-permute-done.23.refs_1_ = bf16[2,256,256]{2,1,0:T(8,128)(2,1)S(1)} collective-permute-done((bf16[2,256,256]{2,1,0:T(8,128)(2,1)S(1)}, bf16[2,256,256]{2,1,0:T(8,128)(2,1)S(1)}, u32[]{:S(2)}, u32[]{:S(2)}) %collective-permute-start.23) | collective-permute-done | bytes 262176 | tf_op jit(solution)/shard_map/ppermute | solution.py:51
  136.5 4.1 %collective-permute-done.24.refs_2_ = bf16[2,256,256]{2,1,0:T(8,128)(2,1)S(1)} collective-permute-done((bf16[2,256,256]{2,1,0:T(8,128)(2,1)S(1)}, bf16[2,256,256]{2,1,0:T(8,128)(2,1)S(1)}, u32[]{:S(2)}, u32[]{:S(2)}) %collective-permute-start.24) | collective-permute-done | bytes 262176 | tf_op jit(solution)/shard_map/ppermute | solution.py:51
  140.7 9.0 %shard_map.161 = bf16[512,1792]{1,0:T(8,128)(2,1)} custom-call(s32[24]{0:T(128)S(1)} %stack.107.place_ref, s32[512,2]{1,0:T(8,128)S(1)} %get-tuple-element.77.index_ref, bf16[2,256,256]{2,1,0:T(8,128)(2,1)S(1)} %get-tuple-element.78.refs_0_, bf16[2,256,256]{2,1,0:T(8,128)(2,1)S(1)} %collective-permute-done.23.refs_1_, ...), custom_call_target="tpu_custom_call" | custom-call | flops 3758096384 | bytes 7340032 | tf_op jit(solution)/shard_map/pallas_call | solution.py:419
  149.6 6.0 %all-to-all-start.1 = ((bf16[64,8,1792]{2,1,0:T(8,128)(2,1)}), bf16[64,8,1792]{2,1,0:T(8,128)(2,1)S(1)}, u32[]{:S(2)}, u32[]{:S(2)}) async-start(bf16[64,8,1792]{2,1,0:T(8,128)(2,1)} %bitcast.85), calls=%async_computation.1 | async-start | bytes 3670016 | tf_op jit(solution)/shard_map/all_to_all | solution.py:585
  155.7 0.2 copy.58
  155.8 0.1 reshape.77
  156.0 25.6 %all-to-all-done.1 = bf16[64,8,1792]{2,1,0:T(8,128)(2,1)S(1)} async-done(((bf16[64,8,1792]{2,1,0:T(8,128)(2,1)}), bf16[64,8,1792]{2,1,0:T(8,128)(2,1)S(1)}, u32[]{:S(2)}, u32[]{:S(2)}) %all-to-all-start.1) | async-done | bytes 1835040 | tf_op jit(solution)/shard_map/all_to_all | solution.py:585
  181.6 0.2 convert_reduce_fusion
  181.8 0.7 add_convert_fusion
  (58 shorter events, 0.6 us)
Async XLA Ops:
  0.0 21.3 %collective-permute-start.1 = (bf16[7168,256]{1,0:T(8,128)(2,1)}, bf16[7168,256]{1,0:T(8,128)(2,1)}, u32[]{:S(2)}, u32[]{:S(2)}) collective-permute-start(bf16[7168,256]{1,0:T(8,128)(2,1)} %bitcast.71), channel_id=1, source_target_pairs={{0,4},{4,0},{8,12},{12,8},{16,20},{20,16},{24,28},{28,24},{32,36},... | collective-permute-start | bytes 11010056 | tf_op jit(solution)/shard_map/ppermute | solution.py:29
  0.0 21.3 %collective-permute-start.2 = (bf16[7168,256]{1,0:T(8,128)(2,1)}, bf16[7168,256]{1,0:T(8,128)(2,1)}, u32[]{:S(2)}, u32[]{:S(2)}) collective-permute-start(bf16[7168,256]{1,0:T(8,128)(2,1)} %bitcast.78), channel_id=1, source_target_pairs={{0,4},{4,0},{8,12},{12,8},{16,20},{20,16},{24,28},{28,24},{32,36},... | collective-permute-start | bytes 11010056 | tf_op jit(solution)/shard_map/ppermute | solution.py:29
  0.5 20.8 %collective-permute-start = (bf16[224,4096]{1,0:T(8,128)(2,1)}, bf16[224,4096]{1,0:T(8,128)(2,1)S(1)}, u32[]{:S(2)}, u32[]{:S(2)}) collective-permute-start(bf16[224,4096]{1,0:T(8,128)(2,1)} %bitcast.86), channel_id=1, source_target_pairs={{0,4},{4,0},{8,12},{12,8},{16,20},{20,16},{24,28},{28,24},{32,36},... | collective-permute-start | bytes 5505032 | tf_op jit(solution)/shard_map/ppermute | solution.py:29
  3.0 18.2 %collective-permute-start.3 = (bf16[256,1792]{1,0:T(8,128)(2,1)S(1)}, bf16[256,1792]{1,0:T(8,128)(2,1)}, u32[]{:S(2)}, u32[]{:S(2)}) collective-permute-start(bf16[256,1792]{1,0:T(8,128)(2,1)S(1)} %get-tuple-element.45), channel_id=1, source_target_pairs={{0,1},{1,0},{2,3},{3,2},{4,7},{5,6},{6,5},{7,4},{8,9},{9,8},{10,11... | collective-permute-start | bytes 2752520 | tf_op jit(solution)/shard_map/ppermute | solution.py:51
  5.0 38.9 %collective-permute-start.4 = (bf16[256,1792]{1,0:T(8,128)(2,1)}, bf16[256,1792]{1,0:T(8,128)(2,1)}, u32[]{:S(2)}, u32[]{:S(2)}) collective-permute-start(bf16[256,1792]{1,0:T(8,128)(2,1)} %get-tuple-element.47), channel_id=1, source_target_pairs={{0,1},{1,0},{2,3},{3,2},{4,7},{5,6},{6,5},{7,4},{8,9},{9,8},{10,11... | collective-permute-start | bytes 2752520 | tf_op jit(solution)/shard_map/ppermute | solution.py:51
  5.1 10.0 %copy-start.3 = (bf16[32,512,128]{2,1,0:T(8,128)(2,1)S(1)}, bf16[32,512,128]{2,1,0:T(8,128)(2,1)}, u32[]{:S(2)}) copy-start(bf16[32,512,128]{2,1,0:T(8,128)(2,1)} %param.24) | copy-start | bytes 12582916
  15.0 1.8 copy-start.6
  15.0 3.0 %copy-start.7 = (f32[8,8]{1,0:T(8,128)S(1)}, f32[8,8]{1,0:T(8,128)}, u32[]{:S(2)}) copy-start(f32[8,8]{1,0:T(8,128)} %param.28) | copy-start | bytes 772
  21.3 1.2 copy-start.4
  22.5 26.7 %all-to-all-start = ((bf16[16,8,4608]{2,1,0:T(8,128)(2,1)}), bf16[16,8,4608]{2,1,0:T(8,128)(2,1)S(1)}, u32[]{:S(2)}, u32[]{:S(2)}) async-start(bf16[16,8,4608]{2,1,0:T(8,128)(2,1)} %shard_map.155), calls=%async_computation | async-start | bytes 2359296 | tf_op jit(solution)/shard_map/all_to_all | solution.py:524
  29.7 10.1 %copy-start.5 = (bf16[7168]{0:T(1024)(128)(2,1)S(1)}, bf16[7168]{0:T(1024)(128)(2,1)}, u32[]{:S(2)}) copy-start(bf16[7168]{0:T(1024)(128)(2,1)} %param.26) | copy-start | bytes 43012
  32.5 15.7 %collective-permute-start.5 = (bf16[256,1792]{1,0:T(8,128)(2,1)}, bf16[256,1792]{1,0:T(8,128)(2,1)}, u32[]{:S(2)}, u32[]{:S(2)}) collective-permute-start(bf16[256,1792]{1,0:T(8,128)(2,1)} %get-tuple-element.84), channel_id=1, source_target_pairs={{0,3},{1,2},{2,1},{3,0},{4,5},{5,4},{6,7},{7,6},{8,11},{9,10},{10,... | collective-permute-start | bytes 2752520 | tf_op jit(solution)/shard_map/ppermute | solution.py:51
  36.5 28.0 %collective-permute-start.8 = (bf16[256,1792]{1,0:T(8,128)(2,1)}, bf16[256,1792]{1,0:T(8,128)(2,1)}, u32[]{:S(2)}, u32[]{:S(2)}) collective-permute-start(bf16[256,1792]{1,0:T(8,128)(2,1)} %collective-permute-done.3), channel_id=1, source_target_pairs={{0,3},{1,2},{2,1},{3,0},{4,5},{5,4},{6,7},{7,6},{8,11},{9,10},{10,... | collective-permute-start | bytes 2752520 | tf_op jit(solution)/shard_map/ppermute | solution.py:51
  49.3 1.6 copy-start.2
  53.0 5.0 %collective-permute-start.6 = (bf16[128,512]{1,0:T(8,128)(2,1)S(1)}, bf16[128,512]{1,0:T(8,128)(2,1)S(1)}, u32[]{:S(2)}, u32[]{:S(2)}) collective-permute-start(bf16[128,512]{1,0:T(8,128)(2,1)S(1)} %shard_map.156), channel_id=1, source_target_pairs={{0,8},{4,28},{8,0},{12,20},{16,24},{20,12},{24,16},{28,4},{32,40},... | collective-permute-start | bytes 393224 | tf_op jit(solution)/shard_map/ppermute | solution.py:51
  58.1 6.5 %collective-permute-start.7 = (bf16[256,512]{1,0:T(8,128)(2,1)S(1)}, bf16[256,512]{1,0:T(8,128)(2,1)S(1)}, u32[]{:S(2)}, u32[]{:S(2)}) collective-permute-start(bf16[256,512]{1,0:T(8,128)(2,1)S(1)} %pad_maximum_fusion.1), channel_id=1, source_target_pairs={{0,32},{4,100},{8,40},{12,108},{16,48},{20,116},{24,56},{28,124},{... | collective-permute-start | bytes 786440 | tf_op jit(solution)/shard_map/ppermute | solution.py:51
  64.6 9.3 %collective-permute-start.9 = (bf16[512,512]{1,0:T(8,128)(2,1)S(1)}, bf16[512,512]{1,0:T(8,128)(2,1)S(1)}, u32[]{:S(2)}, u32[]{:S(2)}) collective-permute-start(bf16[512,512]{1,0:T(8,128)(2,1)S(1)} %pad_maximum_fusion), channel_id=1, source_target_pairs={{0,1},{1,0},{2,3},{3,2},{4,7},{5,6},{6,5},{7,4},{8,9},{9,8},{10,11... | collective-permute-start | bytes 1572872 | tf_op jit(solution)/shard_map/ppermute | solution.py:51
  73.9 16.2 %collective-permute-start.10 = (bf16[1024,512]{1,0:T(8,128)(2,1)S(1)}, bf16[1024,512]{1,0:T(8,128)(2,1)}, u32[]{:S(2)}, u32[]{:S(2)}) collective-permute-start(bf16[1024,512]{1,0:T(8,128)(2,1)S(1)} %constant_dynamic-update-slice_fusion.refs_0_), channel_id=1, source_target_pairs={{0,24},{4,12},{8,16},{12,4},{16,8},{20,28},{24,0},{28,20},{32,56},... | collective-permute-start | bytes 3145736 | tf_op jit(solution)/shard_map/ppermute | solution.py:51
  76.1 16.1 %collective-permute-start.11 = (bf16[1024,512]{1,0:T(8,128)(2,1)S(1)}, bf16[1024,512]{1,0:T(8,128)(2,1)S(1)}, u32[]{:S(2)}, u32[]{:S(2)}) collective-permute-start(bf16[1024,512]{1,0:T(8,128)(2,1)S(1)} %constant_dynamic-update-slice_fusion.refs_0_), channel_id=1, source_target_pairs={{0,96},{4,36},{8,104},{12,44},{16,112},{20,52},{24,120},{28,60},{3... | collective-permute-start | bytes 3145736 | tf_op jit(solution)/shard_map/ppermute | solution.py:51
  78.7 19.9 %collective-permute-start.12 = (bf16[1024,512]{1,0:T(8,128)(2,1)S(1)}, bf16[1024,512]{1,0:T(8,128)(2,1)S(1)}, u32[]{:S(2)}, u32[]{:S(2)}) collective-permute-start(bf16[1024,512]{1,0:T(8,128)(2,1)S(1)} %constant_dynamic-update-slice_fusion.refs_0_), channel_id=1, source_target_pairs={{0,3},{1,2},{2,1},{3,0},{4,5},{5,4},{6,7},{7,6},{8,11},{9,10},{10,... | collective-permute-start | bytes 3145736 | tf_op jit(solution)/shard_map/ppermute | solution.py:51
  82.6 16.0 %collective-permute-start.13 = (bf16[256,1792]{1,0:T(8,128)(2,1)}, bf16[256,1792]{1,0:T(8,128)(2,1)}, u32[]{:S(2)}, u32[]{:S(2)}) collective-permute-start(bf16[256,1792]{1,0:T(8,128)(2,1)} %get-tuple-element.83), channel_id=1, source_target_pairs={{0,4},{4,0},{8,12},{12,8},{16,20},{20,16},{24,28},{28,24},{32,36},... | collective-permute-start | bytes 2752520 | tf_op jit(solution)/shard_map/ppermute | solution.py:29
  82.6 16.0 %collective-permute-start.14 = (bf16[256,1792]{1,0:T(8,128)(2,1)}, bf16[256,1792]{1,0:T(8,128)(2,1)}, u32[]{:S(2)}, u32[]{:S(2)}) collective-permute-start(bf16[256,1792]{1,0:T(8,128)(2,1)} %collective-permute-done.4.refs_5_), channel_id=1, source_target_pairs={{0,4},{4,0},{8,12},{12,8},{16,20},{20,16},{24,28},{28,24},{32,36},... | collective-permute-start | bytes 2752520 | tf_op jit(solution)/shard_map/ppermute | solution.py:29
  83.2 2.0 %copy-start = (bf16[1,7168,256]{2,1,0:T(8,128)(2,1)S(1)}, bf16[1,7168,256]{2,1,0:T(8,128)(2,1)}, u32[]{:S(2)}) copy-start(bf16[1,7168,256]{2,1,0:T(8,128)(2,1)} %param.29) | copy-start | bytes 11010052
  90.1 19.4 %collective-permute-start.15 = (bf16[1024,512]{1,0:T(8,128)(2,1)}, bf16[1024,512]{1,0:T(8,128)(2,1)S(1)}, u32[]{:S(2)}, u32[]{:S(2)}) collective-permute-start(bf16[1024,512]{1,0:T(8,128)(2,1)} %collective-permute-done.10.refs_0_), channel_id=1, source_target_pairs={{0,96},{4,36},{8,104},{12,44},{16,112},{20,52},{24,120},{28,60},{3... | collective-permute-start | bytes 3145736 | tf_op jit(solution)/shard_map/ppermute | solution.py:51
  92.2 19.2 %collective-permute-start.17 = (bf16[1024,512]{1,0:T(8,128)(2,1)S(1)}, bf16[1024,512]{1,0:T(8,128)(2,1)S(1)}, u32[]{:S(2)}, u32[]{:S(2)}) collective-permute-start(bf16[1024,512]{1,0:T(8,128)(2,1)S(1)} %collective-permute-done.11.refs_1_), channel_id=1, source_target_pairs={{0,3},{1,2},{2,1},{3,0},{4,5},{5,4},{6,7},{7,6},{8,11},{9,10},{10,... | collective-permute-start | bytes 3145736 | tf_op jit(solution)/shard_map/ppermute | solution.py:51
  98.6 17.8 %collective-permute-start.19 = (bf16[1024,512]{1,0:T(8,128)(2,1)S(1)}, bf16[1024,512]{1,0:T(8,128)(2,1)S(1)}, u32[]{:S(2)}, u32[]{:S(2)}) collective-permute-start(bf16[1024,512]{1,0:T(8,128)(2,1)S(1)} %collective-permute-done.12.refs_2_), channel_id=1, source_target_pairs={{0,24},{4,12},{8,16},{12,4},{16,8},{20,28},{24,0},{28,20},{32,56},... | collective-permute-start | bytes 3145736 | tf_op jit(solution)/shard_map/ppermute | solution.py:51
  100.4 16.1 %collective-permute-start.20 = (bf16[256,1792]{1,0:T(8,128)(2,1)}, bf16[256,1792]{1,0:T(8,128)(2,1)S(1)}, u32[]{:S(2)}, u32[]{:S(2)}) collective-permute-start(bf16[256,1792]{1,0:T(8,128)(2,1)} %collective-permute-done.5.refs_6_), channel_id=1, source_target_pairs={{0,4},{4,0},{8,12},{12,8},{16,20},{20,16},{24,28},{28,24},{32,36},... | collective-permute-start | bytes 2752520 | tf_op jit(solution)/shard_map/ppermute | solution.py:29
  100.4 16.1 %collective-permute-start.21 = (bf16[256,1792]{1,0:T(8,128)(2,1)}, bf16[256,1792]{1,0:T(8,128)(2,1)S(1)}, u32[]{:S(2)}, u32[]{:S(2)}) collective-permute-start(bf16[256,1792]{1,0:T(8,128)(2,1)} %collective-permute-done.8.refs_7_), channel_id=1, source_target_pairs={{0,4},{4,0},{8,12},{12,8},{16,20},{20,16},{24,28},{28,24},{32,36},... | collective-permute-start | bytes 2752520 | tf_op jit(solution)/shard_map/ppermute | solution.py:29
  111.4 14.0 %collective-permute-start.18 = (bf16[352,512]{1,0:T(8,128)(2,1)S(1)}, bf16[352,512]{1,0:T(8,128)(2,1)S(1)}, u32[]{:S(2)}, u32[]{:S(2)}) collective-permute-start(bf16[352,512]{1,0:T(8,128)(2,1)S(1)} %slice.17), channel_id=1, source_target_pairs={{0,24},{4,12},{8,16},{12,4},{16,8},{20,28},{24,0},{28,20},{32,56},... | collective-permute-start | bytes 1081352 | tf_op jit(solution)/shard_map/ppermute | solution.py:51
  113.2 12.2 %collective-permute-start.16 = (bf16[336,512]{1,0:T(8,128)(2,1)S(1)}, bf16[336,512]{1,0:T(8,128)(2,1)S(1)}, u32[]{:S(2)}, u32[]{:S(2)}) collective-permute-start(bf16[336,512]{1,0:T(8,128)(2,1)S(1)} %slice.16), channel_id=1, source_target_pairs={{0,3},{1,2},{2,1},{3,0},{4,5},{5,4},{6,7},{7,6},{8,11},{9,10},{10,... | collective-permute-start | bytes 1032200 | tf_op jit(solution)/shard_map/ppermute | solution.py:51
  116.5 8.9 %copy-start.8 = (bf16[256,1792]{1,0:T(8,128)(2,1)}, bf16[256,1792]{1,0:T(8,128)(2,1)S(1)}, u32[]{:S(2)}) copy-start(bf16[256,1792]{1,0:T(8,128)(2,1)S(1)} %collective-permute-done.20.refs_10_) | copy-start | bytes 2752516
  116.5 8.9 %copy-start.9 = (bf16[256,1792]{1,0:T(8,128)(2,1)}, bf16[256,1792]{1,0:T(8,128)(2,1)S(1)}, u32[]{:S(2)}) copy-start(bf16[256,1792]{1,0:T(8,128)(2,1)S(1)} %collective-permute-done.21.refs_11_) | copy-start | bytes 2752516
  116.5 8.9 %collective-permute-start.22 = (bf16[336,512]{1,0:T(8,128)(2,1)S(1)}, bf16[336,512]{1,0:T(8,128)(2,1)S(1)}, u32[]{:S(2)}, u32[]{:S(2)}) collective-permute-start(bf16[336,512]{1,0:T(8,128)(2,1)S(1)} %slice.18), channel_id=1, source_target_pairs={{0,96},{4,36},{8,104},{12,44},{16,112},{20,52},{24,120},{28,60},{3... | collective-permute-start | bytes 1032200 | tf_op jit(solution)/shard_map/ppermute | solution.py:51
  118.0 7.4 %copy-start.1 = (bf16[1,7168,256]{2,1,0:T(8,128)(2,1)S(1)}, bf16[1,7168,256]{2,1,0:T(8,128)(2,1)}, u32[]{:S(2)}) copy-start(bf16[1,7168,256]{2,1,0:T(8,128)(2,1)} %param.29) | copy-start | bytes 11010052
  130.1 6.5 %collective-permute-start.23 = (bf16[2,256,256]{2,1,0:T(8,128)(2,1)S(1)}, bf16[2,256,256]{2,1,0:T(8,128)(2,1)S(1)}, u32[]{:S(2)}, u32[]{:S(2)}) collective-permute-start(bf16[2,256,256]{2,1,0:T(8,128)(2,1)S(1)} %get-tuple-element.78.refs_0_), channel_id=1, source_target_pairs={{0,1},{1,0},{2,3},{3,2},{4,7},{5,6},{6,5},{7,4},{8,9},{9,8},{10,11... | collective-permute-start | bytes 786440 | tf_op jit(solution)/shard_map/ppermute | solution.py:51
  130.2 10.5 %collective-permute-start.24 = (bf16[2,256,256]{2,1,0:T(8,128)(2,1)S(1)}, bf16[2,256,256]{2,1,0:T(8,128)(2,1)S(1)}, u32[]{:S(2)}, u32[]{:S(2)}) collective-permute-start(bf16[2,256,256]{2,1,0:T(8,128)(2,1)S(1)} %get-tuple-element.78.refs_0_), channel_id=1, source_target_pairs={{0,3},{1,2},{2,1},{3,0},{4,5},{5,4},{6,7},{7,6},{8,11},{9,10},{10,... | collective-permute-start | bytes 786440 | tf_op jit(solution)/shard_map/ppermute | solution.py:51
  130.3 10.4 %collective-permute-start.25 = (bf16[2,256,256]{2,1,0:T(8,128)(2,1)S(1)}, bf16[2,256,256]{2,1,0:T(8,128)(2,1)S(1)}, u32[]{:S(2)}, u32[]{:S(2)}) collective-permute-start(bf16[2,256,256]{2,1,0:T(8,128)(2,1)S(1)} %get-tuple-element.78.refs_0_), channel_id=1, source_target_pairs={{0,2},{1,3},{2,0},{3,1},{4,6},{5,7},{6,4},{7,5},{8,10},{9,11},{10,... | collective-permute-start | bytes 786440 | tf_op jit(solution)/shard_map/ppermute | solution.py:34
  149.6 32.0 %all-to-all-start.1 = ((bf16[64,8,1792]{2,1,0:T(8,128)(2,1)}), bf16[64,8,1792]{2,1,0:T(8,128)(2,1)S(1)}, u32[]{:S(2)}, u32[]{:S(2)}) async-start(bf16[64,8,1792]{2,1,0:T(8,128)(2,1)} %bitcast.85), calls=%async_computation.1 | async-start | bytes 3670016 | tf_op jit(solution)/shard_map/all_to_all | solution.py:585

commit v3 on v2

--- a/solution.py
+++ b/solution.py
@@ -11,7 +11,7 @@
 BOTH = ("expert", "tensor")
 SIDE = 4
 CHIPS = 16
-THIRDS = ((0, 336), (336, 688), (688, 1024))
+HALVES = ((0, 512), (512, 1024))
 F32 = jnp.float32
 BF16 = jnp.bfloat16
 
@@ -51,8 +51,9 @@
     return lax.ppermute(value, BOTH if axis == "z" else "expert", pairs)
 
 
-def grow(value, axis, turn):
-    return jnp.concatenate([value, exchange(value, axis, turn)], axis=0)
+def pairs_of(core):
+    mask = masks_of(core)[0]
+    return [(v, v ^ mask) for v in range(SIDE) if v < v ^ mask]
 
 
 def attend_kernel(length_ref, q_ref, qr_ref, latent_ref, rope_ref, fresh_ref, fresh_rope_ref, out_ref, *, scale, heads):
@@ -127,26 +128,54 @@
         new_rope,
     )
     head_values = jnp.einsum(
-        "rshl,hlv->rshv",
+        "rshl,hlv->hrsv",
         mixed.reshape(requests, steps, heads, latent),
         value_proj,
         preferred_element_type=F32,
     )
-    return head_values.astype(BF16).reshape(requests * steps, -1)
-
-
-def pack_kernel(heads_ref, residual_ref, routing_ref, out_ref, tail, done):
-    width = heads_ref.shape[1]
+    return head_values.astype(BF16).reshape(heads, requests * steps, -1)
+
+
+def pack_kernel(
+    heads_ref, residual_ref, ids_ref, gates_ref, out_ref, values, tail, done
+):
+    heads, rows, each = heads_ref.shape
+    width = heads * each
     cols = residual_ref.shape[1] // CHIPS
+    for head in range(heads):
+        values[:, head * each : (head + 1) * each] = heads_ref[head]
     copies = [
-        pltpu.make_async_copy(heads_ref, out_ref.at[chip, :, pl.ds(0, width)], done.at[chip])
+        pltpu.make_async_copy(values, out_ref.at[chip, :, pl.ds(0, width)], done.at[chip])
         for chip in range(CHIPS)
     ]
     for copy in copies:
         copy.start()
+    lane = lax.broadcasted_iota(jnp.int32, (rows, 128), 1)
+    gates = jnp.zeros((rows, 128), F32)
+    named = jnp.zeros((rows, 128), F32)
+    for k in range(ids_ref.shape[1]):
+        match = ids_ref[:, k : k + 1] == lane
+        gates = gates + jnp.where(match, gates_ref[:, k : k + 1], 0.0)
+        named = named + jnp.where(match, 1.0, 0.0)
+    above = lax.broadcasted_iota(jnp.int32, (rows, rows), 1)
+    below = above < lax.broadcasted_iota(jnp.int32, (rows, rows), 0)
+    below = jnp.where(below, 1.0, 0.0).astype(BF16)
+    rank = jnp.dot(below, named.astype(BF16), preferred_element_type=F32)
+    rank = jnp.where(named > 0.5, rank, 8.0)
+    high = gates.astype(BF16).astype(F32)
+    low = gates - high
     for chip in range(CHIPS):
+        at = 128 - 2 * chip
+        picked = jnp.where(
+            lane < 2,
+            pltpu.roll(high, at % 128, 1),
+            jnp.where(
+                lane < 4, pltpu.roll(low, (at + 2) % 128, 1), pltpu.roll(rank, (at + 4) % 128, 1)
+            ),
+        )
+        picked = jnp.where(lane < 6, picked, 0.0)[:, : 512 - cols]
         part = residual_ref[:, chip * cols : (chip + 1) * cols]
-        tail[chip] = jnp.concatenate([part, routing_ref[chip]], axis=1)
+        tail[chip] = jnp.concatenate([part, picked.astype(BF16)], axis=1)
     last = pltpu.make_async_copy(
         tail, out_ref.at[:, :, pl.ds(width, tail.shape[2])], done.at[CHIPS]
     )
@@ -155,15 +184,15 @@
         copy.wait()
 
 
-def pack(heads, residual, routing):
-    rows, width = heads.shape
-    cols = residual.shape[1] // CHIPS
-    routing = jnp.pad(routing, ((0, 0), (0, 0), (0, 512 - cols - routing.shape[2])))
+def pack(heads, residual, ids, gates):
+    count, rows, each = heads.shape
+    width = count * each
     return pl.pallas_call(
         pack_kernel,
-        in_specs=[pl.BlockSpec(memory_space=pltpu.VMEM)] * 3,
+        in_specs=[pl.BlockSpec(memory_space=pltpu.VMEM)] * 4,
         out_specs=pl.BlockSpec(memory_space=pl.ANY),
         scratch_shapes=[
+            pltpu.VMEM((rows, width), BF16),
             pltpu.VMEM((CHIPS, rows, 512), BF16),
             pltpu.SemaphoreType.DMA((CHIPS + 1,)),
         ],
@@ -171,7 +200,7 @@
         cost_estimate=pl.CostEstimate(
             flops=0, bytes_accessed=2 * CHIPS * rows * (width + 512), transcendentals=0
         ),
-    )(heads, residual, routing)
+    )(heads, residual, ids, gates)
 
 
 def project_kernel(
@@ -206,7 +235,9 @@
         lane = lax.broadcasted_iota(jnp.int32, extra.shape, 1)
         extra = jnp.where(lane == 6, high, jnp.where(lane == 7, low, extra))
         stream = stream * gain_ref[0].astype(F32)
-        out_ref[...] = jnp.concatenate([stream, extra], axis=1).astype(BF16)
+        value = jnp.concatenate([stream, extra], axis=1).astype(BF16)
+        for i in range(out_ref.shape[0]):
+            out_ref[i] = value
 
 
 def project(place, landed, own, other, gain):
@@ -226,10 +257,10 @@
                 pl.BlockSpec((depth, cols), lambda i, s: (i, 0)),
                 pl.BlockSpec((1, 1, 2 * cols), lambda i, s: (s[1], 0, 0)),
             ],
-            out_specs=pl.BlockSpec((rows, out), lambda i, s: (0, 0)),
+            out_specs=pl.BlockSpec((8, rows, out), lambda i, s: (0, 0, 0)),
             scratch_shapes=[pltpu.VMEM((rows, cols), F32)] * 2,
         ),
-        out_shape=jax.ShapeDtypeStruct((rows, out), BF16),
+        out_shape=jax.ShapeDtypeStruct((8, rows, out), BF16),
         cost_estimate=pl.CostEstimate(
             flops=4 * rows * width * cols, bytes_accessed=4 * width * cols, transcendentals=0
         ),
@@ -280,7 +311,7 @@
         own_ref[...] = own_in[...]
 
     chip = place_ref[20]
-    start = pl.multiple_of((chip // 2) * 16, 16)
+    start = pl.multiple_of(place_ref[24] * 128 + (chip // 2) * 16, 16)
     for unit, (rows, far, far_z) in enumerate(units):
         here, blocks = blocks[: len(rows)], blocks[len(rows) :]
         for (low, high), ref in zip(rows, here):
@@ -297,8 +328,6 @@
         for near in range(4):
             term = tokens[:, near * wide + cols : (near + 1) * wide].astype(F32)
             extra = term if extra is None else extra + term
-            if far == 0 and near == 0:
-                total[far_z, :, width + spare :] = term
             if far_z == 0:
                 mine = tokens[pl.ds(start, 16), near * wide : (near + 1) * wide].astype(F32)
                 own_ref[pl.ds(place_ref[far * 4 + near], 1)] = jnp.where(
@@ -306,6 +335,11 @@
                 )[None]
             for copy in fetch(unit, near):
                 copy.wait()
+        if far == 0:
+            at = pl.multiple_of(place_ref[23] * wide + cols // 128 * 128, 128)
+            total[far_z, :, width + spare :] = tokens[:, pl.ds(at, 128)][:, cols % 128 :].astype(
+                F32
+            )
         total[far_z, :, width : width + spare] += extra
         total[far_z, :, :width] += jnp.dot(
             tokens[...], weight[unit], preferred_element_type=F32
@@ -327,7 +361,7 @@
         bases = jnp.concatenate(
             [group * 4 + place_ref[16 + far_z * 2 + i] * (4 * CHIPS) for i in range(2)], axis=0
         )
-        gates = [names[:, 2 * i : 2 * i + 1] + names[:, 2 * i + 1 : 2 * i + 2] for i in range(2)]
+        gates = [names[:, i : i + 1] + names[:, 2 + i : 3 + i] for i in range(2)]
         ranks = [names[:, 4 + i : 5 + i].astype(jnp.int32) for i in range(2)]
         for i in range(2):
             gate = total[far_z, :, i * part : (i + 1) * part] * inverse
@@ -432,24 +466,8 @@
         cost_estimate=pl.CostEstimate(
             flops=16 * tok * part * width, bytes_accessed=16 * part * width, transcendentals=0
         ),
-        compiler_params=pltpu.CompilerParams(vmem_limit_bytes=48 << 20),
+        compiler_params=pltpu.CompilerParams(vmem_limit_bytes=28 << 20),
     )(place, index, *hidden, *own, *other)
-
-
-def routing_columns(expert_ids, expert_gates):
-    rows, count = expert_ids.shape
-    experts = 2 * CHIPS
-    hot = expert_ids[:, :, None] == jnp.arange(experts, dtype=jnp.int32)
-    gates = jnp.sum(jnp.where(hot, expert_gates[:, :, None], 0.0), axis=1)
-    named = jnp.any(hot, axis=1)
-    ones = named.astype(F32)
-    below = jnp.tril(jnp.ones((rows, rows), F32), -1)
-    rank = jnp.where(named, jnp.sum(below[:, :, None] * ones[None], axis=1), 8.0)
-    high = lax.reduce_precision(gates, 8, 7)
-    low = gates - high
-    pair = lambda v: v.reshape(rows, CHIPS, 2).transpose(1, 0, 2)
-    gate_pair = jnp.stack([pair(high), pair(low)], axis=-1).reshape(CHIPS, rows, 4)
-    return jnp.concatenate([gate_pair, pair(rank)], axis=-1).astype(BF16)
 
 
 def per_device(
@@ -477,18 +495,22 @@
     chip = expert // 2
     first = jnp.where(core == 0, 1, 3)
     second = 4 - first
+    pair = lambda v: (jnp.minimum(v, v ^ first), jnp.maximum(v, v ^ first))
+    row, column = chip // SIDE, chip % SIDE
     table = []
     for far_y in range(2):
         for far_x in range(2):
             for near_y in range(2):
                 for near_x in range(2):
-                    mask_x = (first * near_x) ^ (second * far_x)
-                    mask_y = (first * near_y) ^ (second * far_y)
-                    table.append(chip ^ (mask_y * SIDE + mask_x))
+                    table.append(
+                        pair(row ^ (second * far_y))[near_y] * SIDE
+                        + pair(column ^ (second * far_x))[near_x]
+                    )
     for far_z in range(2):
         for near_z in range(2):
-            table.append(plane ^ ((first * near_z) ^ (second * far_z)))
-    table += [chip, core, plane, chip]
+            table.append(pair(plane ^ (second * far_z))[near_z])
+    is_high = lambda v: jnp.where(v == pair(v)[1], 1, 0)
+    table += [chip, core, plane, is_high(row) * 2 + is_high(column), is_high(plane)]
     place = jnp.stack([jnp.asarray(v, jnp.int32) for v in table])
 
     quarter = model // SIDE
@@ -513,10 +535,11 @@
         value_proj,
     )
     cols = model // CHIPS
-    sent = pack(heads, residual, routing_columns(expert_ids, expert_gates))
+    sent = pack(heads, residual, expert_ids, expert_gates)
     sent, out_other, gate_other, up_other, passed, late_down = lax.optimization_barrier(
         (sent, out_other, gate_other, up_other, passed, w_down[0])
     )
+    here = cut(late_down, plane)
     far = exchange(cut(late_down, plane ^ second), "z", 1)
     lane_plane = [
         [expert_of(y, x, core) for y in range(SIDE) for x in range(SIDE)] for core in range(2)
@@ -533,13 +556,20 @@
         norm_gain,
     )
     last = exchange(passed, "z", 1)
-    block = grow(block, "x", 0)
-    block = grow(block, "y", 0)
-    block, last = lax.optimization_barrier((block, last))
-    block = grow(block, "z", 0)
-    others = [swap_core(v) for v in (cut(late_down, plane), near, far, last)]
+    cubes = [
+        [expert_of(y, x, core) * SIDE + z for z in z_pair for y in y_pair for x in x_pair]
+        for core in range(2)
+        for z_pair in pairs_of(core)
+        for y_pair in pairs_of(core)
+        for x_pair in pairs_of(core)
+    ]
+    block = lax.all_to_all(
+        block, BOTH, split_axis=0, concat_axis=0, tiled=True, axis_index_groups=cubes
+    )
+    block, last = lax.optimization_barrier((block.reshape(-1, block.shape[-1]), last))
+    others = [swap_core(v) for v in (here, near, far, last)]
     weights = (gate_own, gate_other, up_own, up_other)
-    all_rows = (THIRDS[0][:1] + THIRDS[-1][1:],)
+    all_rows = ((0, 1024),)
     by_x, by_y, by_z = exchange(block, "x", 1), exchange(block, "y", 1), exchange(block, "z", 1)
     carried = gather_products(place, ((all_rows, 0, 0),), (block,), weights, None, False)
     own, on_x = lax.optimization_barrier((carried[1], by_x))
@@ -555,16 +585,13 @@
         carried,
         False,
     )
-    cuts = [
-        value[low:high] for value, (low, high) in zip((by_xy, by_yz, by_xz), THIRDS)
-    ]
+    cuts = [value[low:high] for value, (low, high) in zip((by_xy, by_yz), HALVES)]
     own, cuts[0] = lax.optimization_barrier((carried[1], cuts[0]))
-    own, cuts[1] = lax.optimization_barrier((own, cuts[1]))
-    own, cuts[2], others[2], others[3] = lax.optimization_barrier(
-        (own, cuts[2], others[2], others[3])
+    own, cuts[1], others[2], others[3] = lax.optimization_barrier(
+        (own, cuts[1], others[2], others[3])
     )
     carried = (carried[0], own)
-    thirds = [exchange(value, axis, 1) for value, axis in zip(cuts, "zxy")]
+    halves = [exchange(value, axis, 1) for value, axis in zip(cuts, "zx")]
     carried = gather_products(
         place,
         ((all_rows, 3, 0), (all_rows, 2, 1), (all_rows, 1, 1)),
@@ -574,7 +601,7 @@
         False,
     )
     hidden, index, own = gather_products(
-        place, ((THIRDS, 3, 1),), tuple(thirds), weights, carried, True
+        place, ((HALVES, 3, 1),), tuple(halves), weights, carried, True
     )
     spread = [hidden, exchange(hidden, "z", 0), exchange(hidden, "z", 1), shift_z(hidden, 2)]
     sums = down(place, index, spread, (w_down[0], near, far, last), others)

time: 183 us -> 176 us (0.962)
  starting transfers between devices: 54.4 us -> 47.6 us
    ppermute x18 -> x14, waiting for transfers between devices: 30.3 us -> 20.2 us  [exchange(): return lax.ppermute(value, BOTH if axis == 'z' else 'expert', pairs)]
    all_to_all x0 -> x1, waiting for transfers between devices: none -> 9.95 us  [per_device(): lax.all_to_all(block, BOTH, split_axis=0, concat_axis=0, tiled=True, axis...]
    ppermute x18 -> x14, starting transfers between devices: 35.8 us -> 27.8 us  [exchange(): return lax.ppermute(value, BOTH if axis == 'z' else 'expert', pairs)]
    all_to_all x0 -> x1, starting transfers between devices: none -> 3.56 us  [per_device(): lax.all_to_all(block, BOTH, split_axis=0, concat_axis=0, tiled=True, axis...]
    unnamed x23 -> x25, local copies, waits for them, and re-layouts: 8.76 us -> 9.13 us
  transfers between devices with their start and end apart: 28 -> 25, of which waited for: 10 -> 10; matrix products, arithmetic and copies ran while one was open for 9% -> 9% of each run, Pallas kernels for 19% -> 20%
where the time goes in v3:
time: 176 us; the launch traced here: 175 us
  waiting for transfers between devices  56.7 us (32%)
  Pallas kernels  47.8 us (27%)
  starting transfers between devices  47.6 us (27%)
  local copies, waits for them, and re-layouts  19.7 us (11%)
    ppermute x14, starting transfers between devices, exchange(): return lax.ppermute(value, BOTH if axis == 'z' else 'expert', pairs)  27.8 us
    all_to_all x1, waiting for transfers between devices, per_device(): lax.all_to_all(sums.reshape(SIDE * CHIPS, rows, quarter), BOTH, split_axi...  25.5 us
    pallas_call x4, Pallas kernels, gather_products(): pl.pallas_call(functools.partial(gather_kernel, units=units, first=carrie...  24.7 us
    ppermute x14, waiting for transfers between devices, exchange(): return lax.ppermute(value, BOTH if axis == 'z' else 'expert', pairs)  20.2 us
    all_to_all x1, waiting for transfers between devices, per_device(): lax.all_to_all(block, BOTH, split_axis=0, concat_axis=0, tiled=True, axis...  9.95 us
    pallas_call x1, Pallas kernels, attention_heads(): pl.pallas_call(functools.partial(attend_kernel, scale=scale, heads=heads)...  9.95 us
    unnamed x25, local copies, waits for them, and re-layouts  9.13 us
    pallas_call x1, Pallas kernels, down(): pl.pallas_call(down_kernel, grid_spec=pltpu.PrefetchScalarGridSpec(num_sc...  8.59 us
  transfers between devices with their start and end apart: 25, of which 10 were waited for; matrix products, arithmetic and copies ran while one was open for 9% of the time, Pallas kernels for 20%

profile of v3, /device:TPU:0, one launch (start us, length us, event | category | flops | bytes accessed | tf_op | source)
XLA Modules:
  0.0 174.8 jit_solution(9394351310387713791)
XLA Ops:
  0.0 0.0 collective-permute-start.1
  0.0 0.5 collective-permute-start.2
  0.5 2.5 %dynamic-slice_bitcast_fusion = (bf16[256,1792]{1,0:T(8,128)(2,1)}, bf16[256,1792]{1,0:T(8,128)(2,1)S(1)}) fusion(bf16[1,256,7168]{2,1,0:T(8,128)(2,1)} %param.31, s32[]{:T(128)S(6)} %select_n.52, s32[]{:T(128)S(6)} %select_n.51), kind=kLoop, calls=%fused_computation.4 | loop fusion | bytes 3670024 | tf_op jit(solution)/shard_map/dynamic_slice | solution.py:518
  3.0 2.0 %collective-permute-start.3 = (bf16[256,1792]{1,0:T(8,128)(2,1)S(1)}, bf16[256,1792]{1,0:T(8,128)(2,1)}, u32[]{:S(2)}, u32[]{:S(2)}) collective-permute-start(bf16[256,1792]{1,0:T(8,128)(2,1)S(1)} %get-tuple-element.43), channel_id=1, source_target_pairs={{0,1},{1,0},{2,3},{3,2},{4,7},{5,6},{6,5},{7,4},{8,9},{9,8},{10,11... | collective-permute-start | bytes 2752520 | tf_op jit(solution)/shard_map/ppermute | solution.py:51
  5.0 0.0 collective-permute-start.4
  5.1 9.9 %shard_map.154 = bf16[4,64,512]{2,1,0:T(8,128)(2,1)} custom-call(s32[4]{0:T(128)} %length_ref, bf16[4,64,512]{2,1,0:T(8,128)(2,1)} %bitcast.77, bf16[4,64,64]{2,1,0:T(8,128)(2,1)} %bitcast.79, bf16[4,2048,512]{2,1,0:T(8,128)(2,1)} %latent_ref.1, bf16[4,64,2048]{2,1,0:T(8,128)(2,1)} %rope_ref.1, bf16[4,2,512]{2,1,0:T(2,128)(2,1)} %fresh_ref.1, ...), custom_call_target="tpu_custom_call" | custom-call | flops 1140850688 | bytes 9437184 | tf_op jit(solution)/shard_map/pallas_call | solution.py:99
  15.0 1.7 fusion.2
  16.7 0.7 copy.28
  17.4 2.4 %shard_map.155 = bf16[16,8,4608]{2,1,0:T(8,128)(2,1)} custom-call(bf16[32,8,128]{2,1,0:T(8,128)(2,1)} %bitcast.78, bf16[8,7168]{1,0:T(8,128)(2,1)} %residual_ref.1, s32[8,8]{1,0:T(8,128)} %ids_ref.1, f32[8,8]{1,0:T(8,128)} %gates_ref.1), custom_call_target="tpu_custom_call" | custom-call | bytes 1179648 | tf_op jit(solution)/shard_map/pallas_call | solution.py:190
  19.8 0.0 collective-permute-done.3
  19.9 0.0 collective-permute-done.1.refs_2_.refs_4_.refs_3_
  19.9 0.0 collective-permute-done.2.refs_4_.refs_6_.refs_5_
  19.9 1.2 copy-done.10
  21.1 7.1 %all-to-all-start = ((bf16[16,8,4608]{2,1,0:T(8,128)(2,1)}), bf16[16,8,4608]{2,1,0:T(8,128)(2,1)S(1)}, u32[]{:S(2)}, u32[]{:S(2)}) async-start(bf16[16,8,4608]{2,1,0:T(8,128)(2,1)} %shard_map.155), calls=%async_computation | async-start | bytes 2359296 | tf_op jit(solution)/shard_map/all_to_all | solution.py:547
  28.2 0.0 copy-start.11
  28.2 2.8 %constant_dynamic-slice_fusion = (bf16[256,1792]{1,0:T(8,128)(2,1)}, bf16[256,1792]{1,0:T(8,128)(2,1)}) fusion(bf16[256,7168]{1,0:T(8,128)(2,1)} %bitcast.67, s32[]{:T(128)S(6)} %select_n.54, s32[]{:T(128)S(6)} %select_n.53), kind=kLoop, calls=%fused_computation.9 | loop fusion | bytes 3670024 | tf_op jit(solution)/shard_map/dynamic_slice | solution.py:518
  31.0 4.0 %collective-permute-start.5 = (bf16[256,1792]{1,0:T(8,128)(2,1)}, bf16[256,1792]{1,0:T(8,128)(2,1)}, u32[]{:S(2)}, u32[]{:S(2)}) collective-permute-start(bf16[256,1792]{1,0:T(8,128)(2,1)} %get-tuple-element.80), channel_id=1, source_target_pairs={{0,3},{1,2},{2,1},{3,0},{4,5},{5,4},{6,7},{7,6},{8,11},{9,10},{10,... | collective-permute-start | bytes 2752520 | tf_op jit(solution)/shard_map/ppermute | solution.py:51
  35.1 3.2 %copy.30.own_ref = bf16[4096,224]{1,0:T(8,128)(2,1)S(1)} copy(bf16[4096,224]{0,1:T(8,128)(2,1)} %param.25) | data formatting | bytes 3670016 | tf_op args[9]
  38.3 0.1 reshape.48.gain_ref
  38.4 0.1 pad_add_fusion.place_ref
  38.5 4.0 %copy.29 = bf16[224,4096]{0,1:T(8,128)(2,1)} copy(bf16[224,4096]{1,0:T(8,128)(2,1)} %copy-done.10) | data formatting | bytes 3670016 | tf_op jit(solution)/shard_map/optimization_barrier | solution.py:539
  42.4 0.0 collective-permute-start.6
  42.4 4.3 %collective-permute-done.5.refs_6_ = bf16[256,1792]{1,0:T(8,128)(2,1)} collective-permute-done((bf16[256,1792]{1,0:T(8,128)(2,1)}, bf16[256,1792]{1,0:T(8,128)(2,1)}, u32[]{:S(2)}, u32[]{:S(2)}) %collective-permute-start.5) | collective-permute-done | bytes 917536 | tf_op jit(solution)/shard_map/ppermute | solution.py:51
  46.7 1.0 all-to-all-done
  47.7 1.6 copy-done.2
  49.3 2.2 %shard_map.156 = bf16[8,128,512]{2,1,0:T(8,128)(2,1)S(1)} custom-call(s32[2]{0:T(128)S(1)} %pad_add_fusion.place_ref, bf16[128,4608]{1,0:T(8,128)(2,1)S(1)} %bitcast.62, bf16[4096,224]{1,0:T(8,128)(2,1)S(1)} %copy.30.own_ref, bf16[4096,224]{1,0:T(8,128)(2,1)S(1)} %bitcast.61, bf16[16,1,448]{2,1,0:T(2,128)(2,1)S(1)} %reshape.48.gain_ref), custom_call_target="tpu_custom_call" | custom-call | flops 469762048 | bytes 3670016 | tf_op jit(solution)/shard_map/pallas_call | solution.py:249
  51.5 1.1 copy-done.3
  52.6 3.6 %all-to-all-start.1 = ((bf16[8,128,512]{2,1,0:T(8,128)(2,1)}), bf16[8,128,512]{2,1,0:T(8,128)(2,1)S(1)}, u32[]{:S(2)}, u32[]{:S(2)}) async-start(bf16[8,128,512]{2,1,0:T(8,128)(2,1)} %copy-done.3), calls=%async_computation.1 | async-start | bytes 2097152 | tf_op jit(solution)/shard_map/all_to_all | solution.py:566
  56.1 1.2 collective-permute-done.6.refs_7_
  57.4 10.0 %all-to-all-done.1 = bf16[8,128,512]{2,1,0:T(8,128)(2,1)S(1)} async-done(((bf16[8,128,512]{2,1,0:T(8,128)(2,1)}), bf16[8,128,512]{2,1,0:T(8,128)(2,1)S(1)}, u32[]{:S(2)}, u32[]{:S(2)}) %all-to-all-start.1) | async-done | bytes 1048608 | tf_op jit(solution)/shard_map/all_to_all | solution.py:566
  67.3 1.6 collective-permute-start.7
  68.9 2.0 %collective-permute-start.8 = (bf16[1024,512]{1,0:T(8,128)(2,1)S(1)}, bf16[1024,512]{1,0:T(8,128)(2,1)S(1)}, u32[]{:S(2)}, u32[]{:S(2)}) collective-permute-start(bf16[1024,512]{1,0:T(8,128)(2,1)S(1)} %bitcast.64), channel_id=1, source_target_pairs={{0,96},{4,36},{8,104},{12,44},{16,112},{20,52},{24,120},{28,60},{3... | collective-permute-start | bytes 3145736 | tf_op jit(solution)/shard_map/ppermute | solution.py:51
  70.9 3.8 %collective-permute-start.9 = (bf16[1024,512]{1,0:T(8,128)(2,1)S(1)}, bf16[1024,512]{1,0:T(8,128)(2,1)S(1)}, u32[]{:S(2)}, u32[]{:S(2)}) collective-permute-start(bf16[1024,512]{1,0:T(8,128)(2,1)S(1)} %bitcast.65), channel_id=1, source_target_pairs={{0,3},{1,2},{2,1},{3,0},{4,5},{5,4},{6,7},{7,6},{8,11},{9,10},{10,... | collective-permute-start | bytes 3145736 | tf_op jit(solution)/shard_map/ppermute | solution.py:51
  74.6 0.8 collective-permute-start.10
  75.4 0.1 collective-permute-start.11
  75.5 0.1 stack.108.place_ref
  75.6 0.0 copy-start
  75.6 2.0 %copy-done = bf16[1,7168,256]{2,1,0:T(8,128)(2,1)S(1)} copy-done((bf16[1,7168,256]{2,1,0:T(8,128)(2,1)S(1)}, bf16[1,7168,256]{2,1,0:T(8,128)(2,1)}, u32[]{:S(2)}) %copy-start) | copy-done | bytes 3670040
  77.7 3.9 %shard_map.157 = (f32[2,256,1152]{2,1,0:T(8,128)S(1)}, f32[16,8,512]{2,1,0:T(8,128)S(1)}) custom-call(s32[25]{0:T(128)S(1)} %stack.108.place_ref, bf16[1024,512]{1,0:T(8,128)(2,1)S(1)} %bitcast.66, bf16[7168,256]{1,0:T(8,128)(2,1)S(1)} %bitcast.59, bf16[7168,256]{1,0:T(8,128)(2,1)} %collective-permute-done.1.refs_2_.refs_4_.refs_3_, ...), custom_call_target="tpu_custom_call" | custom-call | flops 1073741824 | bytes 4194304 | tf_op jit(solution)/shard_map/pallas_call | solution.py:402
  81.6 1.9 %collective-permute-done.7.refs_0_ = bf16[1024,512]{1,0:T(8,128)(2,1)} collective-permute-done((bf16[1024,512]{1,0:T(8,128)(2,1)S(1)}, bf16[1024,512]{1,0:T(8,128)(2,1)}, u32[]{:S(2)}, u32[]{:S(2)}) %collective-permute-start.7) | collective-permute-done | bytes 1048608 | tf_op jit(solution)/shard_map/ppermute | solution.py:51
  83.4 1.9 %collective-permute-start.12 = (bf16[1024,512]{1,0:T(8,128)(2,1)}, bf16[1024,512]{1,0:T(8,128)(2,1)S(1)}, u32[]{:S(2)}, u32[]{:S(2)}) collective-permute-start(bf16[1024,512]{1,0:T(8,128)(2,1)} %collective-permute-done.7.refs_0_), channel_id=1, source_target_pairs={{0,96},{4,36},{8,104},{12,44},{16,112},{20,52},{24,120},{28,60},{3... | collective-permute-start | bytes 3145736 | tf_op jit(solution)/shard_map/ppermute | solution.py:51
  85.3 5.4 %collective-permute-start.14 = (bf16[1024,512]{1,0:T(8,128)(2,1)S(1)}, bf16[1024,512]{1,0:T(8,128)(2,1)S(1)}, u32[]{:S(2)}, u32[]{:S(2)}) collective-permute-start(bf16[1024,512]{1,0:T(8,128)(2,1)S(1)} %collective-permute-done.8.refs_1_), channel_id=1, source_target_pairs={{0,3},{1,2},{2,1},{3,0},{4,5},{5,4},{6,7},{7,6},{8,11},{9,10},{10,... | collective-permute-start | bytes 3145736 | tf_op jit(solution)/shard_map/ppermute | solution.py:51
  90.7 0.0 collective-permute-start.15
  90.8 0.5 collective-permute-start.16
  91.3 1.3 collective-permute-start.18
  92.5 8.6 %shard_map.158 = (f32[2,256,1152]{2,1,0:T(8,128)S(1)}, f32[16,8,512]{2,1,0:T(8,128)S(1)}) custom-call(s32[25]{0:T(128)S(1)} %stack.108.place_ref, bf16[1024,512]{1,0:T(8,128)(2,1)} %collective-permute-done.7.refs_0_, bf16[1024,512]{1,0:T(8,128)(2,1)S(1)} %collective-permute-done.8.refs_1_, bf16[1024,512]{1,0:T(8,128)(2,1)S(1)} %collective-permute-done.9.refs_2_, ...), custom_call_target="tpu_custom_call" | custom-call | flops 3221225472 | bytes 12582912 | tf_op jit(solution)/shard_map/pallas_call | solution.py:402
  101.2 4.0 %collective-permute-start.13 = (bf16[512,512]{1,0:T(8,128)(2,1)S(1)}, bf16[512,512]{1,0:T(8,128)(2,1)S(1)}, u32[]{:S(2)}, u32[]{:S(2)}) collective-permute-start(bf16[512,512]{1,0:T(8,128)(2,1)S(1)} %slice.12), channel_id=1, source_target_pairs={{0,3},{1,2},{2,1},{3,0},{4,5},{5,4},{6,7},{7,6},{8,11},{9,10},{10,... | collective-permute-start | bytes 1572872 | tf_op jit(solution)/shard_map/ppermute | solution.py:51
  105.3 0.1 collective-permute-start.17
  105.4 1.9 %collective-permute-done.18.refs_2_ = bf16[1024,512]{1,0:T(8,128)(2,1)S(1)} collective-permute-done((bf16[1024,512]{1,0:T(8,128)(2,1)S(1)}, bf16[1024,512]{1,0:T(8,128)(2,1)S(1)}, u32[]{:S(2)}, u32[]{:S(2)}) %collective-permute-start.18) | collective-permute-done | bytes 1048608 | tf_op jit(solution)/shard_map/ppermute | solution.py:51
  107.3 7.4 %shard_map.159 = (f32[2,256,1152]{2,1,0:T(8,128)S(1)}, f32[16,8,512]{2,1,0:T(8,128)S(1)}) custom-call(s32[25]{0:T(128)S(1)} %stack.108.place_ref, bf16[1024,512]{1,0:T(8,128)(2,1)S(1)} %collective-permute-done.12.refs_0_, bf16[1024,512]{1,0:T(8,128)(2,1)S(1)} %collective-permute-done.14.refs_1_, bf16[1024,512]{1,0:T(8,128)(2,1)S(1)} %collective-permute-done.18.refs_2_, ...), custom_call_target="tpu_custom_call" | custom-call | flops 3221225472 | bytes 12582912 | tf_op jit(solution)/shard_map/pallas_call | solution.py:402
  114.7 1.1 collective-permute-done.17.refs_1_
  115.8 4.9 %shard_map.160 = (bf16[2,256,256]{2,1,0:T(8,128)(2,1)S(1)}, s32[512,2]{1,0:T(8,128)S(1)}, f32[16,8,512]{2,1,0:T(8,128)S(1)}) custom-call(s32[25]{0:T(128)S(1)} %stack.108.place_ref, bf16[512,512]{1,0:T(8,128)(2,1)S(1)} %collective-permute-done.13.refs_0_, bf16[512,512]{1,0:T(8,128)(2,1)S(1)} %collective-permute-done.17.refs_1_, ...), custom_call_target="tpu_custom_call" | custom-call | flops 1073741824 | bytes 4194304 | tf_op jit(solution)/shard_map/pallas_call | solution.py:402
  120.7 1.0 collective-permute-start.19
  121.6 0.7 collective-permute-start.20
  122.4 2.5 %collective-permute-start.21 = (bf16[2,256,256]{2,1,0:T(8,128)(2,1)S(1)}, bf16[2,256,256]{2,1,0:T(8,128)(2,1)S(1)}, u32[]{:S(2)}, u32[]{:S(2)}) collective-permute-start(bf16[2,256,256]{2,1,0:T(8,128)(2,1)S(1)} %get-tuple-element.74.refs_0_), channel_id=1, source_target_pairs={{0,2},{1,3},{2,0},{3,1},{4,6},{5,7},{6,4},{7,5},{8,10},{9,11},{10,... | collective-permute-start | bytes 786440 | tf_op jit(solution)/shard_map/ppermute | solution.py:34
  124.8 4.4 %collective-permute-done.19.refs_1_ = bf16[2,256,256]{2,1,0:T(8,128)(2,1)S(1)} collective-permute-done((bf16[2,256,256]{2,1,0:T(8,128)(2,1)S(1)}, bf16[2,256,256]{2,1,0:T(8,128)(2,1)S(1)}, u32[]{:S(2)}, u32[]{:S(2)}) %collective-permute-start.19) | collective-permute-done | bytes 262176 | tf_op jit(solution)/shard_map/ppermute | solution.py:51
  129.2 5.4 %collective-permute-done.20.refs_2_ = bf16[2,256,256]{2,1,0:T(8,128)(2,1)S(1)} collective-permute-done((bf16[2,256,256]{2,1,0:T(8,128)(2,1)S(1)}, bf16[2,256,256]{2,1,0:T(8,128)(2,1)S(1)}, u32[]{:S(2)}, u32[]{:S(2)}) %collective-permute-start.20) | collective-permute-done | bytes 262176 | tf_op jit(solution)/shard_map/ppermute | solution.py:51
  134.7 8.6 %shard_map.161 = bf16[512,1792]{1,0:T(8,128)(2,1)} custom-call(s32[25]{0:T(128)S(1)} %stack.108.place_ref, s32[512,2]{1,0:T(8,128)S(1)} %get-tuple-element.73.index_ref, bf16[2,256,256]{2,1,0:T(8,128)(2,1)S(1)} %get-tuple-element.74.refs_0_, bf16[2,256,256]{2,1,0:T(8,128)(2,1)S(1)} %collective-permute-done.19.refs_1_, ...), custom_call_target="tpu_custom_call" | custom-call | flops 3758096384 | bytes 7340032 | tf_op jit(solution)/shard_map/pallas_call | solution.py:453
  143.3 4.7 %all-to-all-start.2 = ((bf16[64,8,1792]{2,1,0:T(8,128)(2,1)}), bf16[64,8,1792]{2,1,0:T(8,128)(2,1)S(1)}, u32[]{:S(2)}, u32[]{:S(2)}) async-start(bf16[64,8,1792]{2,1,0:T(8,128)(2,1)} %bitcast.41), calls=%async_computation.2 | async-start | bytes 3670016 | tf_op jit(solution)/shard_map/all_to_all | solution.py:612
  148.1 0.2 copy.32
  148.2 0.1 reshape.43
  148.4 25.5 %all-to-all-done.2 = bf16[64,8,1792]{2,1,0:T(8,128)(2,1)S(1)} async-done(((bf16[64,8,1792]{2,1,0:T(8,128)(2,1)}), bf16[64,8,1792]{2,1,0:T(8,128)(2,1)S(1)}, u32[]{:S(2)}, u32[]{:S(2)}) %all-to-all-start.2) | async-done | bytes 1835040 | tf_op jit(solution)/shard_map/all_to_all | solution.py:612
  173.9 0.2 convert_reduce_fusion
  174.1 0.7 add_convert_fusion
  (35 shorter events, 0.2 us)
Async XLA Ops:
  0.0 19.9 %collective-permute-start.1 = (bf16[7168,256]{1,0:T(8,128)(2,1)}, bf16[7168,256]{1,0:T(8,128)(2,1)}, u32[]{:S(2)}, u32[]{:S(2)}) collective-permute-start(bf16[7168,256]{1,0:T(8,128)(2,1)} %bitcast.56), channel_id=1, source_target_pairs={{0,4},{4,0},{8,12},{12,8},{16,20},{20,16},{24,28},{28,24},{32,36},... | collective-permute-start | bytes 11010056 | tf_op jit(solution)/shard_map/ppermute | solution.py:29
  0.0 19.9 %collective-permute-start.2 = (bf16[7168,256]{1,0:T(8,128)(2,1)}, bf16[7168,256]{1,0:T(8,128)(2,1)}, u32[]{:S(2)}, u32[]{:S(2)}) collective-permute-start(bf16[7168,256]{1,0:T(8,128)(2,1)} %bitcast.69), channel_id=1, source_target_pairs={{0,4},{4,0},{8,12},{12,8},{16,20},{20,16},{24,28},{28,24},{32,36},... | collective-permute-start | bytes 11010056 | tf_op jit(solution)/shard_map/ppermute | solution.py:29
  0.5 19.3 %collective-permute-start = (bf16[224,4096]{1,0:T(8,128)(2,1)}, bf16[224,4096]{1,0:T(8,128)(2,1)S(1)}, u32[]{:S(2)}, u32[]{:S(2)}) collective-permute-start(bf16[224,4096]{1,0:T(8,128)(2,1)} %bitcast.74), channel_id=1, source_target_pairs={{0,4},{4,0},{8,12},{12,8},{16,20},{20,16},{24,28},{28,24},{32,36},... | collective-permute-start | bytes 5505032 | tf_op jit(solution)/shard_map/ppermute | solution.py:29
  3.0 16.8 %collective-permute-start.3 = (bf16[256,1792]{1,0:T(8,128)(2,1)S(1)}, bf16[256,1792]{1,0:T(8,128)(2,1)}, u32[]{:S(2)}, u32[]{:S(2)}) collective-permute-start(bf16[256,1792]{1,0:T(8,128)(2,1)S(1)} %get-tuple-element.43), channel_id=1, source_target_pairs={{0,1},{1,0},{2,3},{3,2},{4,7},{5,6},{6,5},{7,4},{8,9},{9,8},{10,11... | collective-permute-start | bytes 2752520 | tf_op jit(solution)/shard_map/ppermute | solution.py:51
  5.0 37.4 %collective-permute-start.4 = (bf16[256,1792]{1,0:T(8,128)(2,1)}, bf16[256,1792]{1,0:T(8,128)(2,1)}, u32[]{:S(2)}, u32[]{:S(2)}) collective-permute-start(bf16[256,1792]{1,0:T(8,128)(2,1)} %get-tuple-element.45), channel_id=1, source_target_pairs={{0,1},{1,0},{2,3},{3,2},{4,7},{5,6},{6,5},{7,4},{8,9},{9,8},{10,11... | collective-permute-start | bytes 2752520 | tf_op jit(solution)/shard_map/ppermute | solution.py:51
  5.1 10.0 %copy-start.9 = (bf16[32,512,128]{2,1,0:T(8,128)(2,1)S(1)}, bf16[32,512,128]{2,1,0:T(8,128)(2,1)}, u32[]{:S(2)}) copy-start(bf16[32,512,128]{2,1,0:T(8,128)(2,1)} %param.24) | copy-start | bytes 12582916
  19.8 1.2 copy-start.10
  21.1 26.7 %all-to-all-start = ((bf16[16,8,4608]{2,1,0:T(8,128)(2,1)}), bf16[16,8,4608]{2,1,0:T(8,128)(2,1)S(1)}, u32[]{:S(2)}, u32[]{:S(2)}) async-start(bf16[16,8,4608]{2,1,0:T(8,128)(2,1)} %shard_map.155), calls=%async_computation | async-start | bytes 2359296 | tf_op jit(solution)/shard_map/all_to_all | solution.py:547
  28.2 10.1 %copy-start.11 = (bf16[7168]{0:T(1024)(128)(2,1)S(1)}, bf16[7168]{0:T(1024)(128)(2,1)}, u32[]{:S(2)}) copy-start(bf16[7168]{0:T(1024)(128)(2,1)} %param.26) | copy-start | bytes 43012
  31.0 15.7 %collective-permute-start.5 = (bf16[256,1792]{1,0:T(8,128)(2,1)}, bf16[256,1792]{1,0:T(8,128)(2,1)}, u32[]{:S(2)}, u32[]{:S(2)}) collective-permute-start(bf16[256,1792]{1,0:T(8,128)(2,1)} %get-tuple-element.80), channel_id=1, source_target_pairs={{0,3},{1,2},{2,1},{3,0},{4,5},{5,4},{6,7},{7,6},{8,11},{9,10},{10,... | collective-permute-start | bytes 2752520 | tf_op jit(solution)/shard_map/ppermute | solution.py:51
  42.4 14.9 %collective-permute-start.6 = (bf16[256,1792]{1,0:T(8,128)(2,1)}, bf16[256,1792]{1,0:T(8,128)(2,1)}, u32[]{:S(2)}, u32[]{:S(2)}) collective-permute-start(bf16[256,1792]{1,0:T(8,128)(2,1)} %collective-permute-done.3), channel_id=1, source_target_pairs={{0,3},{1,2},{2,1},{3,0},{4,5},{5,4},{6,7},{7,6},{8,11},{9,10},{10,... | collective-permute-start | bytes 2752520 | tf_op jit(solution)/shard_map/ppermute | solution.py:51
  47.7 1.6 copy-start.2
  51.5 1.1 copy-start.3
  52.6 14.7 %all-to-all-start.1 = ((bf16[8,128,512]{2,1,0:T(8,128)(2,1)}), bf16[8,128,512]{2,1,0:T(8,128)(2,1)S(1)}, u32[]{:S(2)}, u32[]{:S(2)}) async-start(bf16[8,128,512]{2,1,0:T(8,128)(2,1)} %copy-done.3), calls=%async_computation.1 | async-start | bytes 2097152 | tf_op jit(solution)/shard_map/all_to_all | solution.py:566
  67.3 16.1 %collective-permute-start.7 = (bf16[1024,512]{1,0:T(8,128)(2,1)S(1)}, bf16[1024,512]{1,0:T(8,128)(2,1)}, u32[]{:S(2)}, u32[]{:S(2)}) collective-permute-start(bf16[1024,512]{1,0:T(8,128)(2,1)S(1)} %bitcast.63), channel_id=1, source_target_pairs={{0,24},{4,12},{8,16},{12,4},{16,8},{20,28},{24,0},{28,20},{32,56},... | collective-permute-start | bytes 3145736 | tf_op jit(solution)/shard_map/ppermute | solution.py:51
  68.9 16.4 %collective-permute-start.8 = (bf16[1024,512]{1,0:T(8,128)(2,1)S(1)}, bf16[1024,512]{1,0:T(8,128)(2,1)S(1)}, u32[]{:S(2)}, u32[]{:S(2)}) collective-permute-start(bf16[1024,512]{1,0:T(8,128)(2,1)S(1)} %bitcast.64), channel_id=1, source_target_pairs={{0,96},{4,36},{8,104},{12,44},{16,112},{20,52},{24,120},{28,60},{3... | collective-permute-start | bytes 3145736 | tf_op jit(solution)/shard_map/ppermute | solution.py:51
  70.9 20.4 %collective-permute-start.9 = (bf16[1024,512]{1,0:T(8,128)(2,1)S(1)}, bf16[1024,512]{1,0:T(8,128)(2,1)S(1)}, u32[]{:S(2)}, u32[]{:S(2)}) collective-permute-start(bf16[1024,512]{1,0:T(8,128)(2,1)S(1)} %bitcast.65), channel_id=1, source_target_pairs={{0,3},{1,2},{2,1},{3,0},{4,5},{5,4},{6,7},{7,6},{8,11},{9,10},{10,... | collective-permute-start | bytes 3145736 | tf_op jit(solution)/shard_map/ppermute | solution.py:51
  74.6 16.1 %collective-permute-start.10 = (bf16[256,1792]{1,0:T(8,128)(2,1)}, bf16[256,1792]{1,0:T(8,128)(2,1)}, u32[]{:S(2)}, u32[]{:S(2)}) collective-permute-start(bf16[256,1792]{1,0:T(8,128)(2,1)} %get-tuple-element.79), channel_id=1, source_target_pairs={{0,4},{4,0},{8,12},{12,8},{16,20},{20,16},{24,28},{28,24},{32,36},... | collective-permute-start | bytes 2752520 | tf_op jit(solution)/shard_map/ppermute | solution.py:29
  75.4 15.3 %collective-permute-start.11 = (bf16[256,1792]{1,0:T(8,128)(2,1)}, bf16[256,1792]{1,0:T(8,128)(2,1)}, u32[]{:S(2)}, u32[]{:S(2)}) collective-permute-start(bf16[256,1792]{1,0:T(8,128)(2,1)} %collective-permute-done.4.refs_5_), channel_id=1, source_target_pairs={{0,4},{4,0},{8,12},{12,8},{16,20},{20,16},{24,28},{28,24},{32,36},... | collective-permute-start | bytes 2752520 | tf_op jit(solution)/shard_map/ppermute | solution.py:29
  75.6 2.0 %copy-start = (bf16[1,7168,256]{2,1,0:T(8,128)(2,1)S(1)}, bf16[1,7168,256]{2,1,0:T(8,128)(2,1)}, u32[]{:S(2)}) copy-start(bf16[1,7168,256]{2,1,0:T(8,128)(2,1)} %param.29) | copy-start | bytes 11010052
  83.4 17.7 %collective-permute-start.12 = (bf16[1024,512]{1,0:T(8,128)(2,1)}, bf16[1024,512]{1,0:T(8,128)(2,1)S(1)}, u32[]{:S(2)}, u32[]{:S(2)}) collective-permute-start(bf16[1024,512]{1,0:T(8,128)(2,1)} %collective-permute-done.7.refs_0_), channel_id=1, source_target_pairs={{0,96},{4,36},{8,104},{12,44},{16,112},{20,52},{24,120},{28,60},{3... | collective-permute-start | bytes 3145736 | tf_op jit(solution)/shard_map/ppermute | solution.py:51
  85.3 19.9 %collective-permute-start.14 = (bf16[1024,512]{1,0:T(8,128)(2,1)S(1)}, bf16[1024,512]{1,0:T(8,128)(2,1)S(1)}, u32[]{:S(2)}, u32[]{:S(2)}) collective-permute-start(bf16[1024,512]{1,0:T(8,128)(2,1)S(1)} %collective-permute-done.8.refs_1_), channel_id=1, source_target_pairs={{0,3},{1,2},{2,1},{3,0},{4,5},{5,4},{6,7},{7,6},{8,11},{9,10},{10,... | collective-permute-start | bytes 3145736 | tf_op jit(solution)/shard_map/ppermute | solution.py:51
  90.7 14.5 %collective-permute-start.15 = (bf16[256,1792]{1,0:T(8,128)(2,1)}, bf16[256,1792]{1,0:T(8,128)(2,1)S(1)}, u32[]{:S(2)}, u32[]{:S(2)}) collective-permute-start(bf16[256,1792]{1,0:T(8,128)(2,1)} %collective-permute-done.5.refs_6_), channel_id=1, source_target_pairs={{0,4},{4,0},{8,12},{12,8},{16,20},{20,16},{24,28},{28,24},{32,36},... | collective-permute-start | bytes 2752520 | tf_op jit(solution)/shard_map/ppermute | solution.py:29
  90.8 14.5 %collective-permute-start.16 = (bf16[256,1792]{1,0:T(8,128)(2,1)}, bf16[256,1792]{1,0:T(8,128)(2,1)S(1)}, u32[]{:S(2)}, u32[]{:S(2)}) collective-permute-start(bf16[256,1792]{1,0:T(8,128)(2,1)} %collective-permute-done.6.refs_7_), channel_id=1, source_target_pairs={{0,4},{4,0},{8,12},{12,8},{16,20},{20,16},{24,28},{28,24},{32,36},... | collective-permute-start | bytes 2752520 | tf_op jit(solution)/shard_map/ppermute | solution.py:29
  91.3 16.0 %collective-permute-start.18 = (bf16[1024,512]{1,0:T(8,128)(2,1)S(1)}, bf16[1024,512]{1,0:T(8,128)(2,1)S(1)}, u32[]{:S(2)}, u32[]{:S(2)}) collective-permute-start(bf16[1024,512]{1,0:T(8,128)(2,1)S(1)} %collective-permute-done.9.refs_2_), channel_id=1, source_target_pairs={{0,24},{4,12},{8,16},{12,4},{16,8},{20,28},{24,0},{28,20},{32,56},... | collective-permute-start | bytes 3145736 | tf_op jit(solution)/shard_map/ppermute | solution.py:51
  101.2 13.5 %collective-permute-start.13 = (bf16[512,512]{1,0:T(8,128)(2,1)S(1)}, bf16[512,512]{1,0:T(8,128)(2,1)S(1)}, u32[]{:S(2)}, u32[]{:S(2)}) collective-permute-start(bf16[512,512]{1,0:T(8,128)(2,1)S(1)} %slice.12), channel_id=1, source_target_pairs={{0,3},{1,2},{2,1},{3,0},{4,5},{5,4},{6,7},{7,6},{8,11},{9,10},{10,... | collective-permute-start | bytes 1572872 | tf_op jit(solution)/shard_map/ppermute | solution.py:51
  105.3 9.4 %copy-start.5 = (bf16[256,1792]{1,0:T(8,128)(2,1)}, bf16[256,1792]{1,0:T(8,128)(2,1)S(1)}, u32[]{:S(2)}) copy-start(bf16[256,1792]{1,0:T(8,128)(2,1)S(1)} %collective-permute-done.15.refs_10_) | copy-start | bytes 2752516
  105.3 9.4 %copy-start.7 = (bf16[256,1792]{1,0:T(8,128)(2,1)}, bf16[256,1792]{1,0:T(8,128)(2,1)S(1)}, u32[]{:S(2)}) copy-start(bf16[256,1792]{1,0:T(8,128)(2,1)S(1)} %collective-permute-done.16.refs_11_) | copy-start | bytes 2752516
  105.3 10.5 %collective-permute-start.17 = (bf16[512,512]{1,0:T(8,128)(2,1)S(1)}, bf16[512,512]{1,0:T(8,128)(2,1)S(1)}, u32[]{:S(2)}, u32[]{:S(2)}) collective-permute-start(bf16[512,512]{1,0:T(8,128)(2,1)S(1)} %slice.13), channel_id=1, source_target_pairs={{0,24},{4,12},{8,16},{12,4},{16,8},{20,28},{24,0},{28,20},{32,56},... | collective-permute-start | bytes 1572872 | tf_op jit(solution)/shard_map/ppermute | solution.py:51
  107.3 8.5 %copy-start.1 = (bf16[1,7168,256]{2,1,0:T(8,128)(2,1)S(1)}, bf16[1,7168,256]{2,1,0:T(8,128)(2,1)}, u32[]{:S(2)}) copy-start(bf16[1,7168,256]{2,1,0:T(8,128)(2,1)} %param.29) | copy-start | bytes 11010052
  115.8 18.9 %copy-start.4 = (bf16[1,256,7168]{2,1,0:T(8,128)(2,1)S(1)}, bf16[1,256,7168]{2,1,0:T(8,128)(2,1)}, u32[]{:S(2)}) copy-start(bf16[1,256,7168]{2,1,0:T(8,128)(2,1)} %param.31) | copy-start | bytes 11010052
  115.8 18.9 %copy-start.6 = (bf16[256,1792]{1,0:T(8,128)(2,1)S(1)}, bf16[256,1792]{1,0:T(8,128)(2,1)}, u32[]{:S(2)}) copy-start(bf16[256,1792]{1,0:T(8,128)(2,1)} %copy-done.5) | copy-start | bytes 2752516
  115.8 18.9 %copy-start.8 = (bf16[256,1792]{1,0:T(8,128)(2,1)S(1)}, bf16[256,1792]{1,0:T(8,128)(2,1)}, u32[]{:S(2)}) copy-start(bf16[256,1792]{1,0:T(8,128)(2,1)} %copy-done.7) | copy-start | bytes 2752516
  120.7 8.6 %collective-permute-start.19 = (bf16[2,256,256]{2,1,0:T(8,128)(2,1)S(1)}, bf16[2,256,256]{2,1,0:T(8,128)(2,1)S(1)}, u32[]{:S(2)}, u32[]{:S(2)}) collective-permute-start(bf16[2,256,256]{2,1,0:T(8,128)(2,1)S(1)} %get-tuple-element.74.refs_0_), channel_id=1, source_target_pairs={{0,1},{1,0},{2,3},{3,2},{4,7},{5,6},{6,5},{7,4},{8,9},{9,8},{10,11... | collective-permute-start | bytes 786440 | tf_op jit(solution)/shard_map/ppermute | solution.py:51
  121.6 13.0 %collective-permute-start.20 = (bf16[2,256,256]{2,1,0:T(8,128)(2,1)S(1)}, bf16[2,256,256]{2,1,0:T(8,128)(2,1)S(1)}, u32[]{:S(2)}, u32[]{:S(2)}) collective-permute-start(bf16[2,256,256]{2,1,0:T(8,128)(2,1)S(1)} %get-tuple-element.74.refs_0_), channel_id=1, source_target_pairs={{0,3},{1,2},{2,1},{3,0},{4,5},{5,4},{6,7},{7,6},{8,11},{9,10},{10,... | collective-permute-start | bytes 786440 | tf_op jit(solution)/shard_map/ppermute | solution.py:51
  122.4 12.3 %collective-permute-start.21 = (bf16[2,256,256]{2,1,0:T(8,128)(2,1)S(1)}, bf16[2,256,256]{2,1,0:T(8,128)(2,1)S(1)}, u32[]{:S(2)}, u32[]{:S(2)}) collective-permute-start(bf16[2,256,256]{2,1,0:T(8,128)(2,1)S(1)} %get-tuple-element.74.refs_0_), channel_id=1, source_target_pairs={{0,2},{1,3},{2,0},{3,1},{4,6},{5,7},{6,4},{7,5},{8,10},{9,11},{10,... | collective-permute-start | bytes 786440 | tf_op jit(solution)/shard_map/ppermute | solution.py:34
  143.3 30.6 %all-to-all-start.2 = ((bf16[64,8,1792]{2,1,0:T(8,128)(2,1)}), bf16[64,8,1792]{2,1,0:T(8,128)(2,1)S(1)}, u32[]{:S(2)}, u32[]{:S(2)}) async-start(bf16[64,8,1792]{2,1,0:T(8,128)(2,1)} %bitcast.41), calls=%async_computation.2 | async-start | bytes 3670016 | tf_op jit(solution)/shard_map/all_to_all | solution.py:612

commit v4 on v3

--- a/solution.py
+++ b/solution.py
@@ -268,16 +268,20 @@
     )(place, landed, own, other, gain.reshape(CHIPS, 1, 2 * cols))
 
 
-def gather_kernel(place_ref, *refs, units, first, final, model):
+def gather_kernel(place_ref, *refs, units, first, done, model):
     counts = [len(rows) for rows, _, _ in units]
     blocks, refs = refs[: sum(counts)], refs[sum(counts) :]
     sources, refs = refs[:4], refs[4:]
-    if not first:
-        (total_in, own_in), refs = refs[:2], refs[2:]
+    final = done == 1
     if final:
-        hidden_ref, index_ref, own_ref, total, tokens, weight, arrived = refs
+        total_in, sums_in, hidden_ref, index_ref, total, tokens, weight, arrived = refs
     else:
-        total, own_ref, tokens, weight, arrived = refs
+        if not first:
+            (total_in, own_in), refs = refs[:2], refs[2:]
+        total, own_ref, refs = refs[0], refs[1], refs[2:]
+        if done == 0:
+            (sums_ref, index_ref), refs = refs[:2], refs[2:]
+        tokens, weight, arrived = refs
     part = sources[0].shape[1]
     cols = model // CHIPS
     wide = blocks[0].shape[1]
@@ -306,6 +310,8 @@
     if first:
         total[...] = jnp.zeros_like(total)
         own_ref[...] = jnp.zeros_like(own_ref)
+    elif final:
+        total[1] = total_in[1]
     else:
         total[...] = total_in[...]
         own_ref[...] = own_in[...]
@@ -344,43 +350,41 @@
         total[far_z, :, :width] += jnp.dot(
             tokens[...], weight[unit], preferred_element_type=F32
         )
-    if not final:
+    if done is None:
         return
 
     group = lax.broadcasted_iota(jnp.int32, (128, 1), 0) // 8
-    half = total.shape[1]
     slots = 4 * 4 * CHIPS
     lanes = lax.broadcasted_iota(jnp.int32, (1, slots), 1)
     even = place_ref[21] == 0
-    sums = [None, None]
-    for far_z in range(2):
-        extra = total[far_z, :, width:]
-        square = (extra[:, 6:7] + extra[:, 7:8]) * (1.0 / model)
-        inverse = lax.rsqrt(square + EPSILON)
-        names = extra[:, spare:]
-        bases = jnp.concatenate(
-            [group * 4 + place_ref[16 + far_z * 2 + i] * (4 * CHIPS) for i in range(2)], axis=0
+    extra = total[done, :, width:]
+    square = (extra[:, 6:7] + extra[:, 7:8]) * (1.0 / model)
+    inverse = lax.rsqrt(square + EPSILON)
+    names = extra[:, spare:]
+    bases = jnp.concatenate(
+        [group * 4 + place_ref[16 + done * 2 + i] * (4 * CHIPS) for i in range(2)], axis=0
+    )
+    gates = [names[:, i : i + 1] + names[:, 2 + i : 3 + i] for i in range(2)]
+    ranks = [names[:, 4 + i : 5 + i].astype(jnp.int32) for i in range(2)]
+    for i in range(2):
+        gate = total[done, :, i * part : (i + 1) * part] * inverse
+        up = total[done, :, (2 + i) * part : (3 + i) * part] * inverse
+        share = jnp.where(even, gates[i], gates[1 - i])
+        rank = jnp.where(even, ranks[i], ranks[1 - i])
+        value = gate * (1.0 / (1.0 + jnp.exp(-gate))) * up * share
+        place_index = jnp.where(rank < 4, bases + rank, -1)
+        index_ref[:, i : i + 1] = place_index
+        hot = (place_index == lanes).astype(BF16)
+        term = lax.dot_general(
+            hot, value.astype(BF16), (((0,), (0,)), ((), ())), preferred_element_type=F32
         )
-        gates = [names[:, i : i + 1] + names[:, 2 + i : 3 + i] for i in range(2)]
-        ranks = [names[:, 4 + i : 5 + i].astype(jnp.int32) for i in range(2)]
-        for i in range(2):
-            gate = total[far_z, :, i * part : (i + 1) * part] * inverse
-            up = total[far_z, :, (2 + i) * part : (3 + i) * part] * inverse
-            share = jnp.where(even, gates[i], gates[1 - i])
-            rank = jnp.where(even, ranks[i], ranks[1 - i])
-            value = gate * (1.0 / (1.0 + jnp.exp(-gate))) * up * share
-            place_index = jnp.where(rank < 4, bases + rank, -1)
-            index_ref[far_z * half : (far_z + 1) * half, i : i + 1] = place_index
-            hot = (place_index == lanes).astype(BF16)
-            term = lax.dot_general(
-                hot, value.astype(BF16), (((0,), (0,)), ((), ())), preferred_element_type=F32
-            )
-            sums[i] = term if sums[i] is None else sums[i] + term
-    for i in range(2):
-        hidden_ref[i] = sums[i].astype(BF16)
-
-
-def gather_products(place, units, blocks, weights, carried, final):
+        if final:
+            hidden_ref[i] = (sums_in[i] + term).astype(BF16)
+        else:
+            sums_ref[i] = term
+
+
+def gather_products(place, units, blocks, weights, carried, done=None):
     model, part = weights[0].shape
     wide = blocks[0].shape[1]
     width = 4 * part
@@ -394,21 +398,27 @@
         pltpu.VMEM((len(units), 4 * wide, width), BF16),
         pltpu.SemaphoreType.DMA((len(units), 4, 4)),
     ]
-    if final:
-        outs = [((2, tok // 2, part), BF16), ((tok, 2), jnp.int32), (own_shape, F32)]
+    sums_shape = (2, tok // 2, part)
+    index_out = ((tok // 2, 2), jnp.int32)
+    carried_shapes = (total_shape, own_shape)
+    if done == 1:
+        outs = [(sums_shape, BF16), index_out]
         scratch = [pltpu.VMEM(total_shape, F32)] + scratch
+        carried_shapes = (total_shape, sums_shape)
     else:
         outs = [(total_shape, F32), (own_shape, F32)]
+        if done == 0:
+            outs += [(sums_shape, F32), index_out]
     return pl.pallas_call(
         functools.partial(
-            gather_kernel, units=units, first=carried is None, final=final, model=model
+            gather_kernel, units=units, first=carried is None, done=done, model=model
         ),
         grid_spec=pltpu.PrefetchScalarGridSpec(
             num_scalar_prefetch=1,
             grid=(1,),
             in_specs=[whole(*b.shape) for b in blocks]
             + [pl.BlockSpec(memory_space=pltpu.HBM)] * 4
-            + ([] if carried is None else [whole(*total_shape), whole(*own_shape)]),
+            + ([] if carried is None else [whole(*shape) for shape in carried_shapes]),
             out_specs=[whole(*shape) for shape, _ in outs],
             scratch_shapes=scratch,
         ),
@@ -422,52 +432,70 @@
     )(place, *blocks, *weights, *(() if carried is None else carried))
 
 
-def down_kernel(place_ref, index_ref, *refs):
-    hidden, weights, (out_ref, spread) = refs[:4], refs[4:12], refs[12:]
-    slots, part = hidden[0].shape[1:]
-
-    @pl.when(pl.program_id(0) == 0)
-    def _():
-        lanes = lax.broadcasted_iota(jnp.int32, (1, slots), 1)
-        for i in range(2):
-            hot = (index_ref[:, i : i + 1] == lanes).astype(BF16)
-            for k, ref in enumerate(hidden):
-                at = (i * 4 + (k if i == 0 else (0, 2, 1, 3)[k])) * part
-                spread[:, at : at + part] = jnp.dot(
-                    hot, ref[i], preferred_element_type=F32
-                ).astype(BF16)
-
-    weight = jnp.concatenate([ref[...] for ref in weights], axis=0)
-    total = jnp.dot(spread[...], weight, preferred_element_type=F32).astype(BF16)
+def down_kernel(place_ref, low_ref, high_ref, *refs):
+    hidden, own, other = refs[:4], refs[4:8], refs[8:12]
+    out_ref, values, weight, sums, arrived = refs[12:]
+    slots = values.shape[1]
+    width = weight.shape[2]
+    part = weight.shape[1] // 4
+    start = pl.multiple_of(place_ref[22] * width, 128)
+
+    def fetch(i):
+        copies = []
+        for k in range(4):
+            source = other[(0, 2, 1, 3)[k]]
+            if i == 0:
+                source = own[k].at[:, pl.ds(start, width)] if k == 0 else own[k]
+            rows = pl.ds(k * part, part)
+            copies.append((source, weight.at[i, rows], arrived.at[i, 0, k]))
+            copies.append((hidden[k].at[i], values.at[i, :, rows], arrived.at[i, 1, k]))
+        return [pltpu.make_async_copy(*copy) for copy in copies]
+
+    for i in range(2):
+        for copy in fetch(i):
+            copy.start()
+    lanes = lax.broadcasted_iota(jnp.int32, (1, slots), 1)
+    index = jnp.concatenate([low_ref[...], high_ref[...]], axis=0)
+    hots = [(index[:, i : i + 1] == lanes).astype(BF16) for i in range(2)]
+    for i in range(2):
+        for copy in fetch(i):
+            copy.wait()
+        sums[i * slots : (i + 1) * slots] = jnp.dot(
+            values[i], weight[i], preferred_element_type=F32
+        ).astype(BF16)
+    result = jnp.dot(
+        jnp.concatenate(hots, axis=1), sums[...], preferred_element_type=F32
+    ).astype(BF16)
     for i in range(4):
-        start = pl.multiple_of(place_ref[16 + i] * 128, 128)
-        out_ref[pl.ds(start, 128), :] = total[i * 128 : (i + 1) * 128]
-
-
-def down(place, index, hidden, own, other):
-    tok = index.shape[0]
+        at = pl.multiple_of(place_ref[16 + i] * 128, 128)
+        out_ref[pl.ds(at, 128), :] = result[i * 128 : (i + 1) * 128]
+
+
+def down(place, index_low, index_high, hidden, own, other):
+    half = index_low.shape[0]
     slots, part = hidden[0].shape[1:]
     width = own[1].shape[1]
-    tile = width // 2
-    h_spec = pl.BlockSpec((2, slots, part), lambda i, s: (0, 0, 0))
+    whole = lambda *shape: pl.BlockSpec(shape, lambda i, s: (0,) * len(shape))
     return pl.pallas_call(
         down_kernel,
         grid_spec=pltpu.PrefetchScalarGridSpec(
             num_scalar_prefetch=1,
-            grid=(width // tile,),
-            in_specs=[pl.BlockSpec((tok, 2), lambda i, s: (0, 0))]
-            + [h_spec] * 4
-            + [pl.BlockSpec((part, tile), lambda i, s: (0, s[22] * 2 + i))]
-            + [pl.BlockSpec((part, tile), lambda i, s: (0, i))] * 7,
-            out_specs=pl.BlockSpec((tok, tile), lambda i, s: (0, i)),
-            scratch_shapes=[pltpu.VMEM((tok, 8 * part), BF16)],
-        ),
-        out_shape=jax.ShapeDtypeStruct((tok, width), BF16),
+            grid=(1,),
+            in_specs=[whole(half, 2)] * 2 + [pl.BlockSpec(memory_space=pl.ANY)] * 12,
+            out_specs=whole(2 * half, width),
+            scratch_shapes=[
+                pltpu.VMEM((2, slots, 4 * part), BF16),
+                pltpu.VMEM((2, 4 * part, width), BF16),
+                pltpu.VMEM((2 * slots, width), BF16),
+                pltpu.SemaphoreType.DMA((2, 2, 4)),
+            ],
+        ),
+        out_shape=jax.ShapeDtypeStruct((2 * half, width), BF16),
         cost_estimate=pl.CostEstimate(
-            flops=16 * tok * part * width, bytes_accessed=16 * part * width, transcendentals=0
-        ),
-        compiler_params=pltpu.CompilerParams(vmem_limit_bytes=28 << 20),
-    )(place, index, *hidden, *own, *other)
+            flops=24 * half * part * width, bytes_accessed=16 * part * width, transcendentals=0
+        ),
+        compiler_params=pltpu.CompilerParams(vmem_limit_bytes=32 << 20),
+    )(place, index_low, index_high, *hidden, *own, *other)
 
 
 def per_device(
@@ -571,7 +599,7 @@
     weights = (gate_own, gate_other, up_own, up_other)
     all_rows = ((0, 1024),)
     by_x, by_y, by_z = exchange(block, "x", 1), exchange(block, "y", 1), exchange(block, "z", 1)
-    carried = gather_products(place, ((all_rows, 0, 0),), (block,), weights, None, False)
+    carried = gather_products(place, ((all_rows, 0, 0),), (block,), weights, None)
     own, on_x = lax.optimization_barrier((carried[1], by_x))
     own, on_y = lax.optimization_barrier((own, by_y))
     own, on_z, *others[:2] = lax.optimization_barrier((own, by_z, *others[:2]))
@@ -583,7 +611,6 @@
         (by_x, by_y, by_z),
         weights,
         carried,
-        False,
     )
     cuts = [value[low:high] for value, (low, high) in zip((by_xy, by_yz), HALVES)]
     own, cuts[0] = lax.optimization_barrier((carried[1], cuts[0]))
@@ -592,19 +619,19 @@
     )
     carried = (carried[0], own)
     halves = [exchange(value, axis, 1) for value, axis in zip(cuts, "zx")]
-    carried = gather_products(
+    total, own, part_sums, index_low = gather_products(
         place,
         ((all_rows, 3, 0), (all_rows, 2, 1), (all_rows, 1, 1)),
         (by_xy, by_yz, by_xz),
         weights,
         carried,
-        False,
-    )
-    hidden, index, own = gather_products(
-        place, ((HALVES, 3, 1),), tuple(halves), weights, carried, True
+        0,
+    )
+    hidden, index_high = gather_products(
+        place, ((HALVES, 3, 1),), tuple(halves), weights, (total, part_sums), 1
     )
     spread = [hidden, exchange(hidden, "z", 0), exchange(hidden, "z", 1), shift_z(hidden, 2)]
-    sums = down(place, index, spread, (w_down[0], near, far, last), others)
+    sums = down(place, index_low, index_high, spread, (w_down[0], near, far, last), others)
     lane_all = [
         [expert_of(y, x, core) * SIDE + z for z in range(SIDE) for y in range(SIDE) for x in range(SIDE)]
         for core in range(2)

time: 176 us -> 174 us (0.989)
  Pallas kernels: 47.8 us -> 46 us
    ppermute x14, waiting for transfers between devices: 20.2 us -> 17.3 us  [exchange(): return lax.ppermute(value, BOTH if axis == 'z' else 'expert', pairs)]
    ppermute x1, waiting for transfers between devices: 0.01 us -> 1.84 us  [shift_z(): return lax.ppermute(value, 'tensor', pairs)]
    unnamed x25 -> x17, local copies, waits for them, and re-layouts: 9.13 us -> 9.13 us
where the time goes in v4:
time: 174 us; the launch traced here: 173 us
  waiting for transfers between devices  55.2 us (32%)
  starting transfers between devices  49.2 us (28%)
  Pallas kernels  46 us (26%)
  local copies, waits for them, and re-layouts  19.7 us (11%)
    ppermute x14, starting transfers between devices, exchange(): return lax.ppermute(value, BOTH if axis == 'z' else 'expert', pairs)  29.4 us
    all_to_all x1, waiting for transfers between devices, per_device(): lax.all_to_all(sums.reshape(SIDE * CHIPS, rows, quarter), BOTH, split_axi...  25 us
    pallas_call x4, Pallas kernels, gather_products(): pl.pallas_call(functools.partial(gather_kernel, units=units, first=carrie...  24.2 us
    ppermute x14, waiting for transfers between devices, exchange(): return lax.ppermute(value, BOTH if axis == 'z' else 'expert', pairs)  17.3 us
    all_to_all x1, waiting for transfers between devices, per_device(): lax.all_to_all(block, BOTH, split_axis=0, concat_axis=0, tiled=True, axis...  10 us
    pallas_call x1, Pallas kernels, attention_heads(): pl.pallas_call(functools.partial(attend_kernel, scale=scale, heads=heads)...  9.98 us
    unnamed x17, local copies, waits for them, and re-layouts  9.13 us
    pallas_call x1, Pallas kernels, down(): pl.pallas_call(down_kernel, grid_spec=pltpu.PrefetchScalarGridSpec(num_sc...  7.24 us
  transfers between devices with their start and end apart: 25, of which 10 were waited for; matrix products, arithmetic and copies ran while one was open for 9% of the time, Pallas kernels for 20%

profile of v4, /device:TPU:0, one launch (start us, length us, event | category | flops | bytes accessed | tf_op | source)
XLA Modules:
  0.0 173.2 jit_solution(9917985018836956245)
XLA Ops:
  0.0 0.0 collective-permute-start.1
  0.0 0.5 collective-permute-start.2
  0.5 2.5 %dynamic-slice_bitcast_fusion = (bf16[256,1792]{1,0:T(8,128)(2,1)}, bf16[256,1792]{1,0:T(8,128)(2,1)S(1)}) fusion(bf16[1,256,7168]{2,1,0:T(8,128)(2,1)} %param.31, s32[]{:T(128)S(6)} %select_n.52, s32[]{:T(128)S(6)} %select_n.51), kind=kLoop, calls=%fused_computation.4 | loop fusion | bytes 3670024 | tf_op jit(solution)/shard_map/dynamic_slice | solution.py:546
  3.0 2.0 %collective-permute-start.3 = (bf16[256,1792]{1,0:T(8,128)(2,1)S(1)}, bf16[256,1792]{1,0:T(8,128)(2,1)}, u32[]{:S(2)}, u32[]{:S(2)}) collective-permute-start(bf16[256,1792]{1,0:T(8,128)(2,1)S(1)} %get-tuple-element.44), channel_id=1, source_target_pairs={{0,1},{1,0},{2,3},{3,2},{4,7},{5,6},{6,5},{7,4},{8,9},{9,8},{10,11... | collective-permute-start | bytes 2752520 | tf_op jit(solution)/shard_map/ppermute | solution.py:51
  5.0 0.0 collective-permute-start.4
  5.1 10.0 %shard_map.154 = bf16[4,64,512]{2,1,0:T(8,128)(2,1)} custom-call(s32[4]{0:T(128)} %length_ref, bf16[4,64,512]{2,1,0:T(8,128)(2,1)} %bitcast.77, bf16[4,64,64]{2,1,0:T(8,128)(2,1)} %bitcast.79, bf16[4,2048,512]{2,1,0:T(8,128)(2,1)} %latent_ref.1, bf16[4,64,2048]{2,1,0:T(8,128)(2,1)} %rope_ref.1, bf16[4,2,512]{2,1,0:T(2,128)(2,1)} %fresh_ref.1, ...), custom_call_target="tpu_custom_call" | custom-call | flops 1140850688 | bytes 9437184 | tf_op jit(solution)/shard_map/pallas_call | solution.py:99
  15.1 1.7 fusion.2
  16.8 0.7 copy.28
  17.4 2.4 %shard_map.155 = bf16[16,8,4608]{2,1,0:T(8,128)(2,1)} custom-call(bf16[32,8,128]{2,1,0:T(8,128)(2,1)} %bitcast.78, bf16[8,7168]{1,0:T(8,128)(2,1)} %residual_ref.1, s32[8,8]{1,0:T(8,128)} %ids_ref.1, f32[8,8]{1,0:T(8,128)} %gates_ref.1), custom_call_target="tpu_custom_call" | custom-call | bytes 1179648 | tf_op jit(solution)/shard_map/pallas_call | solution.py:190
  19.8 0.0 collective-permute-done.3
  19.9 0.0 collective-permute-done.1.refs_2_.refs_4_.refs_3_
  19.9 0.0 collective-permute-done.2.refs_4_.refs_6_.refs_5_
  19.9 1.2 copy-done.6
  21.1 7.1 %all-to-all-start = ((bf16[16,8,4608]{2,1,0:T(8,128)(2,1)}), bf16[16,8,4608]{2,1,0:T(8,128)(2,1)S(1)}, u32[]{:S(2)}, u32[]{:S(2)}) async-start(bf16[16,8,4608]{2,1,0:T(8,128)(2,1)} %shard_map.155), calls=%async_computation | async-start | bytes 2359296 | tf_op jit(solution)/shard_map/all_to_all | solution.py:575
  28.2 0.0 copy-start.7
  28.2 2.8 %constant_dynamic-slice_fusion = (bf16[256,1792]{1,0:T(8,128)(2,1)}, bf16[256,1792]{1,0:T(8,128)(2,1)}) fusion(bf16[256,7168]{1,0:T(8,128)(2,1)} %bitcast.61, s32[]{:T(128)S(6)} %select_n.54, s32[]{:T(128)S(6)} %select_n.53), kind=kLoop, calls=%fused_computation.9 | loop fusion | bytes 3670024 | tf_op jit(solution)/shard_map/dynamic_slice | solution.py:546
  31.1 4.0 %collective-permute-start.5 = (bf16[256,1792]{1,0:T(8,128)(2,1)}, bf16[256,1792]{1,0:T(8,128)(2,1)}, u32[]{:S(2)}, u32[]{:S(2)}) collective-permute-start(bf16[256,1792]{1,0:T(8,128)(2,1)} %get-tuple-element.82), channel_id=1, source_target_pairs={{0,3},{1,2},{2,1},{3,0},{4,5},{5,4},{6,7},{7,6},{8,11},{9,10},{10,... | collective-permute-start | bytes 2752520 | tf_op jit(solution)/shard_map/ppermute | solution.py:51
  35.1 3.2 %copy.30.own_ref = bf16[4096,224]{1,0:T(8,128)(2,1)S(1)} copy(bf16[4096,224]{0,1:T(8,128)(2,1)} %param.25) | data formatting | bytes 3670016 | tf_op args[9]
  38.3 0.1 reshape.48.gain_ref
  38.4 0.1 pad_add_fusion.place_ref
  38.5 4.0 %copy.29 = bf16[224,4096]{0,1:T(8,128)(2,1)} copy(bf16[224,4096]{1,0:T(8,128)(2,1)} %copy-done.6) | data formatting | bytes 3670016 | tf_op jit(solution)/shard_map/optimization_barrier | solution.py:567
  42.4 0.0 collective-permute-start.6
  42.4 4.3 %collective-permute-done.5.refs_6_ = bf16[256,1792]{1,0:T(8,128)(2,1)} collective-permute-done((bf16[256,1792]{1,0:T(8,128)(2,1)}, bf16[256,1792]{1,0:T(8,128)(2,1)}, u32[]{:S(2)}, u32[]{:S(2)}) %collective-permute-start.5) | collective-permute-done | bytes 917536 | tf_op jit(solution)/shard_map/ppermute | solution.py:51
  46.8 1.0 all-to-all-done
  47.8 1.6 copy-done.3
  49.4 2.2 %shard_map.156 = bf16[8,128,512]{2,1,0:T(8,128)(2,1)S(1)} custom-call(s32[2]{0:T(128)S(1)} %pad_add_fusion.place_ref, bf16[128,4608]{1,0:T(8,128)(2,1)S(1)} %bitcast.64, bf16[4096,224]{1,0:T(8,128)(2,1)S(1)} %copy.30.own_ref, bf16[4096,224]{1,0:T(8,128)(2,1)S(1)} %bitcast.63, bf16[16,1,448]{2,1,0:T(2,128)(2,1)S(1)} %reshape.48.gain_ref), custom_call_target="tpu_custom_call" | custom-call | flops 469762048 | bytes 3670016 | tf_op jit(solution)/shard_map/pallas_call | solution.py:249
  51.6 1.1 copy-done.4
  52.7 3.6 %all-to-all-start.1 = ((bf16[8,128,512]{2,1,0:T(8,128)(2,1)}), bf16[8,128,512]{2,1,0:T(8,128)(2,1)S(1)}, u32[]{:S(2)}, u32[]{:S(2)}) async-start(bf16[8,128,512]{2,1,0:T(8,128)(2,1)} %copy-done.4), calls=%async_computation.1 | async-start | bytes 2097152 | tf_op jit(solution)/shard_map/all_to_all | solution.py:594
  56.2 1.1 collective-permute-done.6.refs_7_
  57.4 10.0 %all-to-all-done.1 = bf16[8,128,512]{2,1,0:T(8,128)(2,1)S(1)} async-done(((bf16[8,128,512]{2,1,0:T(8,128)(2,1)}), bf16[8,128,512]{2,1,0:T(8,128)(2,1)S(1)}, u32[]{:S(2)}, u32[]{:S(2)}) %all-to-all-start.1) | async-done | bytes 1048608 | tf_op jit(solution)/shard_map/all_to_all | solution.py:594
  67.4 1.5 collective-permute-start.7
  68.9 2.0 %collective-permute-start.9 = (bf16[1024,512]{1,0:T(8,128)(2,1)S(1)}, bf16[1024,512]{1,0:T(8,128)(2,1)S(1)}, u32[]{:S(2)}, u32[]{:S(2)}) collective-permute-start(bf16[1024,512]{1,0:T(8,128)(2,1)S(1)} %bitcast.66), channel_id=1, source_target_pairs={{0,96},{4,36},{8,104},{12,44},{16,112},{20,52},{24,120},{28,60},{3... | collective-permute-start | bytes 3145736 | tf_op jit(solution)/shard_map/ppermute | solution.py:51
  70.9 3.7 %collective-permute-start.11 = (bf16[1024,512]{1,0:T(8,128)(2,1)S(1)}, bf16[1024,512]{1,0:T(8,128)(2,1)S(1)}, u32[]{:S(2)}, u32[]{:S(2)}) collective-permute-start(bf16[1024,512]{1,0:T(8,128)(2,1)S(1)} %bitcast.67), channel_id=1, source_target_pairs={{0,3},{1,2},{2,1},{3,0},{4,5},{5,4},{6,7},{7,6},{8,11},{9,10},{10,... | collective-permute-start | bytes 3145736 | tf_op jit(solution)/shard_map/ppermute | solution.py:51
  74.6 0.8 collective-permute-start.12
  75.4 0.1 collective-permute-start.13
  75.5 0.1 stack.108.place_ref
  75.6 0.0 copy-start
  75.6 2.0 %copy-done = bf16[1,7168,256]{2,1,0:T(8,128)(2,1)S(1)} copy-done((bf16[1,7168,256]{2,1,0:T(8,128)(2,1)S(1)}, bf16[1,7168,256]{2,1,0:T(8,128)(2,1)}, u32[]{:S(2)}) %copy-start) | copy-done | bytes 3670040
  77.7 3.9 %shard_map.157 = (f32[2,256,1152]{2,1,0:T(8,128)S(1)}, f32[16,8,512]{2,1,0:T(8,128)S(1)}) custom-call(s32[25]{0:T(128)S(1)} %stack.108.place_ref, bf16[1024,512]{1,0:T(8,128)(2,1)S(1)} %bitcast.68, bf16[7168,256]{1,0:T(8,128)(2,1)S(1)} %bitcast.59, bf16[7168,256]{1,0:T(8,128)(2,1)} %collective-permute-done.1.refs_2_.refs_4_.refs_3_, ...), custom_call_target="tpu_custom_call" | custom-call | flops 1073741824 | bytes 4194304 | tf_op jit(solution)/shard_map/pallas_call | solution.py:412
  81.5 2.0 %collective-permute-done.7.refs_0_ = bf16[1024,512]{1,0:T(8,128)(2,1)} collective-permute-done((bf16[1024,512]{1,0:T(8,128)(2,1)S(1)}, bf16[1024,512]{1,0:T(8,128)(2,1)}, u32[]{:S(2)}, u32[]{:S(2)}) %collective-permute-start.7) | collective-permute-done | bytes 1048608 | tf_op jit(solution)/shard_map/ppermute | solution.py:51
  83.5 1.8 %collective-permute-start.8 = (bf16[1024,512]{1,0:T(8,128)(2,1)}, bf16[1024,512]{1,0:T(8,128)(2,1)S(1)}, u32[]{:S(2)}, u32[]{:S(2)}) collective-permute-start(bf16[1024,512]{1,0:T(8,128)(2,1)} %collective-permute-done.7.refs_0_), channel_id=1, source_target_pairs={{0,96},{4,36},{8,104},{12,44},{16,112},{20,52},{24,120},{28,60},{3... | collective-permute-start | bytes 3145736 | tf_op jit(solution)/shard_map/ppermute | solution.py:51
  85.3 5.4 %collective-permute-start.10 = (bf16[1024,512]{1,0:T(8,128)(2,1)S(1)}, bf16[1024,512]{1,0:T(8,128)(2,1)S(1)}, u32[]{:S(2)}, u32[]{:S(2)}) collective-permute-start(bf16[1024,512]{1,0:T(8,128)(2,1)S(1)} %collective-permute-done.9.refs_1_), channel_id=1, source_target_pairs={{0,3},{1,2},{2,1},{3,0},{4,5},{5,4},{6,7},{7,6},{8,11},{9,10},{10,... | collective-permute-start | bytes 3145736 | tf_op jit(solution)/shard_map/ppermute | solution.py:51
  90.7 0.5 collective-permute-start.16
  91.3 1.3 collective-permute-start.14
  92.5 8.6 %shard_map.158 = (f32[2,256,1152]{2,1,0:T(8,128)S(1)}, f32[16,8,512]{2,1,0:T(8,128)S(1)}) custom-call(s32[25]{0:T(128)S(1)} %stack.108.place_ref, bf16[1024,512]{1,0:T(8,128)(2,1)} %collective-permute-done.7.refs_0_, bf16[1024,512]{1,0:T(8,128)(2,1)S(1)} %collective-permute-done.9.refs_1_, bf16[1024,512]{1,0:T(8,128)(2,1)S(1)} %collective-permute-done.11.refs_2_, ...), custom_call_target="tpu_custom_call" | custom-call | flops 3221225472 | bytes 12582912 | tf_op jit(solution)/shard_map/pallas_call | solution.py:412
  101.2 2.3 %collective-permute-done.10.refs_1_ = bf16[1024,512]{1,0:T(8,128)(2,1)S(1)} collective-permute-done((bf16[1024,512]{1,0:T(8,128)(2,1)S(1)}, bf16[1024,512]{1,0:T(8,128)(2,1)S(1)}, u32[]{:S(2)}, u32[]{:S(2)}) %collective-permute-start.10) | collective-permute-done | bytes 1048608 | tf_op jit(solution)/shard_map/ppermute | solution.py:51
  103.6 1.4 collective-permute-start.18
  104.9 3.2 %collective-permute-start.17 = (bf16[512,512]{1,0:T(8,128)(2,1)S(1)}, bf16[512,512]{1,0:T(8,128)(2,1)S(1)}, u32[]{:S(2)}, u32[]{:S(2)}) collective-permute-start(bf16[512,512]{1,0:T(8,128)(2,1)S(1)} %slice.12), channel_id=1, source_target_pairs={{0,3},{1,2},{2,1},{3,0},{4,5},{5,4},{6,7},{7,6},{8,11},{9,10},{10,... | collective-permute-start | bytes 1572872 | tf_op jit(solution)/shard_map/ppermute | solution.py:51
  108.2 7.4 %shard_map.159 = (f32[2,256,1152]{2,1,0:T(8,128)S(1)}, f32[16,8,512]{2,1,0:T(8,128)S(1)}, f32[2,256,256]{2,1,0:T(8,128)S(1)}, s32[256,2]{1,0:T(8,128)S(1)}) custom-call(s32[25]{0:T(128)S(1)} %stack.108.place_ref, bf16[1024,512]{1,0:T(8,128)(2,1)S(1)} %collective-permute-done.8.refs_0_, bf16[1024,512]{1,0:T(8,128)(2,1)S(1)} %collective-permute-done.10.refs_1_, ...), custom_call_target="tpu_custom_call" | custom-call | flops 3221225472 | bytes 12582912 | tf_op jit(solution)/shard_map/pallas_call | solution.py:412
  115.6 0.0 copy-start.2
  115.7 4.3 %shard_map.160 = (bf16[2,256,256]{2,1,0:T(8,128)(2,1)S(1)}, s32[256,2]{1,0:T(8,128)S(1)}) custom-call(s32[25]{0:T(128)S(1)} %stack.108.place_ref, bf16[512,512]{1,0:T(8,128)(2,1)S(1)} %collective-permute-done.17.refs_0_, bf16[512,512]{1,0:T(8,128)(2,1)S(1)} %collective-permute-done.18.refs_1_, bf16[7168,256]{1,0:T(8,128)(2,1)S(1)} %bitcast.60, ...), custom_call_target="tpu_custom_call" | custom-call | flops 1073741824 | bytes 4194304 | tf_op jit(solution)/shard_map/pallas_call | solution.py:412
  120.0 0.1 collective-permute-start.19
  120.1 3.0 %collective-permute-start.20 = (bf16[2,256,256]{2,1,0:T(8,128)(2,1)S(1)}, bf16[2,256,256]{2,1,0:T(8,128)(2,1)S(1)}, u32[]{:S(2)}, u32[]{:S(2)}) collective-permute-start(bf16[2,256,256]{2,1,0:T(8,128)(2,1)S(1)} %get-tuple-element.76.refs_0_), channel_id=1, source_target_pairs={{0,3},{1,2},{2,1},{3,0},{4,5},{5,4},{6,7},{7,6},{8,11},{9,10},{10,... | collective-permute-start | bytes 786440 | tf_op jit(solution)/shard_map/ppermute | solution.py:51
  123.0 1.4 collective-permute-start.21
  124.4 4.9 %collective-permute-done.19.refs_1_ = bf16[2,256,256]{2,1,0:T(8,128)(2,1)S(1)} collective-permute-done((bf16[2,256,256]{2,1,0:T(8,128)(2,1)S(1)}, bf16[2,256,256]{2,1,0:T(8,128)(2,1)S(1)}, u32[]{:S(2)}, u32[]{:S(2)}) %collective-permute-start.19) | collective-permute-done | bytes 262176 | tf_op jit(solution)/shard_map/ppermute | solution.py:51
  129.3 2.6 %collective-permute-done.20.refs_2_ = bf16[2,256,256]{2,1,0:T(8,128)(2,1)S(1)} collective-permute-done((bf16[2,256,256]{2,1,0:T(8,128)(2,1)S(1)}, bf16[2,256,256]{2,1,0:T(8,128)(2,1)S(1)}, u32[]{:S(2)}, u32[]{:S(2)}) %collective-permute-start.20) | collective-permute-done | bytes 262176 | tf_op jit(solution)/shard_map/ppermute | solution.py:51
  131.9 1.8 %collective-permute-done.21.refs_3_ = bf16[2,256,256]{2,1,0:T(8,128)(2,1)S(1)} collective-permute-done((bf16[2,256,256]{2,1,0:T(8,128)(2,1)S(1)}, bf16[2,256,256]{2,1,0:T(8,128)(2,1)S(1)}, u32[]{:S(2)}, u32[]{:S(2)}) %collective-permute-start.21) | collective-permute-done | bytes 262176 | tf_op jit(solution)/shard_map/ppermute | solution.py:34
  133.8 7.2 %shard_map.161 = bf16[512,1792]{1,0:T(8,128)(2,1)} custom-call(s32[25]{0:T(128)S(1)} %stack.108.place_ref, s32[256,2]{1,0:T(8,128)S(1)} %get-tuple-element.70.low_ref, s32[256,2]{1,0:T(8,128)S(1)} %get-tuple-element.75.high_ref, bf16[2,256,256]{2,1,0:T(8,128)(2,1)S(1)} %get-tuple-element.76.refs_0_, ...), custom_call_target="tpu_custom_call" | custom-call | flops 2818572288 | bytes 7340032 | tf_op jit(solution)/shard_map/pallas_call | solution.py:479
  141.0 5.9 %all-to-all-start.2 = ((bf16[64,8,1792]{2,1,0:T(8,128)(2,1)}), bf16[64,8,1792]{2,1,0:T(8,128)(2,1)S(1)}, u32[]{:S(2)}, u32[]{:S(2)}) async-start(bf16[64,8,1792]{2,1,0:T(8,128)(2,1)} %bitcast.41), calls=%async_computation.2 | async-start | bytes 3670016 | tf_op jit(solution)/shard_map/all_to_all | solution.py:639
  146.9 0.2 copy.32
  147.1 0.1 reshape.43
  147.2 25.0 %all-to-all-done.2 = bf16[64,8,1792]{2,1,0:T(8,128)(2,1)S(1)} async-done(((bf16[64,8,1792]{2,1,0:T(8,128)(2,1)}), bf16[64,8,1792]{2,1,0:T(8,128)(2,1)S(1)}, u32[]{:S(2)}, u32[]{:S(2)}) %all-to-all-start.2) | async-done | bytes 1835040 | tf_op jit(solution)/shard_map/all_to_all | solution.py:639
  172.2 0.2 convert_reduce_fusion
  172.5 0.7 add_convert_fusion
  (27 shorter events, 0.1 us)
Async XLA Ops:
  0.0 19.9 %collective-permute-start.1 = (bf16[7168,256]{1,0:T(8,128)(2,1)}, bf16[7168,256]{1,0:T(8,128)(2,1)}, u32[]{:S(2)}, u32[]{:S(2)}) collective-permute-start(bf16[7168,256]{1,0:T(8,128)(2,1)} %bitcast.56), channel_id=1, source_target_pairs={{0,4},{4,0},{8,12},{12,8},{16,20},{20,16},{24,28},{28,24},{32,36},... | collective-permute-start | bytes 11010056 | tf_op jit(solution)/shard_map/ppermute | solution.py:29
  0.0 19.9 %collective-permute-start.2 = (bf16[7168,256]{1,0:T(8,128)(2,1)}, bf16[7168,256]{1,0:T(8,128)(2,1)}, u32[]{:S(2)}, u32[]{:S(2)}) collective-permute-start(bf16[7168,256]{1,0:T(8,128)(2,1)} %bitcast.69), channel_id=1, source_target_pairs={{0,4},{4,0},{8,12},{12,8},{16,20},{20,16},{24,28},{28,24},{32,36},... | collective-permute-start | bytes 11010056 | tf_op jit(solution)/shard_map/ppermute | solution.py:29
  0.5 19.3 %collective-permute-start = (bf16[224,4096]{1,0:T(8,128)(2,1)}, bf16[224,4096]{1,0:T(8,128)(2,1)S(1)}, u32[]{:S(2)}, u32[]{:S(2)}) collective-permute-start(bf16[224,4096]{1,0:T(8,128)(2,1)} %bitcast.74), channel_id=1, source_target_pairs={{0,4},{4,0},{8,12},{12,8},{16,20},{20,16},{24,28},{28,24},{32,36},... | collective-permute-start | bytes 5505032 | tf_op jit(solution)/shard_map/ppermute | solution.py:29
  3.0 16.8 %collective-permute-start.3 = (bf16[256,1792]{1,0:T(8,128)(2,1)S(1)}, bf16[256,1792]{1,0:T(8,128)(2,1)}, u32[]{:S(2)}, u32[]{:S(2)}) collective-permute-start(bf16[256,1792]{1,0:T(8,128)(2,1)S(1)} %get-tuple-element.44), channel_id=1, source_target_pairs={{0,1},{1,0},{2,3},{3,2},{4,7},{5,6},{6,5},{7,4},{8,9},{9,8},{10,11... | collective-permute-start | bytes 2752520 | tf_op jit(solution)/shard_map/ppermute | solution.py:51
  5.0 37.4 %collective-permute-start.4 = (bf16[256,1792]{1,0:T(8,128)(2,1)}, bf16[256,1792]{1,0:T(8,128)(2,1)}, u32[]{:S(2)}, u32[]{:S(2)}) collective-permute-start(bf16[256,1792]{1,0:T(8,128)(2,1)} %get-tuple-element.46), channel_id=1, source_target_pairs={{0,1},{1,0},{2,3},{3,2},{4,7},{5,6},{6,5},{7,4},{8,9},{9,8},{10,11... | collective-permute-start | bytes 2752520 | tf_op jit(solution)/shard_map/ppermute | solution.py:51
  5.1 10.0 %copy-start.5 = (bf16[32,512,128]{2,1,0:T(8,128)(2,1)S(1)}, bf16[32,512,128]{2,1,0:T(8,128)(2,1)}, u32[]{:S(2)}) copy-start(bf16[32,512,128]{2,1,0:T(8,128)(2,1)} %param.24) | copy-start | bytes 12582916
  19.9 1.2 copy-start.6
  21.1 26.7 %all-to-all-start = ((bf16[16,8,4608]{2,1,0:T(8,128)(2,1)}), bf16[16,8,4608]{2,1,0:T(8,128)(2,1)S(1)}, u32[]{:S(2)}, u32[]{:S(2)}) async-start(bf16[16,8,4608]{2,1,0:T(8,128)(2,1)} %shard_map.155), calls=%async_computation | async-start | bytes 2359296 | tf_op jit(solution)/shard_map/all_to_all | solution.py:575
  28.2 10.1 %copy-start.7 = (bf16[7168]{0:T(1024)(128)(2,1)S(1)}, bf16[7168]{0:T(1024)(128)(2,1)}, u32[]{:S(2)}) copy-start(bf16[7168]{0:T(1024)(128)(2,1)} %param.26) | copy-start | bytes 43012
  31.1 15.7 %collective-permute-start.5 = (bf16[256,1792]{1,0:T(8,128)(2,1)}, bf16[256,1792]{1,0:T(8,128)(2,1)}, u32[]{:S(2)}, u32[]{:S(2)}) collective-permute-start(bf16[256,1792]{1,0:T(8,128)(2,1)} %get-tuple-element.82), channel_id=1, source_target_pairs={{0,3},{1,2},{2,1},{3,0},{4,5},{5,4},{6,7},{7,6},{8,11},{9,10},{10,... | collective-permute-start | bytes 2752520 | tf_op jit(solution)/shard_map/ppermute | solution.py:51
  42.4 14.9 %collective-permute-start.6 = (bf16[256,1792]{1,0:T(8,128)(2,1)}, bf16[256,1792]{1,0:T(8,128)(2,1)}, u32[]{:S(2)}, u32[]{:S(2)}) collective-permute-start(bf16[256,1792]{1,0:T(8,128)(2,1)} %collective-permute-done.3), channel_id=1, source_target_pairs={{0,3},{1,2},{2,1},{3,0},{4,5},{5,4},{6,7},{7,6},{8,11},{9,10},{10,... | collective-permute-start | bytes 2752520 | tf_op jit(solution)/shard_map/ppermute | solution.py:51
  47.8 1.6 copy-start.3
  51.6 1.1 copy-start.4
  52.7 14.7 %all-to-all-start.1 = ((bf16[8,128,512]{2,1,0:T(8,128)(2,1)}), bf16[8,128,512]{2,1,0:T(8,128)(2,1)S(1)}, u32[]{:S(2)}, u32[]{:S(2)}) async-start(bf16[8,128,512]{2,1,0:T(8,128)(2,1)} %copy-done.4), calls=%async_computation.1 | async-start | bytes 2097152 | tf_op jit(solution)/shard_map/all_to_all | solution.py:594
  67.4 16.1 %collective-permute-start.7 = (bf16[1024,512]{1,0:T(8,128)(2,1)S(1)}, bf16[1024,512]{1,0:T(8,128)(2,1)}, u32[]{:S(2)}, u32[]{:S(2)}) collective-permute-start(bf16[1024,512]{1,0:T(8,128)(2,1)S(1)} %bitcast.65), channel_id=1, source_target_pairs={{0,24},{4,12},{8,16},{12,4},{16,8},{20,28},{24,0},{28,20},{32,56},... | collective-permute-start | bytes 3145736 | tf_op jit(solution)/shard_map/ppermute | solution.py:51
  68.9 16.4 %collective-permute-start.9 = (bf16[1024,512]{1,0:T(8,128)(2,1)S(1)}, bf16[1024,512]{1,0:T(8,128)(2,1)S(1)}, u32[]{:S(2)}, u32[]{:S(2)}) collective-permute-start(bf16[1024,512]{1,0:T(8,128)(2,1)S(1)} %bitcast.66), channel_id=1, source_target_pairs={{0,96},{4,36},{8,104},{12,44},{16,112},{20,52},{24,120},{28,60},{3... | collective-permute-start | bytes 3145736 | tf_op jit(solution)/shard_map/ppermute | solution.py:51
  70.9 20.4 %collective-permute-start.11 = (bf16[1024,512]{1,0:T(8,128)(2,1)S(1)}, bf16[1024,512]{1,0:T(8,128)(2,1)S(1)}, u32[]{:S(2)}, u32[]{:S(2)}) collective-permute-start(bf16[1024,512]{1,0:T(8,128)(2,1)S(1)} %bitcast.67), channel_id=1, source_target_pairs={{0,3},{1,2},{2,1},{3,0},{4,5},{5,4},{6,7},{7,6},{8,11},{9,10},{10,... | collective-permute-start | bytes 3145736 | tf_op jit(solution)/shard_map/ppermute | solution.py:51
  74.6 16.1 %collective-permute-start.12 = (bf16[256,1792]{1,0:T(8,128)(2,1)}, bf16[256,1792]{1,0:T(8,128)(2,1)}, u32[]{:S(2)}, u32[]{:S(2)}) collective-permute-start(bf16[256,1792]{1,0:T(8,128)(2,1)} %get-tuple-element.81), channel_id=1, source_target_pairs={{0,4},{4,0},{8,12},{12,8},{16,20},{20,16},{24,28},{28,24},{32,36},... | collective-permute-start | bytes 2752520 | tf_op jit(solution)/shard_map/ppermute | solution.py:29
  75.4 15.3 %collective-permute-start.13 = (bf16[256,1792]{1,0:T(8,128)(2,1)}, bf16[256,1792]{1,0:T(8,128)(2,1)}, u32[]{:S(2)}, u32[]{:S(2)}) collective-permute-start(bf16[256,1792]{1,0:T(8,128)(2,1)} %collective-permute-done.4.refs_5_), channel_id=1, source_target_pairs={{0,4},{4,0},{8,12},{12,8},{16,20},{20,16},{24,28},{28,24},{32,36},... | collective-permute-start | bytes 2752520 | tf_op jit(solution)/shard_map/ppermute | solution.py:29
  75.6 2.0 %copy-start = (bf16[1,7168,256]{2,1,0:T(8,128)(2,1)S(1)}, bf16[1,7168,256]{2,1,0:T(8,128)(2,1)}, u32[]{:S(2)}) copy-start(bf16[1,7168,256]{2,1,0:T(8,128)(2,1)} %param.29) | copy-start | bytes 11010052
  83.5 17.6 %collective-permute-start.8 = (bf16[1024,512]{1,0:T(8,128)(2,1)}, bf16[1024,512]{1,0:T(8,128)(2,1)S(1)}, u32[]{:S(2)}, u32[]{:S(2)}) collective-permute-start(bf16[1024,512]{1,0:T(8,128)(2,1)} %collective-permute-done.7.refs_0_), channel_id=1, source_target_pairs={{0,96},{4,36},{8,104},{12,44},{16,112},{20,52},{24,120},{28,60},{3... | collective-permute-start | bytes 3145736 | tf_op jit(solution)/shard_map/ppermute | solution.py:51
  85.3 18.2 %collective-permute-start.10 = (bf16[1024,512]{1,0:T(8,128)(2,1)S(1)}, bf16[1024,512]{1,0:T(8,128)(2,1)S(1)}, u32[]{:S(2)}, u32[]{:S(2)}) collective-permute-start(bf16[1024,512]{1,0:T(8,128)(2,1)S(1)} %collective-permute-done.9.refs_1_), channel_id=1, source_target_pairs={{0,3},{1,2},{2,1},{3,0},{4,5},{5,4},{6,7},{7,6},{8,11},{9,10},{10,... | collective-permute-start | bytes 3145736 | tf_op jit(solution)/shard_map/ppermute | solution.py:51
  90.7 12.8 %collective-permute-start.15 = (bf16[256,1792]{1,0:T(8,128)(2,1)}, bf16[256,1792]{1,0:T(8,128)(2,1)S(1)}, u32[]{:S(2)}, u32[]{:S(2)}) collective-permute-start(bf16[256,1792]{1,0:T(8,128)(2,1)} %collective-permute-done.5.refs_6_), channel_id=1, source_target_pairs={{0,4},{4,0},{8,12},{12,8},{16,20},{20,16},{24,28},{28,24},{32,36},... | collective-permute-start | bytes 2752520 | tf_op jit(solution)/shard_map/ppermute | solution.py:29
  90.7 12.8 %collective-permute-start.16 = (bf16[256,1792]{1,0:T(8,128)(2,1)}, bf16[256,1792]{1,0:T(8,128)(2,1)S(1)}, u32[]{:S(2)}, u32[]{:S(2)}) collective-permute-start(bf16[256,1792]{1,0:T(8,128)(2,1)} %collective-permute-done.6.refs_7_), channel_id=1, source_target_pairs={{0,4},{4,0},{8,12},{12,8},{16,20},{20,16},{24,28},{28,24},{32,36},... | collective-permute-start | bytes 2752520 | tf_op jit(solution)/shard_map/ppermute | solution.py:29
  91.3 16.9 %collective-permute-start.14 = (bf16[1024,512]{1,0:T(8,128)(2,1)S(1)}, bf16[1024,512]{1,0:T(8,128)(2,1)S(1)}, u32[]{:S(2)}, u32[]{:S(2)}) collective-permute-start(bf16[1024,512]{1,0:T(8,128)(2,1)S(1)} %collective-permute-done.11.refs_2_), channel_id=1, source_target_pairs={{0,24},{4,12},{8,16},{12,4},{16,8},{20,28},{24,0},{28,20},{32,56},... | collective-permute-start | bytes 3145736 | tf_op jit(solution)/shard_map/ppermute | solution.py:51
  103.6 12.1 %collective-permute-start.18 = (bf16[512,512]{1,0:T(8,128)(2,1)S(1)}, bf16[512,512]{1,0:T(8,128)(2,1)S(1)}, u32[]{:S(2)}, u32[]{:S(2)}) collective-permute-start(bf16[512,512]{1,0:T(8,128)(2,1)S(1)} %slice.13), channel_id=1, source_target_pairs={{0,24},{4,12},{8,16},{12,4},{16,8},{20,28},{24,0},{28,20},{32,56},... | collective-permute-start | bytes 1572872 | tf_op jit(solution)/shard_map/ppermute | solution.py:51
  104.9 10.7 %collective-permute-start.17 = (bf16[512,512]{1,0:T(8,128)(2,1)S(1)}, bf16[512,512]{1,0:T(8,128)(2,1)S(1)}, u32[]{:S(2)}, u32[]{:S(2)}) collective-permute-start(bf16[512,512]{1,0:T(8,128)(2,1)S(1)} %slice.12), channel_id=1, source_target_pairs={{0,3},{1,2},{2,1},{3,0},{4,5},{5,4},{6,7},{7,6},{8,11},{9,10},{10,... | collective-permute-start | bytes 1572872 | tf_op jit(solution)/shard_map/ppermute | solution.py:51
  108.2 7.5 %copy-start.1 = (bf16[1,7168,256]{2,1,0:T(8,128)(2,1)S(1)}, bf16[1,7168,256]{2,1,0:T(8,128)(2,1)}, u32[]{:S(2)}) copy-start(bf16[1,7168,256]{2,1,0:T(8,128)(2,1)} %param.29) | copy-start | bytes 11010052
  115.6 18.1 %copy-start.2 = (bf16[1,256,7168]{2,1,0:T(8,128)(2,1)S(1)}, bf16[1,256,7168]{2,1,0:T(8,128)(2,1)}, u32[]{:S(2)}) copy-start(bf16[1,256,7168]{2,1,0:T(8,128)(2,1)} %param.31) | copy-start | bytes 11010052
  120.0 9.3 %collective-permute-start.19 = (bf16[2,256,256]{2,1,0:T(8,128)(2,1)S(1)}, bf16[2,256,256]{2,1,0:T(8,128)(2,1)S(1)}, u32[]{:S(2)}, u32[]{:S(2)}) collective-permute-start(bf16[2,256,256]{2,1,0:T(8,128)(2,1)S(1)} %get-tuple-element.76.refs_0_), channel_id=1, source_target_pairs={{0,1},{1,0},{2,3},{3,2},{4,7},{5,6},{6,5},{7,4},{8,9},{9,8},{10,11... | collective-permute-start | bytes 786440 | tf_op jit(solution)/shard_map/ppermute | solution.py:51
  120.1 11.8 %collective-permute-start.20 = (bf16[2,256,256]{2,1,0:T(8,128)(2,1)S(1)}, bf16[2,256,256]{2,1,0:T(8,128)(2,1)S(1)}, u32[]{:S(2)}, u32[]{:S(2)}) collective-permute-start(bf16[2,256,256]{2,1,0:T(8,128)(2,1)S(1)} %get-tuple-element.76.refs_0_), channel_id=1, source_target_pairs={{0,3},{1,2},{2,1},{3,0},{4,5},{5,4},{6,7},{7,6},{8,11},{9,10},{10,... | collective-permute-start | bytes 786440 | tf_op jit(solution)/shard_map/ppermute | solution.py:51
  123.0 10.7 %collective-permute-start.21 = (bf16[2,256,256]{2,1,0:T(8,128)(2,1)S(1)}, bf16[2,256,256]{2,1,0:T(8,128)(2,1)S(1)}, u32[]{:S(2)}, u32[]{:S(2)}) collective-permute-start(bf16[2,256,256]{2,1,0:T(8,128)(2,1)S(1)} %get-tuple-element.76.refs_0_), channel_id=1, source_target_pairs={{0,2},{1,3},{2,0},{3,1},{4,6},{5,7},{6,4},{7,5},{8,10},{9,11},{10,... | collective-permute-start | bytes 786440 | tf_op jit(solution)/shard_map/ppermute | solution.py:34
  141.0 31.2 %all-to-all-start.2 = ((bf16[64,8,1792]{2,1,0:T(8,128)(2,1)}), bf16[64,8,1792]{2,1,0:T(8,128)(2,1)S(1)}, u32[]{:S(2)}, u32[]{:S(2)}) async-start(bf16[64,8,1792]{2,1,0:T(8,128)(2,1)} %bitcast.41), calls=%async_computation.2 | async-start | bytes 3670016 | tf_op jit(solution)/shard_map/all_to_all | solution.py:639

commit v5 on v4

--- a/solution.py
+++ b/solution.py
@@ -136,20 +136,11 @@
     return head_values.astype(BF16).reshape(heads, requests * steps, -1)
 
 
-def pack_kernel(
-    heads_ref, residual_ref, ids_ref, gates_ref, out_ref, values, tail, done
-):
+def pack_kernel(heads_ref, residual_ref, ids_ref, gates_ref, out_ref):
     heads, rows, each = heads_ref.shape
     width = heads * each
     cols = residual_ref.shape[1] // CHIPS
-    for head in range(heads):
-        values[:, head * each : (head + 1) * each] = heads_ref[head]
-    copies = [
-        pltpu.make_async_copy(values, out_ref.at[chip, :, pl.ds(0, width)], done.at[chip])
-        for chip in range(CHIPS)
-    ]
-    for copy in copies:
-        copy.start()
+    values = jnp.concatenate([heads_ref[head] for head in range(heads)], axis=1)
     lane = lax.broadcasted_iota(jnp.int32, (rows, 128), 1)
     gates = jnp.zeros((rows, 128), F32)
     named = jnp.zeros((rows, 128), F32)
@@ -175,13 +166,8 @@
         )
         picked = jnp.where(lane < 6, picked, 0.0)[:, : 512 - cols]
         part = residual_ref[:, chip * cols : (chip + 1) * cols]
-        tail[chip] = jnp.concatenate([part, picked.astype(BF16)], axis=1)
-    last = pltpu.make_async_copy(
-        tail, out_ref.at[:, :, pl.ds(width, tail.shape[2])], done.at[CHIPS]
-    )
-    last.start()
-    for copy in copies + [last]:
-        copy.wait()
+        out_ref[chip, :, :width] = values
+        out_ref[chip, :, width:] = jnp.concatenate([part, picked.astype(BF16)], axis=1)
 
 
 def pack(heads, residual, ids, gates):
@@ -190,12 +176,7 @@
     return pl.pallas_call(
         pack_kernel,
         in_specs=[pl.BlockSpec(memory_space=pltpu.VMEM)] * 4,
-        out_specs=pl.BlockSpec(memory_space=pl.ANY),
-        scratch_shapes=[
-            pltpu.VMEM((rows, width), BF16),
-            pltpu.VMEM((CHIPS, rows, 512), BF16),
-            pltpu.SemaphoreType.DMA((CHIPS + 1,)),
-        ],
+        out_specs=pl.BlockSpec(memory_space=pltpu.VMEM),
         out_shape=jax.ShapeDtypeStruct((CHIPS, rows, width + 512), BF16),
         cost_estimate=pl.CostEstimate(
             flops=0, bytes_accessed=2 * CHIPS * rows * (width + 512), transcendentals=0

time: 174 us -> 174 us (level)
  no operation moved by 1% of the time
where the time goes in v5:
time: 174 us; the launch traced here: 173 us
  waiting for transfers between devices  55.2 us (32%)
  starting transfers between devices  49.2 us (28%)
  Pallas kernels  45.9 us (26%)
  local copies, waits for them, and re-layouts  19.7 us (11%)
    ppermute x14, starting transfers between devices, exchange(): return lax.ppermute(value, BOTH if axis == 'z' else 'expert', pairs)  29.4 us
    all_to_all x1, waiting for transfers between devices, per_device(): lax.all_to_all(sums.reshape(SIDE * CHIPS, rows, quarter), BOTH, split_axi...  25 us
    pallas_call x4, Pallas kernels, gather_products(): pl.pallas_call(functools.partial(gather_kernel, units=units, first=carrie...  24.2 us
    ppermute x14, waiting for transfers between devices, exchange(): return lax.ppermute(value, BOTH if axis == 'z' else 'expert', pairs)  17.3 us
    all_to_all x1, waiting for transfers between devices, per_device(): lax.all_to_all(block, BOTH, split_axis=0, concat_axis=0, tiled=True, axis...  10 us
    pallas_call x1, Pallas kernels, attention_heads(): pl.pallas_call(functools.partial(attend_kernel, scale=scale, heads=heads)...  9.98 us
    unnamed x17, local copies, waits for them, and re-layouts  9.13 us
    pallas_call x1, Pallas kernels, down(): pl.pallas_call(down_kernel, grid_spec=pltpu.PrefetchScalarGridSpec(num_sc...  7.25 us
  transfers between devices with their start and end apart: 25, of which 10 were waited for; matrix products, arithmetic and copies ran while one was open for 9% of the time, Pallas kernels for 20%

profile of v5, /device:TPU:0, one launch (start us, length us, event | category | flops | bytes accessed | tf_op | source)
XLA Modules:
  0.0 173.1 jit_solution(13450639721881964709)
XLA Ops:
  0.0 0.0 collective-permute-start.1
  0.0 0.5 collective-permute-start.2
  0.5 2.5 %dynamic-slice_bitcast_fusion = (bf16[256,1792]{1,0:T(8,128)(2,1)}, bf16[256,1792]{1,0:T(8,128)(2,1)S(1)}) fusion(bf16[1,256,7168]{2,1,0:T(8,128)(2,1)} %param.31, s32[]{:T(128)S(6)} %select_n.52, s32[]{:T(128)S(6)} %select_n.51), kind=kLoop, calls=%fused_computation.4 | loop fusion | bytes 3670024 | tf_op jit(solution)/shard_map/dynamic_slice | solution.py:527
  3.0 2.0 %collective-permute-start.3 = (bf16[256,1792]{1,0:T(8,128)(2,1)S(1)}, bf16[256,1792]{1,0:T(8,128)(2,1)}, u32[]{:S(2)}, u32[]{:S(2)}) collective-permute-start(bf16[256,1792]{1,0:T(8,128)(2,1)S(1)} %get-tuple-element.44), channel_id=1, source_target_pairs={{0,1},{1,0},{2,3},{3,2},{4,7},{5,6},{6,5},{7,4},{8,9},{9,8},{10,11... | collective-permute-start | bytes 2752520 | tf_op jit(solution)/shard_map/ppermute | solution.py:51
  5.0 0.0 collective-permute-start.4
  5.1 10.0 %shard_map.154 = bf16[4,64,512]{2,1,0:T(8,128)(2,1)} custom-call(s32[4]{0:T(128)} %length_ref, bf16[4,64,512]{2,1,0:T(8,128)(2,1)} %bitcast.77, bf16[4,64,64]{2,1,0:T(8,128)(2,1)} %bitcast.79, bf16[4,2048,512]{2,1,0:T(8,128)(2,1)} %latent_ref.1, bf16[4,64,2048]{2,1,0:T(8,128)(2,1)} %rope_ref.1, bf16[4,2,512]{2,1,0:T(2,128)(2,1)} %fresh_ref.1, ...), custom_call_target="tpu_custom_call" | custom-call | flops 1140850688 | bytes 9437184 | tf_op jit(solution)/shard_map/pallas_call | solution.py:99
  15.1 1.7 fusion.2
  16.8 0.7 copy.28
  17.4 2.3 %shard_map.155 = bf16[16,8,4608]{2,1,0:T(8,128)(2,1)} custom-call(bf16[32,8,128]{2,1,0:T(8,128)(2,1)} %bitcast.78, bf16[8,7168]{1,0:T(8,128)(2,1)} %residual_ref.1, s32[8,8]{1,0:T(8,128)} %ids_ref.1, f32[8,8]{1,0:T(8,128)} %gates_ref.1), custom_call_target="tpu_custom_call" | custom-call | bytes 1179648 | tf_op jit(solution)/shard_map/pallas_call | solution.py:176
  19.8 0.0 collective-permute-done
  19.8 1.2 copy-done.6
  21.0 7.1 %all-to-all-start = ((bf16[16,8,4608]{2,1,0:T(8,128)(2,1)}), bf16[16,8,4608]{2,1,0:T(8,128)(2,1)S(1)}, u32[]{:S(2)}, u32[]{:S(2)}) async-start(bf16[16,8,4608]{2,1,0:T(8,128)(2,1)} %shard_map.155), calls=%async_computation | async-start | bytes 2359296 | tf_op jit(solution)/shard_map/all_to_all | solution.py:556
  28.1 0.0 copy-start.7
  28.1 2.8 %constant_dynamic-slice_fusion = (bf16[256,1792]{1,0:T(8,128)(2,1)}, bf16[256,1792]{1,0:T(8,128)(2,1)}) fusion(bf16[256,7168]{1,0:T(8,128)(2,1)} %bitcast.61, s32[]{:T(128)S(6)} %select_n.54, s32[]{:T(128)S(6)} %select_n.53), kind=kLoop, calls=%fused_computation.9 | loop fusion | bytes 3670024 | tf_op jit(solution)/shard_map/dynamic_slice | solution.py:527
  31.0 4.0 %collective-permute-start.5 = (bf16[256,1792]{1,0:T(8,128)(2,1)}, bf16[256,1792]{1,0:T(8,128)(2,1)}, u32[]{:S(2)}, u32[]{:S(2)}) collective-permute-start(bf16[256,1792]{1,0:T(8,128)(2,1)} %get-tuple-element.82), channel_id=1, source_target_pairs={{0,3},{1,2},{2,1},{3,0},{4,5},{5,4},{6,7},{7,6},{8,11},{9,10},{10,... | collective-permute-start | bytes 2752520 | tf_op jit(solution)/shard_map/ppermute | solution.py:51
  35.0 3.2 %copy.30.own_ref = bf16[4096,224]{1,0:T(8,128)(2,1)S(1)} copy(bf16[4096,224]{0,1:T(8,128)(2,1)} %param.25) | data formatting | bytes 3670016 | tf_op args[9]
  38.2 0.1 reshape.48.gain_ref
  38.3 0.1 pad_add_fusion.place_ref
  38.4 4.0 %copy.29 = bf16[224,4096]{0,1:T(8,128)(2,1)} copy(bf16[224,4096]{1,0:T(8,128)(2,1)} %copy-done.6) | data formatting | bytes 3670016 | tf_op jit(solution)/shard_map/optimization_barrier | solution.py:548
  42.3 0.0 collective-permute-start.6
  42.3 0.0 collective-permute-done.4.refs_5_
  42.3 4.3 %collective-permute-done.5.refs_6_ = bf16[256,1792]{1,0:T(8,128)(2,1)} collective-permute-done((bf16[256,1792]{1,0:T(8,128)(2,1)}, bf16[256,1792]{1,0:T(8,128)(2,1)}, u32[]{:S(2)}, u32[]{:S(2)}) %collective-permute-start.5) | collective-permute-done | bytes 917536 | tf_op jit(solution)/shard_map/ppermute | solution.py:51
  46.7 1.0 all-to-all-done
  47.7 1.6 copy-done.3
  49.3 2.2 %shard_map.156 = bf16[8,128,512]{2,1,0:T(8,128)(2,1)S(1)} custom-call(s32[2]{0:T(128)S(1)} %pad_add_fusion.place_ref, bf16[128,4608]{1,0:T(8,128)(2,1)S(1)} %bitcast.64, bf16[4096,224]{1,0:T(8,128)(2,1)S(1)} %copy.30.own_ref, bf16[4096,224]{1,0:T(8,128)(2,1)S(1)} %bitcast.63, bf16[16,1,448]{2,1,0:T(2,128)(2,1)S(1)} %reshape.48.gain_ref), custom_call_target="tpu_custom_call" | custom-call | flops 469762048 | bytes 3670016 | tf_op jit(solution)/shard_map/pallas_call | solution.py:230
  51.5 1.1 copy-done.4
  52.6 3.6 %all-to-all-start.1 = ((bf16[8,128,512]{2,1,0:T(8,128)(2,1)}), bf16[8,128,512]{2,1,0:T(8,128)(2,1)S(1)}, u32[]{:S(2)}, u32[]{:S(2)}) async-start(bf16[8,128,512]{2,1,0:T(8,128)(2,1)} %copy-done.4), calls=%async_computation.1 | async-start | bytes 2097152 | tf_op jit(solution)/shard_map/all_to_all | solution.py:575
  56.1 1.1 collective-permute-done.6.refs_7_
  57.3 10.0 %all-to-all-done.1 = bf16[8,128,512]{2,1,0:T(8,128)(2,1)S(1)} async-done(((bf16[8,128,512]{2,1,0:T(8,128)(2,1)}), bf16[8,128,512]{2,1,0:T(8,128)(2,1)S(1)}, u32[]{:S(2)}, u32[]{:S(2)}) %all-to-all-start.1) | async-done | bytes 1048608 | tf_op jit(solution)/shard_map/all_to_all | solution.py:575
  67.3 1.5 collective-permute-start.7
  68.8 2.0 %collective-permute-start.9 = (bf16[1024,512]{1,0:T(8,128)(2,1)S(1)}, bf16[1024,512]{1,0:T(8,128)(2,1)S(1)}, u32[]{:S(2)}, u32[]{:S(2)}) collective-permute-start(bf16[1024,512]{1,0:T(8,128)(2,1)S(1)} %bitcast.66), channel_id=1, source_target_pairs={{0,96},{4,36},{8,104},{12,44},{16,112},{20,52},{24,120},{28,60},{3... | collective-permute-start | bytes 3145736 | tf_op jit(solution)/shard_map/ppermute | solution.py:51
  70.8 3.7 %collective-permute-start.11 = (bf16[1024,512]{1,0:T(8,128)(2,1)S(1)}, bf16[1024,512]{1,0:T(8,128)(2,1)S(1)}, u32[]{:S(2)}, u32[]{:S(2)}) collective-permute-start(bf16[1024,512]{1,0:T(8,128)(2,1)S(1)} %bitcast.67), channel_id=1, source_target_pairs={{0,3},{1,2},{2,1},{3,0},{4,5},{5,4},{6,7},{7,6},{8,11},{9,10},{10,... | collective-permute-start | bytes 3145736 | tf_op jit(solution)/shard_map/ppermute | solution.py:51
  74.5 0.8 collective-permute-start.12
  75.3 0.1 collective-permute-start.13
  75.4 0.1 stack.108.place_ref
  75.5 0.0 copy-start
  75.5 2.0 %copy-done = bf16[1,7168,256]{2,1,0:T(8,128)(2,1)S(1)} copy-done((bf16[1,7168,256]{2,1,0:T(8,128)(2,1)S(1)}, bf16[1,7168,256]{2,1,0:T(8,128)(2,1)}, u32[]{:S(2)}) %copy-start) | copy-done | bytes 3670040
  77.6 3.9 %shard_map.157 = (f32[2,256,1152]{2,1,0:T(8,128)S(1)}, f32[16,8,512]{2,1,0:T(8,128)S(1)}) custom-call(s32[25]{0:T(128)S(1)} %stack.108.place_ref, bf16[1024,512]{1,0:T(8,128)(2,1)S(1)} %bitcast.68, bf16[7168,256]{1,0:T(8,128)(2,1)S(1)} %bitcast.59, bf16[7168,256]{1,0:T(8,128)(2,1)} %collective-permute-done.1.refs_2_.refs_4_.refs_3_, ...), custom_call_target="tpu_custom_call" | custom-call | flops 1073741824 | bytes 4194304 | tf_op jit(solution)/shard_map/pallas_call | solution.py:393
  81.4 2.0 %collective-permute-done.7.refs_0_ = bf16[1024,512]{1,0:T(8,128)(2,1)} collective-permute-done((bf16[1024,512]{1,0:T(8,128)(2,1)S(1)}, bf16[1024,512]{1,0:T(8,128)(2,1)}, u32[]{:S(2)}, u32[]{:S(2)}) %collective-permute-start.7) | collective-permute-done | bytes 1048608 | tf_op jit(solution)/shard_map/ppermute | solution.py:51
  83.4 1.8 %collective-permute-start.8 = (bf16[1024,512]{1,0:T(8,128)(2,1)}, bf16[1024,512]{1,0:T(8,128)(2,1)S(1)}, u32[]{:S(2)}, u32[]{:S(2)}) collective-permute-start(bf16[1024,512]{1,0:T(8,128)(2,1)} %collective-permute-done.7.refs_0_), channel_id=1, source_target_pairs={{0,96},{4,36},{8,104},{12,44},{16,112},{20,52},{24,120},{28,60},{3... | collective-permute-start | bytes 3145736 | tf_op jit(solution)/shard_map/ppermute | solution.py:51
  85.2 0.0 collective-permute-done.9.refs_1_
  85.2 5.4 %collective-permute-start.10 = (bf16[1024,512]{1,0:T(8,128)(2,1)S(1)}, bf16[1024,512]{1,0:T(8,128)(2,1)S(1)}, u32[]{:S(2)}, u32[]{:S(2)}) collective-permute-start(bf16[1024,512]{1,0:T(8,128)(2,1)S(1)} %collective-permute-done.9.refs_1_), channel_id=1, source_target_pairs={{0,3},{1,2},{2,1},{3,0},{4,5},{5,4},{6,7},{7,6},{8,11},{9,10},{10,... | collective-permute-start | bytes 3145736 | tf_op jit(solution)/shard_map/ppermute | solution.py:51
  90.6 0.5 collective-permute-start.16
  91.2 1.3 collective-permute-start.14
  92.4 8.6 %shard_map.158 = (f32[2,256,1152]{2,1,0:T(8,128)S(1)}, f32[16,8,512]{2,1,0:T(8,128)S(1)}) custom-call(s32[25]{0:T(128)S(1)} %stack.108.place_ref, bf16[1024,512]{1,0:T(8,128)(2,1)} %collective-permute-done.7.refs_0_, bf16[1024,512]{1,0:T(8,128)(2,1)S(1)} %collective-permute-done.9.refs_1_, bf16[1024,512]{1,0:T(8,128)(2,1)S(1)} %collective-permute-done.11.refs_2_, ...), custom_call_target="tpu_custom_call" | custom-call | flops 3221225472 | bytes 12582912 | tf_op jit(solution)/shard_map/pallas_call | solution.py:393
  101.1 2.3 %collective-permute-done.10.refs_1_ = bf16[1024,512]{1,0:T(8,128)(2,1)S(1)} collective-permute-done((bf16[1024,512]{1,0:T(8,128)(2,1)S(1)}, bf16[1024,512]{1,0:T(8,128)(2,1)S(1)}, u32[]{:S(2)}, u32[]{:S(2)}) %collective-permute-start.10) | collective-permute-done | bytes 1048608 | tf_op jit(solution)/shard_map/ppermute | solution.py:51
  103.5 1.4 collective-permute-start.18
  104.8 3.2 %collective-permute-start.17 = (bf16[512,512]{1,0:T(8,128)(2,1)S(1)}, bf16[512,512]{1,0:T(8,128)(2,1)S(1)}, u32[]{:S(2)}, u32[]{:S(2)}) collective-permute-start(bf16[512,512]{1,0:T(8,128)(2,1)S(1)} %slice.12), channel_id=1, source_target_pairs={{0,3},{1,2},{2,1},{3,0},{4,5},{5,4},{6,7},{7,6},{8,11},{9,10},{10,... | collective-permute-start | bytes 1572872 | tf_op jit(solution)/shard_map/ppermute | solution.py:51
  108.1 7.5 %shard_map.159 = (f32[2,256,1152]{2,1,0:T(8,128)S(1)}, f32[16,8,512]{2,1,0:T(8,128)S(1)}, f32[2,256,256]{2,1,0:T(8,128)S(1)}, s32[256,2]{1,0:T(8,128)S(1)}) custom-call(s32[25]{0:T(128)S(1)} %stack.108.place_ref, bf16[1024,512]{1,0:T(8,128)(2,1)S(1)} %collective-permute-done.8.refs_0_, bf16[1024,512]{1,0:T(8,128)(2,1)S(1)} %collective-permute-done.10.refs_1_, ...), custom_call_target="tpu_custom_call" | custom-call | flops 3221225472 | bytes 12582912 | tf_op jit(solution)/shard_map/pallas_call | solution.py:393
  115.5 0.0 copy-start.2
  115.6 4.3 %shard_map.160 = (bf16[2,256,256]{2,1,0:T(8,128)(2,1)S(1)}, s32[256,2]{1,0:T(8,128)S(1)}) custom-call(s32[25]{0:T(128)S(1)} %stack.108.place_ref, bf16[512,512]{1,0:T(8,128)(2,1)S(1)} %collective-permute-done.17.refs_0_, bf16[512,512]{1,0:T(8,128)(2,1)S(1)} %collective-permute-done.18.refs_1_, bf16[7168,256]{1,0:T(8,128)(2,1)S(1)} %bitcast.60, ...), custom_call_target="tpu_custom_call" | custom-call | flops 1073741824 | bytes 4194304 | tf_op jit(solution)/shard_map/pallas_call | solution.py:393
  119.9 0.1 collective-permute-start.19
  120.0 3.0 %collective-permute-start.20 = (bf16[2,256,256]{2,1,0:T(8,128)(2,1)S(1)}, bf16[2,256,256]{2,1,0:T(8,128)(2,1)S(1)}, u32[]{:S(2)}, u32[]{:S(2)}) collective-permute-start(bf16[2,256,256]{2,1,0:T(8,128)(2,1)S(1)} %get-tuple-element.76.refs_0_), channel_id=1, source_target_pairs={{0,3},{1,2},{2,1},{3,0},{4,5},{5,4},{6,7},{7,6},{8,11},{9,10},{10,... | collective-permute-start | bytes 786440 | tf_op jit(solution)/shard_map/ppermute | solution.py:51
  122.9 1.4 collective-permute-start.21
  124.3 4.9 %collective-permute-done.19.refs_1_ = bf16[2,256,256]{2,1,0:T(8,128)(2,1)S(1)} collective-permute-done((bf16[2,256,256]{2,1,0:T(8,128)(2,1)S(1)}, bf16[2,256,256]{2,1,0:T(8,128)(2,1)S(1)}, u32[]{:S(2)}, u32[]{:S(2)}) %collective-permute-start.19) | collective-permute-done | bytes 262176 | tf_op jit(solution)/shard_map/ppermute | solution.py:51
  129.2 2.6 %collective-permute-done.20.refs_2_ = bf16[2,256,256]{2,1,0:T(8,128)(2,1)S(1)} collective-permute-done((bf16[2,256,256]{2,1,0:T(8,128)(2,1)S(1)}, bf16[2,256,256]{2,1,0:T(8,128)(2,1)S(1)}, u32[]{:S(2)}, u32[]{:S(2)}) %collective-permute-start.20) | collective-permute-done | bytes 262176 | tf_op jit(solution)/shard_map/ppermute | solution.py:51
  131.8 1.8 %collective-permute-done.21.refs_3_ = bf16[2,256,256]{2,1,0:T(8,128)(2,1)S(1)} collective-permute-done((bf16[2,256,256]{2,1,0:T(8,128)(2,1)S(1)}, bf16[2,256,256]{2,1,0:T(8,128)(2,1)S(1)}, u32[]{:S(2)}, u32[]{:S(2)}) %collective-permute-start.21) | collective-permute-done | bytes 262176 | tf_op jit(solution)/shard_map/ppermute | solution.py:34
  133.7 7.2 %shard_map.161 = bf16[512,1792]{1,0:T(8,128)(2,1)} custom-call(s32[25]{0:T(128)S(1)} %stack.108.place_ref, s32[256,2]{1,0:T(8,128)S(1)} %get-tuple-element.70.low_ref, s32[256,2]{1,0:T(8,128)S(1)} %get-tuple-element.75.high_ref, bf16[2,256,256]{2,1,0:T(8,128)(2,1)S(1)} %get-tuple-element.76.refs_0_, ...), custom_call_target="tpu_custom_call" | custom-call | flops 2818572288 | bytes 7340032 | tf_op jit(solution)/shard_map/pallas_call | solution.py:460
  140.9 5.9 %all-to-all-start.2 = ((bf16[64,8,1792]{2,1,0:T(8,128)(2,1)}), bf16[64,8,1792]{2,1,0:T(8,128)(2,1)S(1)}, u32[]{:S(2)}, u32[]{:S(2)}) async-start(bf16[64,8,1792]{2,1,0:T(8,128)(2,1)} %bitcast.41), calls=%async_computation.2 | async-start | bytes 3670016 | tf_op jit(solution)/shard_map/all_to_all | solution.py:620
  146.8 0.2 copy.32
  147.0 0.1 reshape.43
  147.1 25.0 %all-to-all-done.2 = bf16[64,8,1792]{2,1,0:T(8,128)(2,1)S(1)} async-done(((bf16[64,8,1792]{2,1,0:T(8,128)(2,1)}), bf16[64,8,1792]{2,1,0:T(8,128)(2,1)S(1)}, u32[]{:S(2)}, u32[]{:S(2)}) %all-to-all-start.2) | async-done | bytes 1835040 | tf_op jit(solution)/shard_map/all_to_all | solution.py:620
  172.1 0.2 convert_reduce_fusion
  172.4 0.7 add_convert_fusion
  (27 shorter events, 0.1 us)
Async XLA Ops:
  0.0 19.8 %collective-permute-start.1 = (bf16[7168,256]{1,0:T(8,128)(2,1)}, bf16[7168,256]{1,0:T(8,128)(2,1)}, u32[]{:S(2)}, u32[]{:S(2)}) collective-permute-start(bf16[7168,256]{1,0:T(8,128)(2,1)} %bitcast.56), channel_id=1, source_target_pairs={{0,4},{4,0},{8,12},{12,8},{16,20},{20,16},{24,28},{28,24},{32,36},... | collective-permute-start | bytes 11010056 | tf_op jit(solution)/shard_map/ppermute | solution.py:29
  0.0 19.8 %collective-permute-start.2 = (bf16[7168,256]{1,0:T(8,128)(2,1)}, bf16[7168,256]{1,0:T(8,128)(2,1)}, u32[]{:S(2)}, u32[]{:S(2)}) collective-permute-start(bf16[7168,256]{1,0:T(8,128)(2,1)} %bitcast.69), channel_id=1, source_target_pairs={{0,4},{4,0},{8,12},{12,8},{16,20},{20,16},{24,28},{28,24},{32,36},... | collective-permute-start | bytes 11010056 | tf_op jit(solution)/shard_map/ppermute | solution.py:29
  0.5 19.3 %collective-permute-start = (bf16[224,4096]{1,0:T(8,128)(2,1)}, bf16[224,4096]{1,0:T(8,128)(2,1)S(1)}, u32[]{:S(2)}, u32[]{:S(2)}) collective-permute-start(bf16[224,4096]{1,0:T(8,128)(2,1)} %bitcast.74), channel_id=1, source_target_pairs={{0,4},{4,0},{8,12},{12,8},{16,20},{20,16},{24,28},{28,24},{32,36},... | collective-permute-start | bytes 5505032 | tf_op jit(solution)/shard_map/ppermute | solution.py:29
  3.0 16.7 %collective-permute-start.3 = (bf16[256,1792]{1,0:T(8,128)(2,1)S(1)}, bf16[256,1792]{1,0:T(8,128)(2,1)}, u32[]{:S(2)}, u32[]{:S(2)}) collective-permute-start(bf16[256,1792]{1,0:T(8,128)(2,1)S(1)} %get-tuple-element.44), channel_id=1, source_target_pairs={{0,1},{1,0},{2,3},{3,2},{4,7},{5,6},{6,5},{7,4},{8,9},{9,8},{10,11... | collective-permute-start | bytes 2752520 | tf_op jit(solution)/shard_map/ppermute | solution.py:51
  5.0 37.3 %collective-permute-start.4 = (bf16[256,1792]{1,0:T(8,128)(2,1)}, bf16[256,1792]{1,0:T(8,128)(2,1)}, u32[]{:S(2)}, u32[]{:S(2)}) collective-permute-start(bf16[256,1792]{1,0:T(8,128)(2,1)} %get-tuple-element.46), channel_id=1, source_target_pairs={{0,1},{1,0},{2,3},{3,2},{4,7},{5,6},{6,5},{7,4},{8,9},{9,8},{10,11... | collective-permute-start | bytes 2752520 | tf_op jit(solution)/shard_map/ppermute | solution.py:51
  5.1 10.0 %copy-start.5 = (bf16[32,512,128]{2,1,0:T(8,128)(2,1)S(1)}, bf16[32,512,128]{2,1,0:T(8,128)(2,1)}, u32[]{:S(2)}) copy-start(bf16[32,512,128]{2,1,0:T(8,128)(2,1)} %param.24) | copy-start | bytes 12582916
  19.8 1.2 copy-start.6
  21.0 26.7 %all-to-all-start = ((bf16[16,8,4608]{2,1,0:T(8,128)(2,1)}), bf16[16,8,4608]{2,1,0:T(8,128)(2,1)S(1)}, u32[]{:S(2)}, u32[]{:S(2)}) async-start(bf16[16,8,4608]{2,1,0:T(8,128)(2,1)} %shard_map.155), calls=%async_computation | async-start | bytes 2359296 | tf_op jit(solution)/shard_map/all_to_all | solution.py:556
  28.1 10.1 %copy-start.7 = (bf16[7168]{0:T(1024)(128)(2,1)S(1)}, bf16[7168]{0:T(1024)(128)(2,1)}, u32[]{:S(2)}) copy-start(bf16[7168]{0:T(1024)(128)(2,1)} %param.26) | copy-start | bytes 43012
  31.0 15.7 %collective-permute-start.5 = (bf16[256,1792]{1,0:T(8,128)(2,1)}, bf16[256,1792]{1,0:T(8,128)(2,1)}, u32[]{:S(2)}, u32[]{:S(2)}) collective-permute-start(bf16[256,1792]{1,0:T(8,128)(2,1)} %get-tuple-element.82), channel_id=1, source_target_pairs={{0,3},{1,2},{2,1},{3,0},{4,5},{5,4},{6,7},{7,6},{8,11},{9,10},{10,... | collective-permute-start | bytes 2752520 | tf_op jit(solution)/shard_map/ppermute | solution.py:51
  42.3 14.9 %collective-permute-start.6 = (bf16[256,1792]{1,0:T(8,128)(2,1)}, bf16[256,1792]{1,0:T(8,128)(2,1)}, u32[]{:S(2)}, u32[]{:S(2)}) collective-permute-start(bf16[256,1792]{1,0:T(8,128)(2,1)} %collective-permute-done.3), channel_id=1, source_target_pairs={{0,3},{1,2},{2,1},{3,0},{4,5},{5,4},{6,7},{7,6},{8,11},{9,10},{10,... | collective-permute-start | bytes 2752520 | tf_op jit(solution)/shard_map/ppermute | solution.py:51
  47.7 1.6 copy-start.3
  51.5 1.1 copy-start.4
  52.6 14.7 %all-to-all-start.1 = ((bf16[8,128,512]{2,1,0:T(8,128)(2,1)}), bf16[8,128,512]{2,1,0:T(8,128)(2,1)S(1)}, u32[]{:S(2)}, u32[]{:S(2)}) async-start(bf16[8,128,512]{2,1,0:T(8,128)(2,1)} %copy-done.4), calls=%async_computation.1 | async-start | bytes 2097152 | tf_op jit(solution)/shard_map/all_to_all | solution.py:575
  67.3 16.1 %collective-permute-start.7 = (bf16[1024,512]{1,0:T(8,128)(2,1)S(1)}, bf16[1024,512]{1,0:T(8,128)(2,1)}, u32[]{:S(2)}, u32[]{:S(2)}) collective-permute-start(bf16[1024,512]{1,0:T(8,128)(2,1)S(1)} %bitcast.65), channel_id=1, source_target_pairs={{0,24},{4,12},{8,16},{12,4},{16,8},{20,28},{24,0},{28,20},{32,56},... | collective-permute-start | bytes 3145736 | tf_op jit(solution)/shard_map/ppermute | solution.py:51
  68.8 16.4 %collective-permute-start.9 = (bf16[1024,512]{1,0:T(8,128)(2,1)S(1)}, bf16[1024,512]{1,0:T(8,128)(2,1)S(1)}, u32[]{:S(2)}, u32[]{:S(2)}) collective-permute-start(bf16[1024,512]{1,0:T(8,128)(2,1)S(1)} %bitcast.66), channel_id=1, source_target_pairs={{0,96},{4,36},{8,104},{12,44},{16,112},{20,52},{24,120},{28,60},{3... | collective-permute-start | bytes 3145736 | tf_op jit(solution)/shard_map/ppermute | solution.py:51
  70.8 20.4 %collective-permute-start.11 = (bf16[1024,512]{1,0:T(8,128)(2,1)S(1)}, bf16[1024,512]{1,0:T(8,128)(2,1)S(1)}, u32[]{:S(2)}, u32[]{:S(2)}) collective-permute-start(bf16[1024,512]{1,0:T(8,128)(2,1)S(1)} %bitcast.67), channel_id=1, source_target_pairs={{0,3},{1,2},{2,1},{3,0},{4,5},{5,4},{6,7},{7,6},{8,11},{9,10},{10,... | collective-permute-start | bytes 3145736 | tf_op jit(solution)/shard_map/ppermute | solution.py:51
  74.5 16.1 %collective-permute-start.12 = (bf16[256,1792]{1,0:T(8,128)(2,1)}, bf16[256,1792]{1,0:T(8,128)(2,1)}, u32[]{:S(2)}, u32[]{:S(2)}) collective-permute-start(bf16[256,1792]{1,0:T(8,128)(2,1)} %get-tuple-element.81), channel_id=1, source_target_pairs={{0,4},{4,0},{8,12},{12,8},{16,20},{20,16},{24,28},{28,24},{32,36},... | collective-permute-start | bytes 2752520 | tf_op jit(solution)/shard_map/ppermute | solution.py:29
  75.3 15.3 %collective-permute-start.13 = (bf16[256,1792]{1,0:T(8,128)(2,1)}, bf16[256,1792]{1,0:T(8,128)(2,1)}, u32[]{:S(2)}, u32[]{:S(2)}) collective-permute-start(bf16[256,1792]{1,0:T(8,128)(2,1)} %collective-permute-done.4.refs_5_), channel_id=1, source_target_pairs={{0,4},{4,0},{8,12},{12,8},{16,20},{20,16},{24,28},{28,24},{32,36},... | collective-permute-start | bytes 2752520 | tf_op jit(solution)/shard_map/ppermute | solution.py:29
  75.5 2.0 %copy-start = (bf16[1,7168,256]{2,1,0:T(8,128)(2,1)S(1)}, bf16[1,7168,256]{2,1,0:T(8,128)(2,1)}, u32[]{:S(2)}) copy-start(bf16[1,7168,256]{2,1,0:T(8,128)(2,1)} %param.29) | copy-start | bytes 11010052
  83.4 17.6 %collective-permute-start.8 = (bf16[1024,512]{1,0:T(8,128)(2,1)}, bf16[1024,512]{1,0:T(8,128)(2,1)S(1)}, u32[]{:S(2)}, u32[]{:S(2)}) collective-permute-start(bf16[1024,512]{1,0:T(8,128)(2,1)} %collective-permute-done.7.refs_0_), channel_id=1, source_target_pairs={{0,96},{4,36},{8,104},{12,44},{16,112},{20,52},{24,120},{28,60},{3... | collective-permute-start | bytes 3145736 | tf_op jit(solution)/shard_map/ppermute | solution.py:51
  85.2 18.2 %collective-permute-start.10 = (bf16[1024,512]{1,0:T(8,128)(2,1)S(1)}, bf16[1024,512]{1,0:T(8,128)(2,1)S(1)}, u32[]{:S(2)}, u32[]{:S(2)}) collective-permute-start(bf16[1024,512]{1,0:T(8,128)(2,1)S(1)} %collective-permute-done.9.refs_1_), channel_id=1, source_target_pairs={{0,3},{1,2},{2,1},{3,0},{4,5},{5,4},{6,7},{7,6},{8,11},{9,10},{10,... | collective-permute-start | bytes 3145736 | tf_op jit(solution)/shard_map/ppermute | solution.py:51
  90.6 12.8 %collective-permute-start.15 = (bf16[256,1792]{1,0:T(8,128)(2,1)}, bf16[256,1792]{1,0:T(8,128)(2,1)S(1)}, u32[]{:S(2)}, u32[]{:S(2)}) collective-permute-start(bf16[256,1792]{1,0:T(8,128)(2,1)} %collective-permute-done.5.refs_6_), channel_id=1, source_target_pairs={{0,4},{4,0},{8,12},{12,8},{16,20},{20,16},{24,28},{28,24},{32,36},... | collective-permute-start | bytes 2752520 | tf_op jit(solution)/shard_map/ppermute | solution.py:29
  90.6 12.8 %collective-permute-start.16 = (bf16[256,1792]{1,0:T(8,128)(2,1)}, bf16[256,1792]{1,0:T(8,128)(2,1)S(1)}, u32[]{:S(2)}, u32[]{:S(2)}) collective-permute-start(bf16[256,1792]{1,0:T(8,128)(2,1)} %collective-permute-done.6.refs_7_), channel_id=1, source_target_pairs={{0,4},{4,0},{8,12},{12,8},{16,20},{20,16},{24,28},{28,24},{32,36},... | collective-permute-start | bytes 2752520 | tf_op jit(solution)/shard_map/ppermute | solution.py:29
  91.2 16.9 %collective-permute-start.14 = (bf16[1024,512]{1,0:T(8,128)(2,1)S(1)}, bf16[1024,512]{1,0:T(8,128)(2,1)S(1)}, u32[]{:S(2)}, u32[]{:S(2)}) collective-permute-start(bf16[1024,512]{1,0:T(8,128)(2,1)S(1)} %collective-permute-done.11.refs_2_), channel_id=1, source_target_pairs={{0,24},{4,12},{8,16},{12,4},{16,8},{20,28},{24,0},{28,20},{32,56},... | collective-permute-start | bytes 3145736 | tf_op jit(solution)/shard_map/ppermute | solution.py:51
  103.5 12.1 %collective-permute-start.18 = (bf16[512,512]{1,0:T(8,128)(2,1)S(1)}, bf16[512,512]{1,0:T(8,128)(2,1)S(1)}, u32[]{:S(2)}, u32[]{:S(2)}) collective-permute-start(bf16[512,512]{1,0:T(8,128)(2,1)S(1)} %slice.13), channel_id=1, source_target_pairs={{0,24},{4,12},{8,16},{12,4},{16,8},{20,28},{24,0},{28,20},{32,56},... | collective-permute-start | bytes 1572872 | tf_op jit(solution)/shard_map/ppermute | solution.py:51
  104.8 10.7 %collective-permute-start.17 = (bf16[512,512]{1,0:T(8,128)(2,1)S(1)}, bf16[512,512]{1,0:T(8,128)(2,1)S(1)}, u32[]{:S(2)}, u32[]{:S(2)}) collective-permute-start(bf16[512,512]{1,0:T(8,128)(2,1)S(1)} %slice.12), channel_id=1, source_target_pairs={{0,3},{1,2},{2,1},{3,0},{4,5},{5,4},{6,7},{7,6},{8,11},{9,10},{10,... | collective-permute-start | bytes 1572872 | tf_op jit(solution)/shard_map/ppermute | solution.py:51
  108.1 7.5 %copy-start.1 = (bf16[1,7168,256]{2,1,0:T(8,128)(2,1)S(1)}, bf16[1,7168,256]{2,1,0:T(8,128)(2,1)}, u32[]{:S(2)}) copy-start(bf16[1,7168,256]{2,1,0:T(8,128)(2,1)} %param.29) | copy-start | bytes 11010052
  115.5 18.1 %copy-start.2 = (bf16[1,256,7168]{2,1,0:T(8,128)(2,1)S(1)}, bf16[1,256,7168]{2,1,0:T(8,128)(2,1)}, u32[]{:S(2)}) copy-start(bf16[1,256,7168]{2,1,0:T(8,128)(2,1)} %param.31) | copy-start | bytes 11010052
  119.9 9.3 %collective-permute-start.19 = (bf16[2,256,256]{2,1,0:T(8,128)(2,1)S(1)}, bf16[2,256,256]{2,1,0:T(8,128)(2,1)S(1)}, u32[]{:S(2)}, u32[]{:S(2)}) collective-permute-start(bf16[2,256,256]{2,1,0:T(8,128)(2,1)S(1)} %get-tuple-element.76.refs_0_), channel_id=1, source_target_pairs={{0,1},{1,0},{2,3},{3,2},{4,7},{5,6},{6,5},{7,4},{8,9},{9,8},{10,11... | collective-permute-start | bytes 786440 | tf_op jit(solution)/shard_map/ppermute | solution.py:51
  120.0 11.8 %collective-permute-start.20 = (bf16[2,256,256]{2,1,0:T(8,128)(2,1)S(1)}, bf16[2,256,256]{2,1,0:T(8,128)(2,1)S(1)}, u32[]{:S(2)}, u32[]{:S(2)}) collective-permute-start(bf16[2,256,256]{2,1,0:T(8,128)(2,1)S(1)} %get-tuple-element.76.refs_0_), channel_id=1, source_target_pairs={{0,3},{1,2},{2,1},{3,0},{4,5},{5,4},{6,7},{7,6},{8,11},{9,10},{10,... | collective-permute-start | bytes 786440 | tf_op jit(solution)/shard_map/ppermute | solution.py:51
  122.9 10.7 %collective-permute-start.21 = (bf16[2,256,256]{2,1,0:T(8,128)(2,1)S(1)}, bf16[2,256,256]{2,1,0:T(8,128)(2,1)S(1)}, u32[]{:S(2)}, u32[]{:S(2)}) collective-permute-start(bf16[2,256,256]{2,1,0:T(8,128)(2,1)S(1)} %get-tuple-element.76.refs_0_), channel_id=1, source_target_pairs={{0,2},{1,3},{2,0},{3,1},{4,6},{5,7},{6,4},{7,5},{8,10},{9,11},{10,... | collective-permute-start | bytes 786440 | tf_op jit(solution)/shard_map/ppermute | solution.py:34
  140.9 31.2 %all-to-all-start.2 = ((bf16[64,8,1792]{2,1,0:T(8,128)(2,1)}), bf16[64,8,1792]{2,1,0:T(8,128)(2,1)S(1)}, u32[]{:S(2)}, u32[]{:S(2)}) async-start(bf16[64,8,1792]{2,1,0:T(8,128)(2,1)} %bitcast.41), calls=%async_computation.2 | async-start | bytes 3670016 | tf_op jit(solution)/shard_map/all_to_all | solution.py:620

commit v6 on v5

--- a/solution.py
+++ b/solution.py
@@ -39,7 +39,7 @@
     for y in range(SIDE):
         for x in range(SIDE):
             for core in range(2):
-                mask = masks_of(core)[turn]
+                mask = masks_of(core)[1 - turn if axis == "y" else turn]
                 here = expert_of(y, x, core)
                 if axis == "x":
                     pairs.append((here, expert_of(y, x ^ mask, core)))
@@ -51,8 +51,8 @@
     return lax.ppermute(value, BOTH if axis == "z" else "expert", pairs)
 
 
-def pairs_of(core):
-    mask = masks_of(core)[0]
+def pairs_of(core, turn):
+    mask = masks_of(core)[turn]
     return [(v, v ^ mask) for v in range(SIDE) if v < v ^ mask]
 
 
@@ -504,7 +504,7 @@
     chip = expert // 2
     first = jnp.where(core == 0, 1, 3)
     second = 4 - first
-    pair = lambda v: (jnp.minimum(v, v ^ first), jnp.maximum(v, v ^ first))
+    pair = lambda v, mask: (jnp.minimum(v, v ^ mask), jnp.maximum(v, v ^ mask))
     row, column = chip // SIDE, chip % SIDE
     table = []
     for far_y in range(2):
@@ -512,14 +512,15 @@
             for near_y in range(2):
                 for near_x in range(2):
                     table.append(
-                        pair(row ^ (second * far_y))[near_y] * SIDE
-                        + pair(column ^ (second * far_x))[near_x]
+                        pair(row ^ (first * far_y), second)[near_y] * SIDE
+                        + pair(column ^ (second * far_x), first)[near_x]
                     )
     for far_z in range(2):
         for near_z in range(2):
-            table.append(pair(plane ^ (second * far_z))[near_z])
-    is_high = lambda v: jnp.where(v == pair(v)[1], 1, 0)
-    table += [chip, core, plane, is_high(row) * 2 + is_high(column), is_high(plane)]
+            table.append(pair(plane ^ (second * far_z), first)[near_z])
+    is_high = lambda v, mask: jnp.where(v == pair(v, mask)[1], 1, 0)
+    spot = is_high(row, second) * 2 + is_high(column, first)
+    table += [chip, core, plane, spot, is_high(plane, first)]
     place = jnp.stack([jnp.asarray(v, jnp.int32) for v in table])
 
     quarter = model // SIDE
@@ -568,9 +569,9 @@
     cubes = [
         [expert_of(y, x, core) * SIDE + z for z in z_pair for y in y_pair for x in x_pair]
         for core in range(2)
-        for z_pair in pairs_of(core)
-        for y_pair in pairs_of(core)
-        for x_pair in pairs_of(core)
+        for z_pair in pairs_of(core, 0)
+        for y_pair in pairs_of(core, 1)
+        for x_pair in pairs_of(core, 0)
     ]
     block = lax.all_to_all(
         block, BOTH, split_axis=0, concat_axis=0, tiled=True, axis_index_groups=cubes

time: 174 us -> 175 us (level)
    all_to_all x1, waiting for transfers between devices: 10 us -> 12 us  [per_device(): lax.all_to_all(block, BOTH, split_axis=0, concat_axis=0, tiled=True, axis...]
    ppermute x14, waiting for transfers between devices: 17.3 us -> 15.5 us  [exchange(): return lax.ppermute(value, BOTH if axis == 'z' else 'expert', pairs)]
  transfers between devices with their start and end apart: 25 -> 25, of which waited for: 10 -> 11; matrix products, arithmetic and copies ran while one was open for 9% -> 9% of each run, Pallas kernels for 20% -> 20%
where the time goes in v6:
time: 175 us; the launch traced here: 174 us
  waiting for transfers between devices  56.3 us (32%)
  starting transfers between devices  49.2 us (28%)
  Pallas kernels  45.9 us (26%)
  local copies, waits for them, and re-layouts  19.7 us (11%)
    ppermute x14, starting transfers between devices, exchange(): return lax.ppermute(value, BOTH if axis == 'z' else 'expert', pairs)  29.7 us
    all_to_all x1, waiting for transfers between devices, per_device(): lax.all_to_all(sums.reshape(SIDE * CHIPS, rows, quarter), BOTH, split_axi...  25.2 us
    pallas_call x4, Pallas kernels, gather_products(): pl.pallas_call(functools.partial(gather_kernel, units=units, first=carrie...  24.2 us
    ppermute x14, waiting for transfers between devices, exchange(): return lax.ppermute(value, BOTH if axis == 'z' else 'expert', pairs)  15.5 us
    all_to_all x1, waiting for transfers between devices, per_device(): lax.all_to_all(block, BOTH, split_axis=0, concat_axis=0, tiled=True, axis...  12 us
    pallas_call x1, Pallas kernels, attention_heads(): pl.pallas_call(functools.partial(attend_kernel, scale=scale, heads=heads)...  9.98 us
    unnamed x17, local copies, waits for them, and re-layouts  9.13 us
    pallas_call x1, Pallas kernels, down(): pl.pallas_call(down_kernel, grid_spec=pltpu.PrefetchScalarGridSpec(num_sc...  7.24 us
  transfers between devices with their start and end apart: 25, of which 11 were waited for; matrix products, arithmetic and copies ran while one was open for 9% of the time, Pallas kernels for 20%

profile of v6, /device:TPU:0, one launch (start us, length us, event | category | flops | bytes accessed | tf_op | source)
XLA Modules:
  0.0 174.2 jit_solution(13038076295638774418)
XLA Ops:
  0.0 0.0 collective-permute-start.1
  0.0 0.5 collective-permute-start.2
  0.5 2.5 %dynamic-slice_bitcast_fusion = (bf16[256,1792]{1,0:T(8,128)(2,1)}, bf16[256,1792]{1,0:T(8,128)(2,1)S(1)}) fusion(bf16[1,256,7168]{2,1,0:T(8,128)(2,1)} %param.31, s32[]{:T(128)S(6)} %select_n.52, s32[]{:T(128)S(6)} %select_n.51), kind=kLoop, calls=%fused_computation.4 | loop fusion | bytes 3670024 | tf_op jit(solution)/shard_map/dynamic_slice | solution.py:528
  3.0 2.0 %collective-permute-start.3 = (bf16[256,1792]{1,0:T(8,128)(2,1)S(1)}, bf16[256,1792]{1,0:T(8,128)(2,1)}, u32[]{:S(2)}, u32[]{:S(2)}) collective-permute-start(bf16[256,1792]{1,0:T(8,128)(2,1)S(1)} %get-tuple-element.44), channel_id=1, source_target_pairs={{0,1},{1,0},{2,3},{3,2},{4,7},{5,6},{6,5},{7,4},{8,9},{9,8},{10,11... | collective-permute-start | bytes 2752520 | tf_op jit(solution)/shard_map/ppermute | solution.py:51
  5.0 0.0 collective-permute-start.4
  5.1 10.0 %shard_map.154 = bf16[4,64,512]{2,1,0:T(8,128)(2,1)} custom-call(s32[4]{0:T(128)} %length_ref, bf16[4,64,512]{2,1,0:T(8,128)(2,1)} %bitcast.77, bf16[4,64,64]{2,1,0:T(8,128)(2,1)} %bitcast.79, bf16[4,2048,512]{2,1,0:T(8,128)(2,1)} %latent_ref.1, bf16[4,64,2048]{2,1,0:T(8,128)(2,1)} %rope_ref.1, bf16[4,2,512]{2,1,0:T(2,128)(2,1)} %fresh_ref.1, ...), custom_call_target="tpu_custom_call" | custom-call | flops 1140850688 | bytes 9437184 | tf_op jit(solution)/shard_map/pallas_call | solution.py:99
  15.1 1.7 fusion.2
  16.8 0.7 copy.28
  17.4 2.3 %shard_map.155 = bf16[16,8,4608]{2,1,0:T(8,128)(2,1)} custom-call(bf16[32,8,128]{2,1,0:T(8,128)(2,1)} %bitcast.78, bf16[8,7168]{1,0:T(8,128)(2,1)} %residual_ref.1, s32[8,8]{1,0:T(8,128)} %ids_ref.1, f32[8,8]{1,0:T(8,128)} %gates_ref.1), custom_call_target="tpu_custom_call" | custom-call | bytes 1179648 | tf_op jit(solution)/shard_map/pallas_call | solution.py:176
  19.8 0.0 collective-permute-done
  19.8 1.2 copy-done.6
  21.0 7.1 %all-to-all-start = ((bf16[16,8,4608]{2,1,0:T(8,128)(2,1)}), bf16[16,8,4608]{2,1,0:T(8,128)(2,1)S(1)}, u32[]{:S(2)}, u32[]{:S(2)}) async-start(bf16[16,8,4608]{2,1,0:T(8,128)(2,1)} %shard_map.155), calls=%async_computation | async-start | bytes 2359296 | tf_op jit(solution)/shard_map/all_to_all | solution.py:557
  28.1 0.0 copy-start.7
  28.1 2.8 %constant_dynamic-slice_fusion = (bf16[256,1792]{1,0:T(8,128)(2,1)}, bf16[256,1792]{1,0:T(8,128)(2,1)}) fusion(bf16[256,7168]{1,0:T(8,128)(2,1)} %bitcast.61, s32[]{:T(128)S(6)} %select_n.54, s32[]{:T(128)S(6)} %select_n.53), kind=kLoop, calls=%fused_computation.9 | loop fusion | bytes 3670024 | tf_op jit(solution)/shard_map/dynamic_slice | solution.py:528
  31.0 4.0 %collective-permute-start.5 = (bf16[256,1792]{1,0:T(8,128)(2,1)}, bf16[256,1792]{1,0:T(8,128)(2,1)}, u32[]{:S(2)}, u32[]{:S(2)}) collective-permute-start(bf16[256,1792]{1,0:T(8,128)(2,1)} %get-tuple-element.82), channel_id=1, source_target_pairs={{0,3},{1,2},{2,1},{3,0},{4,5},{5,4},{6,7},{7,6},{8,11},{9,10},{10,... | collective-permute-start | bytes 2752520 | tf_op jit(solution)/shard_map/ppermute | solution.py:51
  35.0 3.2 %copy.30.own_ref = bf16[4096,224]{1,0:T(8,128)(2,1)S(1)} copy(bf16[4096,224]{0,1:T(8,128)(2,1)} %param.25) | data formatting | bytes 3670016 | tf_op args[9]
  38.2 0.1 reshape.48.gain_ref
  38.3 0.1 pad_add_fusion.place_ref
  38.4 4.0 %copy.29 = bf16[224,4096]{0,1:T(8,128)(2,1)} copy(bf16[224,4096]{1,0:T(8,128)(2,1)} %copy-done.6) | data formatting | bytes 3670016 | tf_op jit(solution)/shard_map/optimization_barrier | solution.py:549
  42.3 0.0 collective-permute-start.6
  42.3 0.0 collective-permute-done.4.refs_5_
  42.3 4.3 %collective-permute-done.5.refs_6_ = bf16[256,1792]{1,0:T(8,128)(2,1)} collective-permute-done((bf16[256,1792]{1,0:T(8,128)(2,1)}, bf16[256,1792]{1,0:T(8,128)(2,1)}, u32[]{:S(2)}, u32[]{:S(2)}) %collective-permute-start.5) | collective-permute-done | bytes 917536 | tf_op jit(solution)/shard_map/ppermute | solution.py:51
  46.7 1.0 all-to-all-done
  47.7 1.6 copy-done.3
  49.3 2.2 %shard_map.156 = bf16[8,128,512]{2,1,0:T(8,128)(2,1)S(1)} custom-call(s32[2]{0:T(128)S(1)} %pad_add_fusion.place_ref, bf16[128,4608]{1,0:T(8,128)(2,1)S(1)} %bitcast.64, bf16[4096,224]{1,0:T(8,128)(2,1)S(1)} %copy.30.own_ref, bf16[4096,224]{1,0:T(8,128)(2,1)S(1)} %bitcast.63, bf16[16,1,448]{2,1,0:T(2,128)(2,1)S(1)} %reshape.48.gain_ref), custom_call_target="tpu_custom_call" | custom-call | flops 469762048 | bytes 3670016 | tf_op jit(solution)/shard_map/pallas_call | solution.py:230
  51.5 1.1 copy-done.4
  52.6 4.3 %all-to-all-start.1 = ((bf16[8,128,512]{2,1,0:T(8,128)(2,1)}), bf16[8,128,512]{2,1,0:T(8,128)(2,1)S(1)}, u32[]{:S(2)}, u32[]{:S(2)}) async-start(bf16[8,128,512]{2,1,0:T(8,128)(2,1)} %copy-done.4), calls=%async_computation.1 | async-start | bytes 2097152 | tf_op jit(solution)/shard_map/all_to_all | solution.py:576
  56.8 0.4 collective-permute-done.6.refs_7_
  57.3 12.0 %all-to-all-done.1 = bf16[8,128,512]{2,1,0:T(8,128)(2,1)S(1)} async-done(((bf16[8,128,512]{2,1,0:T(8,128)(2,1)}), bf16[8,128,512]{2,1,0:T(8,128)(2,1)S(1)}, u32[]{:S(2)}, u32[]{:S(2)}) %all-to-all-start.1) | async-done | bytes 1048608 | tf_op jit(solution)/shard_map/all_to_all | solution.py:576
  69.3 1.7 collective-permute-start.7
  71.0 0.0 collective-permute-start.9
  71.0 5.2 %collective-permute-start.11 = (bf16[1024,512]{1,0:T(8,128)(2,1)S(1)}, bf16[1024,512]{1,0:T(8,128)(2,1)S(1)}, u32[]{:S(2)}, u32[]{:S(2)}) collective-permute-start(bf16[1024,512]{1,0:T(8,128)(2,1)S(1)} %bitcast.67), channel_id=1, source_target_pairs={{0,3},{1,2},{2,1},{3,0},{4,5},{5,4},{6,7},{7,6},{8,11},{9,10},{10,... | collective-permute-start | bytes 3145736 | tf_op jit(solution)/shard_map/ppermute | solution.py:51
  76.2 0.5 collective-permute-start.13
  76.7 0.1 stack.108.place_ref
  76.8 0.0 copy-start
  76.8 2.0 %copy-done = bf16[1,7168,256]{2,1,0:T(8,128)(2,1)S(1)} copy-done((bf16[1,7168,256]{2,1,0:T(8,128)(2,1)S(1)}, bf16[1,7168,256]{2,1,0:T(8,128)(2,1)}, u32[]{:S(2)}) %copy-start) | copy-done | bytes 3670040
  78.9 3.9 %shard_map.157 = (f32[2,256,1152]{2,1,0:T(8,128)S(1)}, f32[16,8,512]{2,1,0:T(8,128)S(1)}) custom-call(s32[25]{0:T(128)S(1)} %stack.108.place_ref, bf16[1024,512]{1,0:T(8,128)(2,1)S(1)} %bitcast.68, bf16[7168,256]{1,0:T(8,128)(2,1)S(1)} %bitcast.59, bf16[7168,256]{1,0:T(8,128)(2,1)} %collective-permute-done.1.refs_2_.refs_4_.refs_3_, ...), custom_call_target="tpu_custom_call" | custom-call | flops 1073741824 | bytes 4194304 | tf_op jit(solution)/shard_map/pallas_call | solution.py:393
  82.7 2.6 %collective-permute-done.7.refs_0_ = bf16[1024,512]{1,0:T(8,128)(2,1)} collective-permute-done((bf16[1024,512]{1,0:T(8,128)(2,1)S(1)}, bf16[1024,512]{1,0:T(8,128)(2,1)}, u32[]{:S(2)}, u32[]{:S(2)}) %collective-permute-start.7) | collective-permute-done | bytes 1048608 | tf_op jit(solution)/shard_map/ppermute | solution.py:51
  85.4 0.0 collective-permute-start.8
  85.4 0.4 collective-permute-done.9.refs_1_
  85.8 6.5 %collective-permute-start.10 = (bf16[1024,512]{1,0:T(8,128)(2,1)S(1)}, bf16[1024,512]{1,0:T(8,128)(2,1)S(1)}, u32[]{:S(2)}, u32[]{:S(2)}) collective-permute-start(bf16[1024,512]{1,0:T(8,128)(2,1)S(1)} %collective-permute-done.9.refs_1_), channel_id=1, source_target_pairs={{0,3},{1,2},{2,1},{3,0},{4,5},{5,4},{6,7},{7,6},{8,11},{9,10},{10,... | collective-permute-start | bytes 3145736 | tf_op jit(solution)/shard_map/ppermute | solution.py:51
  92.3 0.0 collective-permute-done.12.refs_8_
  92.3 0.5 collective-permute-start.16
  92.8 1.9 %collective-permute-start.14 = (bf16[1024,512]{1,0:T(8,128)(2,1)S(1)}, bf16[1024,512]{1,0:T(8,128)(2,1)S(1)}, u32[]{:S(2)}, u32[]{:S(2)}) collective-permute-start(bf16[1024,512]{1,0:T(8,128)(2,1)S(1)} %collective-permute-done.11.refs_2_), channel_id=1, source_target_pairs={{0,24},{4,12},{8,16},{12,4},{16,8},{20,28},{24,0},{28,20},{32,56},... | collective-permute-start | bytes 3145736 | tf_op jit(solution)/shard_map/ppermute | solution.py:51
  94.8 8.6 %shard_map.158 = (f32[2,256,1152]{2,1,0:T(8,128)S(1)}, f32[16,8,512]{2,1,0:T(8,128)S(1)}) custom-call(s32[25]{0:T(128)S(1)} %stack.108.place_ref, bf16[1024,512]{1,0:T(8,128)(2,1)} %collective-permute-done.7.refs_0_, bf16[1024,512]{1,0:T(8,128)(2,1)S(1)} %collective-permute-done.9.refs_1_, bf16[1024,512]{1,0:T(8,128)(2,1)S(1)} %collective-permute-done.11.refs_2_, ...), custom_call_target="tpu_custom_call" | custom-call | flops 3221225472 | bytes 12582912 | tf_op jit(solution)/shard_map/pallas_call | solution.py:393
  103.4 1.7 collective-permute-done.10.refs_1_
  105.2 2.0 %collective-permute-start.18 = (bf16[512,512]{1,0:T(8,128)(2,1)S(1)}, bf16[512,512]{1,0:T(8,128)(2,1)S(1)}, u32[]{:S(2)}, u32[]{:S(2)}) collective-permute-start(bf16[512,512]{1,0:T(8,128)(2,1)S(1)} %slice.13), channel_id=1, source_target_pairs={{0,24},{4,12},{8,16},{12,4},{16,8},{20,28},{24,0},{28,20},{32,56},... | collective-permute-start | bytes 1572872 | tf_op jit(solution)/shard_map/ppermute | solution.py:51
  107.2 3.2 %collective-permute-start.17 = (bf16[512,512]{1,0:T(8,128)(2,1)S(1)}, bf16[512,512]{1,0:T(8,128)(2,1)S(1)}, u32[]{:S(2)}, u32[]{:S(2)}) collective-permute-start(bf16[512,512]{1,0:T(8,128)(2,1)S(1)} %slice.12), channel_id=1, source_target_pairs={{0,3},{1,2},{2,1},{3,0},{4,5},{5,4},{6,7},{7,6},{8,11},{9,10},{10,... | collective-permute-start | bytes 1572872 | tf_op jit(solution)/shard_map/ppermute | solution.py:51
  110.4 7.5 %shard_map.159 = (f32[2,256,1152]{2,1,0:T(8,128)S(1)}, f32[16,8,512]{2,1,0:T(8,128)S(1)}, f32[2,256,256]{2,1,0:T(8,128)S(1)}, s32[256,2]{1,0:T(8,128)S(1)}) custom-call(s32[25]{0:T(128)S(1)} %stack.108.place_ref, bf16[1024,512]{1,0:T(8,128)(2,1)S(1)} %collective-permute-done.8.refs_0_, bf16[1024,512]{1,0:T(8,128)(2,1)S(1)} %collective-permute-done.10.refs_1_, ...), custom_call_target="tpu_custom_call" | custom-call | flops 3221225472 | bytes 12582912 | tf_op jit(solution)/shard_map/pallas_call | solution.py:393
  117.9 0.0 copy-start.2
  117.9 4.3 %shard_map.160 = (bf16[2,256,256]{2,1,0:T(8,128)(2,1)S(1)}, s32[256,2]{1,0:T(8,128)S(1)}) custom-call(s32[25]{0:T(128)S(1)} %stack.108.place_ref, bf16[512,512]{1,0:T(8,128)(2,1)S(1)} %collective-permute-done.17.refs_0_, bf16[512,512]{1,0:T(8,128)(2,1)S(1)} %collective-permute-done.18.refs_1_, bf16[7168,256]{1,0:T(8,128)(2,1)S(1)} %bitcast.60, ...), custom_call_target="tpu_custom_call" | custom-call | flops 1073741824 | bytes 4194304 | tf_op jit(solution)/shard_map/pallas_call | solution.py:393
  122.2 0.1 collective-permute-start.19
  122.3 3.0 %collective-permute-start.20 = (bf16[2,256,256]{2,1,0:T(8,128)(2,1)S(1)}, bf16[2,256,256]{2,1,0:T(8,128)(2,1)S(1)}, u32[]{:S(2)}, u32[]{:S(2)}) collective-permute-start(bf16[2,256,256]{2,1,0:T(8,128)(2,1)S(1)} %get-tuple-element.76.refs_0_), channel_id=1, source_target_pairs={{0,3},{1,2},{2,1},{3,0},{4,5},{5,4},{6,7},{7,6},{8,11},{9,10},{10,... | collective-permute-start | bytes 786440 | tf_op jit(solution)/shard_map/ppermute | solution.py:51
  125.3 1.4 collective-permute-start.21
  126.7 3.4 %collective-permute-done.19.refs_1_ = bf16[2,256,256]{2,1,0:T(8,128)(2,1)S(1)} collective-permute-done((bf16[2,256,256]{2,1,0:T(8,128)(2,1)S(1)}, bf16[2,256,256]{2,1,0:T(8,128)(2,1)S(1)}, u32[]{:S(2)}, u32[]{:S(2)}) %collective-permute-start.19) | collective-permute-done | bytes 262176 | tf_op jit(solution)/shard_map/ppermute | solution.py:51
  130.1 2.5 %collective-permute-done.20.refs_2_ = bf16[2,256,256]{2,1,0:T(8,128)(2,1)S(1)} collective-permute-done((bf16[2,256,256]{2,1,0:T(8,128)(2,1)S(1)}, bf16[2,256,256]{2,1,0:T(8,128)(2,1)S(1)}, u32[]{:S(2)}, u32[]{:S(2)}) %collective-permute-start.20) | collective-permute-done | bytes 262176 | tf_op jit(solution)/shard_map/ppermute | solution.py:51
  132.6 2.6 %collective-permute-done.21.refs_3_ = bf16[2,256,256]{2,1,0:T(8,128)(2,1)S(1)} collective-permute-done((bf16[2,256,256]{2,1,0:T(8,128)(2,1)S(1)}, bf16[2,256,256]{2,1,0:T(8,128)(2,1)S(1)}, u32[]{:S(2)}, u32[]{:S(2)}) %collective-permute-start.21) | collective-permute-done | bytes 262176 | tf_op jit(solution)/shard_map/ppermute | solution.py:34
  135.2 7.2 %shard_map.161 = bf16[512,1792]{1,0:T(8,128)(2,1)} custom-call(s32[25]{0:T(128)S(1)} %stack.108.place_ref, s32[256,2]{1,0:T(8,128)S(1)} %get-tuple-element.70.low_ref, s32[256,2]{1,0:T(8,128)S(1)} %get-tuple-element.75.high_ref, bf16[2,256,256]{2,1,0:T(8,128)(2,1)S(1)} %get-tuple-element.76.refs_0_, ...), custom_call_target="tpu_custom_call" | custom-call | flops 2818572288 | bytes 7340032 | tf_op jit(solution)/shard_map/pallas_call | solution.py:460
  142.4 5.3 %all-to-all-start.2 = ((bf16[64,8,1792]{2,1,0:T(8,128)(2,1)}), bf16[64,8,1792]{2,1,0:T(8,128)(2,1)S(1)}, u32[]{:S(2)}, u32[]{:S(2)}) async-start(bf16[64,8,1792]{2,1,0:T(8,128)(2,1)} %bitcast.41), calls=%async_computation.2 | async-start | bytes 3670016 | tf_op jit(solution)/shard_map/all_to_all | solution.py:621
  147.8 0.2 copy.32
  147.9 0.1 reshape.43
  148.1 25.2 %all-to-all-done.2 = bf16[64,8,1792]{2,1,0:T(8,128)(2,1)S(1)} async-done(((bf16[64,8,1792]{2,1,0:T(8,128)(2,1)}), bf16[64,8,1792]{2,1,0:T(8,128)(2,1)S(1)}, u32[]{:S(2)}, u32[]{:S(2)}) %all-to-all-start.2) | async-done | bytes 1835040 | tf_op jit(solution)/shard_map/all_to_all | solution.py:621
  173.3 0.2 convert_reduce_fusion
  173.5 0.7 add_convert_fusion
  (27 shorter events, 0.1 us)
Async XLA Ops:
  0.0 19.8 %collective-permute-start.1 = (bf16[7168,256]{1,0:T(8,128)(2,1)}, bf16[7168,256]{1,0:T(8,128)(2,1)}, u32[]{:S(2)}, u32[]{:S(2)}) collective-permute-start(bf16[7168,256]{1,0:T(8,128)(2,1)} %bitcast.56), channel_id=1, source_target_pairs={{0,4},{4,0},{8,12},{12,8},{16,20},{20,16},{24,28},{28,24},{32,36},... | collective-permute-start | bytes 11010056 | tf_op jit(solution)/shard_map/ppermute | solution.py:29
  0.0 19.8 %collective-permute-start.2 = (bf16[7168,256]{1,0:T(8,128)(2,1)}, bf16[7168,256]{1,0:T(8,128)(2,1)}, u32[]{:S(2)}, u32[]{:S(2)}) collective-permute-start(bf16[7168,256]{1,0:T(8,128)(2,1)} %bitcast.69), channel_id=1, source_target_pairs={{0,4},{4,0},{8,12},{12,8},{16,20},{20,16},{24,28},{28,24},{32,36},... | collective-permute-start | bytes 11010056 | tf_op jit(solution)/shard_map/ppermute | solution.py:29
  0.5 19.3 %collective-permute-start = (bf16[224,4096]{1,0:T(8,128)(2,1)}, bf16[224,4096]{1,0:T(8,128)(2,1)S(1)}, u32[]{:S(2)}, u32[]{:S(2)}) collective-permute-start(bf16[224,4096]{1,0:T(8,128)(2,1)} %bitcast.74), channel_id=1, source_target_pairs={{0,4},{4,0},{8,12},{12,8},{16,20},{20,16},{24,28},{28,24},{32,36},... | collective-permute-start | bytes 5505032 | tf_op jit(solution)/shard_map/ppermute | solution.py:29
  3.0 16.7 %collective-permute-start.3 = (bf16[256,1792]{1,0:T(8,128)(2,1)S(1)}, bf16[256,1792]{1,0:T(8,128)(2,1)}, u32[]{:S(2)}, u32[]{:S(2)}) collective-permute-start(bf16[256,1792]{1,0:T(8,128)(2,1)S(1)} %get-tuple-element.44), channel_id=1, source_target_pairs={{0,1},{1,0},{2,3},{3,2},{4,7},{5,6},{6,5},{7,4},{8,9},{9,8},{10,11... | collective-permute-start | bytes 2752520 | tf_op jit(solution)/shard_map/ppermute | solution.py:51
  5.0 37.3 %collective-permute-start.4 = (bf16[256,1792]{1,0:T(8,128)(2,1)}, bf16[256,1792]{1,0:T(8,128)(2,1)}, u32[]{:S(2)}, u32[]{:S(2)}) collective-permute-start(bf16[256,1792]{1,0:T(8,128)(2,1)} %get-tuple-element.46), channel_id=1, source_target_pairs={{0,1},{1,0},{2,3},{3,2},{4,7},{5,6},{6,5},{7,4},{8,9},{9,8},{10,11... | collective-permute-start | bytes 2752520 | tf_op jit(solution)/shard_map/ppermute | solution.py:51
  5.1 10.0 %copy-start.5 = (bf16[32,512,128]{2,1,0:T(8,128)(2,1)S(1)}, bf16[32,512,128]{2,1,0:T(8,128)(2,1)}, u32[]{:S(2)}) copy-start(bf16[32,512,128]{2,1,0:T(8,128)(2,1)} %param.24) | copy-start | bytes 12582916
  19.8 1.2 copy-start.6
  21.0 26.7 %all-to-all-start = ((bf16[16,8,4608]{2,1,0:T(8,128)(2,1)}), bf16[16,8,4608]{2,1,0:T(8,128)(2,1)S(1)}, u32[]{:S(2)}, u32[]{:S(2)}) async-start(bf16[16,8,4608]{2,1,0:T(8,128)(2,1)} %shard_map.155), calls=%async_computation | async-start | bytes 2359296 | tf_op jit(solution)/shard_map/all_to_all | solution.py:557
  28.1 10.1 %copy-start.7 = (bf16[7168]{0:T(1024)(128)(2,1)S(1)}, bf16[7168]{0:T(1024)(128)(2,1)}, u32[]{:S(2)}) copy-start(bf16[7168]{0:T(1024)(128)(2,1)} %param.26) | copy-start | bytes 43012
  31.0 15.7 %collective-permute-start.5 = (bf16[256,1792]{1,0:T(8,128)(2,1)}, bf16[256,1792]{1,0:T(8,128)(2,1)}, u32[]{:S(2)}, u32[]{:S(2)}) collective-permute-start(bf16[256,1792]{1,0:T(8,128)(2,1)} %get-tuple-element.82), channel_id=1, source_target_pairs={{0,3},{1,2},{2,1},{3,0},{4,5},{5,4},{6,7},{7,6},{8,11},{9,10},{10,... | collective-permute-start | bytes 2752520 | tf_op jit(solution)/shard_map/ppermute | solution.py:51
  42.3 14.9 %collective-permute-start.6 = (bf16[256,1792]{1,0:T(8,128)(2,1)}, bf16[256,1792]{1,0:T(8,128)(2,1)}, u32[]{:S(2)}, u32[]{:S(2)}) collective-permute-start(bf16[256,1792]{1,0:T(8,128)(2,1)} %collective-permute-done.3), channel_id=1, source_target_pairs={{0,3},{1,2},{2,1},{3,0},{4,5},{5,4},{6,7},{7,6},{8,11},{9,10},{10,... | collective-permute-start | bytes 2752520 | tf_op jit(solution)/shard_map/ppermute | solution.py:51
  47.7 1.6 copy-start.3
  51.5 1.1 copy-start.4
  52.6 16.7 %all-to-all-start.1 = ((bf16[8,128,512]{2,1,0:T(8,128)(2,1)}), bf16[8,128,512]{2,1,0:T(8,128)(2,1)S(1)}, u32[]{:S(2)}, u32[]{:S(2)}) async-start(bf16[8,128,512]{2,1,0:T(8,128)(2,1)} %copy-done.4), calls=%async_computation.1 | async-start | bytes 2097152 | tf_op jit(solution)/shard_map/all_to_all | solution.py:576
  69.3 16.1 %collective-permute-start.7 = (bf16[1024,512]{1,0:T(8,128)(2,1)S(1)}, bf16[1024,512]{1,0:T(8,128)(2,1)}, u32[]{:S(2)}, u32[]{:S(2)}) collective-permute-start(bf16[1024,512]{1,0:T(8,128)(2,1)S(1)} %bitcast.65), channel_id=1, source_target_pairs={{0,24},{4,12},{8,16},{12,4},{16,8},{20,28},{24,0},{28,20},{32,56},... | collective-permute-start | bytes 3145736 | tf_op jit(solution)/shard_map/ppermute | solution.py:51
  71.0 14.8 %collective-permute-start.9 = (bf16[1024,512]{1,0:T(8,128)(2,1)S(1)}, bf16[1024,512]{1,0:T(8,128)(2,1)S(1)}, u32[]{:S(2)}, u32[]{:S(2)}) collective-permute-start(bf16[1024,512]{1,0:T(8,128)(2,1)S(1)} %bitcast.66), channel_id=1, source_target_pairs={{0,32},{4,100},{8,40},{12,108},{16,48},{20,116},{24,56},{28,124},{... | collective-permute-start | bytes 3145736 | tf_op jit(solution)/shard_map/ppermute | solution.py:51
  71.0 21.8 %collective-permute-start.11 = (bf16[1024,512]{1,0:T(8,128)(2,1)S(1)}, bf16[1024,512]{1,0:T(8,128)(2,1)S(1)}, u32[]{:S(2)}, u32[]{:S(2)}) collective-permute-start(bf16[1024,512]{1,0:T(8,128)(2,1)S(1)} %bitcast.67), channel_id=1, source_target_pairs={{0,3},{1,2},{2,1},{3,0},{4,5},{5,4},{6,7},{7,6},{8,11},{9,10},{10,... | collective-permute-start | bytes 3145736 | tf_op jit(solution)/shard_map/ppermute | solution.py:51
  76.2 16.1 %collective-permute-start.12 = (bf16[256,1792]{1,0:T(8,128)(2,1)}, bf16[256,1792]{1,0:T(8,128)(2,1)}, u32[]{:S(2)}, u32[]{:S(2)}) collective-permute-start(bf16[256,1792]{1,0:T(8,128)(2,1)} %get-tuple-element.81), channel_id=1, source_target_pairs={{0,4},{4,0},{8,12},{12,8},{16,20},{20,16},{24,28},{28,24},{32,36},... | collective-permute-start | bytes 2752520 | tf_op jit(solution)/shard_map/ppermute | solution.py:29
  76.2 16.1 %collective-permute-start.13 = (bf16[256,1792]{1,0:T(8,128)(2,1)}, bf16[256,1792]{1,0:T(8,128)(2,1)}, u32[]{:S(2)}, u32[]{:S(2)}) collective-permute-start(bf16[256,1792]{1,0:T(8,128)(2,1)} %collective-permute-done.4.refs_5_), channel_id=1, source_target_pairs={{0,4},{4,0},{8,12},{12,8},{16,20},{20,16},{24,28},{28,24},{32,36},... | collective-permute-start | bytes 2752520 | tf_op jit(solution)/shard_map/ppermute | solution.py:29
  76.8 2.0 %copy-start = (bf16[1,7168,256]{2,1,0:T(8,128)(2,1)S(1)}, bf16[1,7168,256]{2,1,0:T(8,128)(2,1)}, u32[]{:S(2)}) copy-start(bf16[1,7168,256]{2,1,0:T(8,128)(2,1)} %param.29) | copy-start | bytes 11010052
  85.4 18.0 %collective-permute-start.8 = (bf16[1024,512]{1,0:T(8,128)(2,1)}, bf16[1024,512]{1,0:T(8,128)(2,1)S(1)}, u32[]{:S(2)}, u32[]{:S(2)}) collective-permute-start(bf16[1024,512]{1,0:T(8,128)(2,1)} %collective-permute-done.7.refs_0_), channel_id=1, source_target_pairs={{0,32},{4,100},{8,40},{12,108},{16,48},{20,116},{24,56},{28,124},{... | collective-permute-start | bytes 3145736 | tf_op jit(solution)/shard_map/ppermute | solution.py:51
  85.8 19.3 %collective-permute-start.10 = (bf16[1024,512]{1,0:T(8,128)(2,1)S(1)}, bf16[1024,512]{1,0:T(8,128)(2,1)S(1)}, u32[]{:S(2)}, u32[]{:S(2)}) collective-permute-start(bf16[1024,512]{1,0:T(8,128)(2,1)S(1)} %collective-permute-done.9.refs_1_), channel_id=1, source_target_pairs={{0,3},{1,2},{2,1},{3,0},{4,5},{5,4},{6,7},{7,6},{8,11},{9,10},{10,... | collective-permute-start | bytes 3145736 | tf_op jit(solution)/shard_map/ppermute | solution.py:51
  92.3 12.8 %collective-permute-start.15 = (bf16[256,1792]{1,0:T(8,128)(2,1)}, bf16[256,1792]{1,0:T(8,128)(2,1)S(1)}, u32[]{:S(2)}, u32[]{:S(2)}) collective-permute-start(bf16[256,1792]{1,0:T(8,128)(2,1)} %collective-permute-done.5.refs_6_), channel_id=1, source_target_pairs={{0,4},{4,0},{8,12},{12,8},{16,20},{20,16},{24,28},{28,24},{32,36},... | collective-permute-start | bytes 2752520 | tf_op jit(solution)/shard_map/ppermute | solution.py:29
  92.3 12.8 %collective-permute-start.16 = (bf16[256,1792]{1,0:T(8,128)(2,1)}, bf16[256,1792]{1,0:T(8,128)(2,1)S(1)}, u32[]{:S(2)}, u32[]{:S(2)}) collective-permute-start(bf16[256,1792]{1,0:T(8,128)(2,1)} %collective-permute-done.6.refs_7_), channel_id=1, source_target_pairs={{0,4},{4,0},{8,12},{12,8},{16,20},{20,16},{24,28},{28,24},{32,36},... | collective-permute-start | bytes 2752520 | tf_op jit(solution)/shard_map/ppermute | solution.py:29
  92.8 17.5 %collective-permute-start.14 = (bf16[1024,512]{1,0:T(8,128)(2,1)S(1)}, bf16[1024,512]{1,0:T(8,128)(2,1)S(1)}, u32[]{:S(2)}, u32[]{:S(2)}) collective-permute-start(bf16[1024,512]{1,0:T(8,128)(2,1)S(1)} %collective-permute-done.11.refs_2_), channel_id=1, source_target_pairs={{0,24},{4,12},{8,16},{12,4},{16,8},{20,28},{24,0},{28,20},{32,56},... | collective-permute-start | bytes 3145736 | tf_op jit(solution)/shard_map/ppermute | solution.py:51
  105.2 12.7 %collective-permute-start.18 = (bf16[512,512]{1,0:T(8,128)(2,1)S(1)}, bf16[512,512]{1,0:T(8,128)(2,1)S(1)}, u32[]{:S(2)}, u32[]{:S(2)}) collective-permute-start(bf16[512,512]{1,0:T(8,128)(2,1)S(1)} %slice.13), channel_id=1, source_target_pairs={{0,24},{4,12},{8,16},{12,4},{16,8},{20,28},{24,0},{28,20},{32,56},... | collective-permute-start | bytes 1572872 | tf_op jit(solution)/shard_map/ppermute | solution.py:51
  107.2 10.7 %collective-permute-start.17 = (bf16[512,512]{1,0:T(8,128)(2,1)S(1)}, bf16[512,512]{1,0:T(8,128)(2,1)S(1)}, u32[]{:S(2)}, u32[]{:S(2)}) collective-permute-start(bf16[512,512]{1,0:T(8,128)(2,1)S(1)} %slice.12), channel_id=1, source_target_pairs={{0,3},{1,2},{2,1},{3,0},{4,5},{5,4},{6,7},{7,6},{8,11},{9,10},{10,... | collective-permute-start | bytes 1572872 | tf_op jit(solution)/shard_map/ppermute | solution.py:51
  110.4 7.5 %copy-start.1 = (bf16[1,7168,256]{2,1,0:T(8,128)(2,1)S(1)}, bf16[1,7168,256]{2,1,0:T(8,128)(2,1)}, u32[]{:S(2)}) copy-start(bf16[1,7168,256]{2,1,0:T(8,128)(2,1)} %param.29) | copy-start | bytes 11010052
  117.9 17.3 %copy-start.2 = (bf16[1,256,7168]{2,1,0:T(8,128)(2,1)S(1)}, bf16[1,256,7168]{2,1,0:T(8,128)(2,1)}, u32[]{:S(2)}) copy-start(bf16[1,256,7168]{2,1,0:T(8,128)(2,1)} %param.31) | copy-start | bytes 11010052
  122.2 7.9 %collective-permute-start.19 = (bf16[2,256,256]{2,1,0:T(8,128)(2,1)S(1)}, bf16[2,256,256]{2,1,0:T(8,128)(2,1)S(1)}, u32[]{:S(2)}, u32[]{:S(2)}) collective-permute-start(bf16[2,256,256]{2,1,0:T(8,128)(2,1)S(1)} %get-tuple-element.76.refs_0_), channel_id=1, source_target_pairs={{0,1},{1,0},{2,3},{3,2},{4,7},{5,6},{6,5},{7,4},{8,9},{9,8},{10,11... | collective-permute-start | bytes 786440 | tf_op jit(solution)/shard_map/ppermute | solution.py:51
  122.3 10.3 %collective-permute-start.20 = (bf16[2,256,256]{2,1,0:T(8,128)(2,1)S(1)}, bf16[2,256,256]{2,1,0:T(8,128)(2,1)S(1)}, u32[]{:S(2)}, u32[]{:S(2)}) collective-permute-start(bf16[2,256,256]{2,1,0:T(8,128)(2,1)S(1)} %get-tuple-element.76.refs_0_), channel_id=1, source_target_pairs={{0,3},{1,2},{2,1},{3,0},{4,5},{5,4},{6,7},{7,6},{8,11},{9,10},{10,... | collective-permute-start | bytes 786440 | tf_op jit(solution)/shard_map/ppermute | solution.py:51
  125.3 9.9 %collective-permute-start.21 = (bf16[2,256,256]{2,1,0:T(8,128)(2,1)S(1)}, bf16[2,256,256]{2,1,0:T(8,128)(2,1)S(1)}, u32[]{:S(2)}, u32[]{:S(2)}) collective-permute-start(bf16[2,256,256]{2,1,0:T(8,128)(2,1)S(1)} %get-tuple-element.76.refs_0_), channel_id=1, source_target_pairs={{0,2},{1,3},{2,0},{3,1},{4,6},{5,7},{6,4},{7,5},{8,10},{9,11},{10,... | collective-permute-start | bytes 786440 | tf_op jit(solution)/shard_map/ppermute | solution.py:34
  142.4 30.8 %all-to-all-start.2 = ((bf16[64,8,1792]{2,1,0:T(8,128)(2,1)}), bf16[64,8,1792]{2,1,0:T(8,128)(2,1)S(1)}, u32[]{:S(2)}, u32[]{:S(2)}) async-start(bf16[64,8,1792]{2,1,0:T(8,128)(2,1)} %bitcast.41), calls=%async_computation.2 | async-start | bytes 3670016 | tf_op jit(solution)/shard_map/all_to_all | solution.py:621
